TPU v7x, 32 devices: a whole 2x2x4 slice. The times are simulated.
32 devices in a mesh: grp: 1, wide: 8 (over z, y), narrow: 4 (over x, core).
Axes of the slice: x: 2, y: 2, z: 4, core: 2. Of those that a mesh axis runs over, the one named last changes fastest.
Arguments:
- vectors: bfloat16 [512, 2, 3, 16, 512], P('grp', None, None, 'wide', 'narrow'), may hold values from -6 to 6
- links: float32 [3, 2, 3, 3, 16, 512], P('grp', None, None, None, 'wide', 'narrow'), may hold values from -4 to 4
- directions: int32 [3], replicated, may hold values from 0 to 2, each once
- peram: bfloat16 [2, 512, 256], P('grp', 'wide', 'narrow'), may hold values from -0.1875 to 0.1875
Outputs:
- elementals: float32 [3, 2, 512, 512], P('grp', None, 'wide')
- products: float32 [3, 2, 512, 256], P('grp', None, 'wide', 'narrow')
All inputs are finite; a program needn't handle non-finite values.
Results may differ from a plain program's by a relative error of at most 0.004.
Values may be sent and summed in bfloat16 or wider, within the bound.
No kernel may reach another device: no remote copies, remote signals or barrier semaphores. Data moves between devices by JAX's collectives and lax.ppermute only.
A program may use at most 64 MiB of HBM per device.

v0:
```python
import math

import jax
import jax.numpy as jnp
from jax import lax
from jax.sharding import PartitionSpec as P

LZ = 16


def from_behind(x, axis, by):
    length = lax.axis_size(axis)
    return lax.ppermute(x, axis, [(i, (i + by) % length) for i in range(length)])


def covariant_product(link_field, shifted):
    link_real = link_field[0][None]
    link_imag = link_field[1][None]
    vec_real = shifted[:, 0][:, None]
    vec_imag = shifted[:, 1][:, None]
    out_real = jnp.sum(link_real * vec_real - link_imag * vec_imag, axis=2)
    out_imag = jnp.sum(link_real * vec_imag + link_imag * vec_real, axis=2)
    return jnp.stack([out_real, out_imag], 1).astype(jnp.bfloat16)


def on_device(vectors, links, directions, peram):
    vec_count = vectors.shape[0]
    plane_count = vectors.shape[3]
    row_length = vectors.shape[4]
    direction_count = directions.shape[0]
    col_count = peram.shape[2]
    wide_count = lax.axis_size("wide")
    narrow_count = lax.axis_size("narrow")
    norm_factor = 1.0 / math.sqrt(12.0 * plane_count * wide_count * row_length * narrow_count)
    next_first = from_behind(vectors[:, :, :, 0:1], "wide", -1)
    along_first = jnp.concatenate([vectors[:, :, :, 1:], next_first], 3)
    next_second = from_behind(vectors[:, :, :, :, 0:LZ], "narrow", -1)
    along_second = jnp.concatenate([vectors[:, :, :, :, LZ:], next_second], 4)
    along_third = jnp.roll(
        vectors.reshape(vec_count, 2, 3, plane_count, row_length // LZ, LZ), -1, axis=5
    ).reshape(vectors.shape)
    rotated = jnp.concatenate([-vectors[:, 1:2], vectors[:, 0:1]], 1)
    left_block = jnp.concatenate(
        [vectors.reshape(vec_count, -1), rotated.reshape(vec_count, -1)], 0
    )
    partials = []
    for slot_index in range(direction_count):
        chosen = directions[slot_index]
        shifted = jnp.where(
            chosen == 0, along_first, jnp.where(chosen == 1, along_second, along_third)
        )
        link_field = jnp.where(chosen == 0, links[0], jnp.where(chosen == 1, links[1], links[2]))
        product = covariant_product(link_field, shifted).reshape(vec_count, -1)
        partials.append(
            lax.dot_general(
                left_block, product, (((1,), (1,)), ((), ())), preferred_element_type=jnp.float32
            )
        )
    halves = jnp.stack(partials).reshape(direction_count, 2, vec_count, vec_count) * norm_factor
    real_part = halves[:, 0]
    imag_part = halves[:, 1]
    local_terms = jnp.stack(
        [real_part - jnp.swapaxes(real_part, 1, 2), imag_part + jnp.swapaxes(imag_part, 1, 2)], 1
    )
    rows_here = vec_count // wide_count
    thin_rows = lax.psum_scatter(local_terms, ("wide", "narrow"), scatter_dimension=2, tiled=True)
    elementals = lax.all_gather(thin_rows, "narrow", axis=2, tiled=True)
    elem_low = elementals.astype(jnp.bfloat16)
    real_rows = elem_low[:, 0]
    imag_rows = elem_low[:, 1]
    piece = lax.all_gather(peram, "wide", axis=1, tiled=True)
    width = piece.shape[1]
    left_part = jnp.concatenate([real_rows, imag_rows], 2).reshape(-1, 2 * width)
    right_part = jnp.concatenate(
        [jnp.concatenate([piece[0], piece[1]], 1), jnp.concatenate([-piece[1], piece[0]], 1)], 0
    )
    summed = jnp.dot(left_part, right_part, preferred_element_type=jnp.float32)
    products = summed.reshape(direction_count, rows_here, 2, col_count).transpose(0, 2, 1, 3)
    return (elementals, products)


def solution(mesh):
    placed = (
        P("grp", None, None, "wide", "narrow"),
        P("grp", None, None, None, "wide", "narrow"),
        P(),
        P("grp", "wide", "narrow"),
    )
    return jax.shard_map(
        on_device,
        mesh=mesh,
        in_specs=placed,
        out_specs=(P("grp", None, "wide", None), P("grp", None, "wide", "narrow")),
        check_vma=False,
    )
```

profile of v0, /device:TPU:0, one launch (start us, length us, event | category | flops | bytes accessed | tf_op | source)
XLA Modules:
  0.0 245.6 jit_solution(10593543814689281994)
XLA Ops:
  7.2 3.6 %copy.27 = bf16[512,2,3,2,128]{0,4,3,2,1:T(8,128)(2,1)S(1)} copy(bf16[512,2,3,2,128]{4,3,2,1,0:T(2,128)(2,1)} %param.4) | data formatting | bytes 3145728 | tf_op args[0]
  12.1 6.0 %collective-permute-start = (bf16[512,2,3,1,128]{0,4,3,2,1:T(8,128)(2,1)}, bf16[512,2,3,1,128]{0,4,3,2,1:T(8,128)(2,1)}, u32[]{:S(2)}, u32[]{:S(2)}) collective-permute-start(bf16[512,2,3,1,128]{0,4,3,2,1:T(8,128)(2,1)} %get-tuple-element.28), channel_id=1, source_target_pairs={{0,28},{4,0},{8,4},{12,8},{16,12},{20,16},{24,20},{28,24},{1,29},{... | collective-permute-start | bytes 2359304 | tf_op jit(solution)/shard_map/ppermute | solution.py:13
  25.1 3.2 %pad_maximum_fusion.2 = bf16[512,2,3,2,128]{4,3,2,1,0:T(2,128)(2,1)} fusion(bf16[512,1,3,2,128]{4,3,2,1,0:T(2,128)(2,1)S(1)} %get-tuple-element.30, bf16[512,1,3,2,128]{4,3,2,1,0:T(2,128)(2,1)S(1)} %get-tuple-element.29), kind=kLoop, calls=%fused_computation.17 | loop fusion | flops 786432 | bytes 3145728 | tf_op jit(solution)/shard_map/concatenate | solution.py:42
  29.0 1.7 pad_maximum_fusion.5
  31.9 1.5 reshape.106
  36.6 3.4 %pad_maximum_fusion.1 = bf16[1024,1536]{1,0:T(8,128)(2,1)} fusion(bf16[512,1536]{1,0:T(8,128)(2,1)} %reshape.107, bf16[512,1536]{1,0:T(8,128)(2,1)S(1)} %copy-done.3), kind=kLoop, calls=%fused_computation.9 | loop fusion | flops 6291456 | bytes 6291456 | tf_op jit(solution)/shard_map/concatenate | solution.py:43
  40.6 3.5 %fusion.2 = (bf16[512,2,3,2,128]{0,4,3,2,1:T(8,128)(2,1)S(1)}, bf16[512,2,3,2,128]{0,4,3,2,1:T(8,128)(2,1)}, bf16[512,2,3,2,128]{0,4,3,2,1:T(8,128)(2,1)}) fusion(bf16[512,2,3,2,8,16]{0,5,4,3,2,1:T(8,128)(2,1)S(1)} %copy-done.5, pred[]{:T(512)} %bitcast.2, pred[]{:T(512)} %bitcast.1, bf16[512,2,3,2,16]{0,4,3,2,1:T(8,128)(2,1)S(1)} %collective-permute-done.1, ...), kind=kLoop, calls=%fused_computation.27 | loop fusion | flops 11010048 | bytes 9437190 | tf_op jit(solution)/shard_map/jit(_where)/select_n | solution.py:49
  44.2 1.6 fusion.10
  46.3 1.9 copy.33
  49.8 1.6 copy.34
  51.4 1.5 reshape.117
  52.9 4.4 %fusion.6 = (f32[512,3,2,128]{0,3,2,1:T(8,128)S(1)}, f32[512,3,2,128]{0,3,2,1:T(8,128)S(1)}, f32[512,3,2,128]{0,3,2,1:T(8,128)}, f32[512,3,2,128]{0,3,2,1:T(8,128)}) fusion(bf16[512,2,3,2,128]{0,4,3,2,1:T(8,128)(2,1)} %get-tuple-element.20, bf16[512,2,3,2,128]{0,4,3,2,1:T(8,128)(2,1)} %get-tuple-element.19), kind=kLoop, calls=%fused_computation.34 | loop fusion | flops 1572864 | bytes 9437184 | tf_op jit(solution)/shard_map/mul | solution.py:21
  57.4 3.1 %copy.35 = f32[512,3,2,128]{3,0,2,1:T(8,128)} copy(f32[512,3,2,128]{0,3,2,1:T(8,128)} %get-tuple-element.48) | data formatting | bytes 3145728 | tf_op jit(solution)/shard_map/mul | solution.py:21
  60.5 3.1 %copy.36 = f32[512,3,2,128]{3,0,2,1:T(8,128)} copy(f32[512,3,2,128]{0,3,2,1:T(8,128)} %get-tuple-element.47) | data formatting | bytes 3145728 | tf_op jit(solution)/shard_map/mul | solution.py:21
  63.5 3.3 %subtract_reduce_fusion.1 = (bf16[512,3,2,128]{3,0,2,1:T(8,128)(2,1)S(1)}, bf16[512,3,2,128]{3,0,2,1:T(8,128)(2,1)S(1)}) fusion(f32[512,3,2,128]{3,0,2,1:T(8,128)} %copy.36, f32[3,3,2,128]{3,2,1,0:T(2,128)S(1)} %copy-done.15, f32[512,3,2,128]{3,0,2,1:T(8,128)} %copy.35, f32[3,3,2,128]{3,2,1,0:T(2,128)S(1)} %copy-done.16), kind=kLoop, calls=%fused_computation.5 | loop fusion | flops 8650752 | bytes 4737024 | tf_op jit(solution)/shard_map/reduce_sum | solution.py:21
  67.0 2.8 %copy.37 = bf16[512,2,3,2,128]{4,3,2,1,0:T(2,128)(2,1)} copy(bf16[512,2,3,2,128]{4,0,3,2,1:T(8,128)(2,1)S(1)} %pad_maximum_fusion.7) | data formatting | bytes 3145728 | tf_op jit(solution)/shard_map/stack | solution.py:23
  69.8 4.9 %reshape.118 = bf16[512,1536,1]{1,0,2:T(8,128)(2,1)} reshape(bf16[512,2,3,2,128]{4,3,2,1,0:T(2,128)(2,1)} %copy.37) | data formatting | bytes 3145728 | tf_op jit(solution)/shard_map/convert_element_type | solution.py:23
  74.7 5.7 %convolution_bitcast_fusion.2 = f32[1,2,512,512]{3,2,1,0:T(8,128)} fusion(bf16[2,512,1536]{2,1,0:T(8,128)(2,1)} %bitcast.135, bf16[512,1536,1]{1,0,2:T(8,128)(2,1)} %reshape.117), kind=kOutput, calls=%fused_computation.16 | convolution fusion | flops 1610612736 | bytes 6815744 | tf_op jit(solution)/shard_map/dot_general | solution.py:55
  80.4 3.2 %convolution_bitcast_fusion.1 = f32[1,2,512,512]{3,2,1,0:T(8,128)} fusion(bf16[2,512,1536]{2,1,0:T(8,128)(2,1)S(1)} %bitcast.137, bf16[512,1536,1]{1,0,2:T(8,128)(2,1)S(1)} %copy-done.11), kind=kOutput, calls=%fused_computation.15 | convolution fusion | flops 1610612736 | bytes 6815744 | tf_op jit(solution)/shard_map/dot_general | solution.py:55
  83.5 1.6 copy.38
  85.2 1.7 copy.39
  86.9 2.8 %subtract_reduce_fusion = (bf16[512,3,2,128]{3,0,2,1:T(8,128)(2,1)S(1)}, bf16[512,3,2,128]{3,0,2,1:T(8,128)(2,1)S(1)}) fusion(f32[512,3,2,128]{3,0,2,1:T(8,128)} %copy.39, f32[3,3,2,128]{3,2,1,0:T(2,128)S(1)} %copy-done.14, f32[512,3,2,128]{3,0,2,1:T(8,128)S(1)} %copy-done.4, f32[3,3,2,128]{3,2,1,0:T(2,128)S(1)} %get-tuple-element.42), kind=kLoop, calls=%fused_computation.3 | loop fusion | flops 8650752 | bytes 4737024 | tf_op jit(solution)/shard_map/reduce_sum | solution.py:21
  89.9 1.6 copy.40
  92.2 3.9 %convolution_bitcast_fusion = f32[1,2,512,512]{3,2,1,0:T(8,128)S(1)} fusion(bf16[2,512,1536]{2,1,0:T(8,128)(2,1)} %bitcast.136, bf16[512,1536,1]{1,0,2:T(8,128)(2,1)S(1)} %reshape.119), kind=kOutput, calls=%fused_computation.14 | convolution fusion | flops 1610612736 | bytes 6815744 | tf_op jit(solution)/shard_map/dot_general | solution.py:55
  97.3 3.7 %fusion.15 = (f32[3,1,512,512]{3,2,1,0:T(8,128)}, f32[3,512,512]{2,1,0:T(8,128)}) fusion(f32[3,2,512,512]{3,2,1,0:T(8,128)S(1)} %maximum_multiply_fusion), kind=kLoop, calls=%fused_computation.69 | loop fusion | bytes 12582912 | tf_op jit(solution)/shard_map/slice | solution.py:60
  101.9 2.4 copy.43
  104.3 3.5 %copy.47 = f32[3,1,512,512]{2,3,0,1:T(8,128)} copy(f32[3,1,512,512]{3,2,1,0:T(8,128)} %get-tuple-element.16) | data formatting | bytes 6291456
  107.8 5.3 %fusion = (f32[3,1,512,512]{3,2,0,1:T(8,128)S(1)}, f32[3,1,512,512]{3,2,0,1:T(8,128)S(1)}) fusion(f32[3,1,512,512]{2,3,0,1:T(8,128)} %copy.47, f32[3,2,512,512]{3,2,1,0:T(8,128)} %copy-done, f32[3,512,512]{1,2,0:T(8,128)S(1)} %copy.43), kind=kLoop, calls=%fused_computation.11 | loop fusion | flops 1572864 | bytes 18874368 | tf_op jit(solution)/shard_map/stack | solution.py:62
  113.1 3.4 %pad_maximum_fusion = f32[3,2,512,512]{3,2,0,1:T(8,128)} fusion(f32[3,1,512,512]{3,2,0,1:T(8,128)S(1)} %get-tuple-element.15, f32[3,1,512,512]{3,2,0,1:T(8,128)S(1)} %get-tuple-element.14), kind=kLoop, calls=%fused_computation.1 | loop fusion | flops 1572864 | bytes 12582912 | tf_op jit(solution)/shard_map/stack | solution.py:62
  117.3 30.8 %all_gather.7 = bf16[2,512,64]{2,1,0:T(8,128)(2,1)S(1)} all-gather(bf16[2,64,64]{2,1,0:T(8,128)(2,1)S(1)} %copy-done.19), channel_id=1, replica_groups=mesh['grp'=1,'wide'=8,'narrow'=4] {'wide'}, dimensions={1}, use_global_device_ids=true | all-gather | bytes 147456 | tf_op jit(solution)/shard_map/all_gather | solution.py:71
  148.4 79.6 %reduce-scatter.2.cloned.1.call-done = f32[3,2,16,512]{3,2,0,1:T(8,128)} async-done(((f32[3,2,512,512]{3,2,0,1:T(8,128)}), f32[3,2,16,512]{3,2,0,1:T(8,128)}) %reduce-scatter.2.cloned.1.call-update) | async-done | bytes 196624 | tf_op jit(solution)/shard_map/reduce_scatter | solution.py:66
  228.0 8.7 %all_gather.6 = f32[3,2,64,512]{3,2,0,1:T(8,128)S(1)} all-gather(f32[3,2,16,512]{3,2,0,1:T(8,128)} %reduce-scatter.2.cloned.1.call-done), channel_id=1, replica_groups=mesh['grp'=1,'wide'=8,'narrow'=4] {'narrow'}, dimensions={2}, use_global_device_ids=true | all-gather | bytes 983040 | tf_op jit(solution)/shard_map/all_gather | solution.py:67
  (73 shorter events, 18.5 us)
Async XLA Ops:
  7.2 220.9 %reduce-scatter.2.cloned.1.call-start = ((), (), s32[]{:S(2)}) async-start(), calls=%async_computation.1 | async-start | bytes 6488064 | tf_op jit(solution)/shard_map/reduce_scatter | solution.py:66
  12.1 7.6 %copy-start.20 = (s32[3]{0:T(128)S(1)}, s32[3]{0:T(128)}, u32[]{:S(2)}) copy-start(s32[3]{0:T(128)} %param.6) | copy-start | bytes 40
  12.1 11.9 %copy-start.1 = (bf16[512,2,3,2,128]{4,3,2,1,0:T(2,128)(2,1)S(1)}, bf16[512,2,3,2,128]{4,3,2,1,0:T(2,128)(2,1)}, u32[]{:S(2)}) copy-start(bf16[512,2,3,2,128]{4,3,2,1,0:T(2,128)(2,1)} %param.4) | copy-start | bytes 4718596
  12.1 28.5 %collective-permute-start = (bf16[512,2,3,1,128]{0,4,3,2,1:T(8,128)(2,1)}, bf16[512,2,3,1,128]{0,4,3,2,1:T(8,128)(2,1)}, u32[]{:S(2)}, u32[]{:S(2)}) collective-permute-start(bf16[512,2,3,1,128]{0,4,3,2,1:T(8,128)(2,1)} %get-tuple-element.28), channel_id=1, source_target_pairs={{0,28},{4,0},{8,4},{12,8},{16,12},{20,16},{24,20},{28,24},{1,29},{... | collective-permute-start | bytes 2359304 | tf_op jit(solution)/shard_map/ppermute | solution.py:13
  18.2 22.5 %collective-permute-start.1 = (bf16[512,2,3,2,16]{0,4,3,2,1:T(8,128)(2,1)S(1)}, bf16[512,2,3,2,16]{0,4,3,2,1:T(8,128)(2,1)S(1)}, u32[]{:S(2)}, u32[]{:S(2)}) collective-permute-start(bf16[512,2,3,2,16]{0,4,3,2,1:T(8,128)(2,1)S(1)} %slice.148), channel_id=1, source_target_pairs={{0,3},{1,0},{2,1},{3,2},{4,7},{5,4},{6,5},{7,6},{8,11},{9,8},{10,9... | collective-permute-start | bytes 589832 | tf_op jit(solution)/shard_map/ppermute | solution.py:13
  25.1 3.2 %copy-start.13 = (f32[3,2,3,3,2,128]{5,4,3,2,1,0:T(2,128)S(1)}, f32[3,2,3,3,2,128]{5,4,3,2,1,0:T(2,128)}, u32[]{:S(2)}) copy-start(f32[3,2,3,3,2,128]{5,4,3,2,1,0:T(2,128)} %param.5) | copy-start | bytes 165892
  31.9 1.8 copy-start.2
  33.7 2.9 %copy-start.3 = (bf16[512,1536]{1,0:T(8,128)(2,1)S(1)}, bf16[512,1536]{1,0:T(8,128)(2,1)}, u32[]{:S(2)}) copy-start(bf16[512,1536]{1,0:T(8,128)(2,1)} %reshape.106) | copy-start | bytes 4718596
  36.6 3.4 %copy-start.12 = (f32[1,2,3,3,2,128]{5,4,3,2,1,0:T(2,128)S(1)}, f32[1,2,3,3,2,128]{5,4,3,2,1,0:T(2,128)}, u32[]{:S(2)}) copy-start(f32[1,2,3,3,2,128]{5,4,3,2,1,0:T(2,128)} %get-tuple-element.35) | copy-start | bytes 55300
  36.6 4.1 %copy-start.5 = (bf16[512,2,3,2,8,16]{0,5,4,3,2,1:T(8,128)(2,1)S(1)}, bf16[512,2,3,2,8,16]{0,5,4,3,2,1:T(8,128)(2,1)}, u32[]{:S(2)}) copy-start(bf16[512,2,3,2,8,16]{0,5,4,3,2,1:T(8,128)(2,1)} %pad_maximum_fusion.5) | copy-start | bytes 4718596
  36.6 4.1 %copy-start.6 = (bf16[512,2,3,2,112]{0,4,3,2,1:T(8,128)(2,1)S(1)}, bf16[512,2,3,2,112]{0,4,3,2,1:T(8,128)(2,1)}, u32[]{:S(2)}) copy-start(bf16[512,2,3,2,112]{0,4,3,2,1:T(8,128)(2,1)} %slice.147) | copy-start | bytes 4128772
  36.6 4.1 %copy-start.8 = (bf16[512,2,3,1,128]{0,4,3,2,1:T(8,128)(2,1)S(1)}, bf16[512,2,3,1,128]{0,4,3,2,1:T(8,128)(2,1)}, u32[]{:S(2)}) copy-start(bf16[512,2,3,1,128]{0,4,3,2,1:T(8,128)(2,1)} %get-tuple-element.27) | copy-start | bytes 2359300
  46.2 1.9 copy-start.17
  46.3 1.9 copy-start.18
  60.5 3.1 %copy-start.15 = (f32[3,3,2,128]{3,2,1,0:T(2,128)S(1)}, f32[3,3,2,128]{3,2,1,0:T(2,128)}, u32[]{:S(2)}) copy-start(f32[3,3,2,128]{3,2,1,0:T(2,128)} %get-tuple-element.49) | copy-start | bytes 27652
  60.5 3.1 %copy-start.16 = (f32[3,3,2,128]{3,2,1,0:T(2,128)S(1)}, f32[3,3,2,128]{3,2,1,0:T(2,128)}, u32[]{:S(2)}) copy-start(f32[3,3,2,128]{3,2,1,0:T(2,128)} %get-tuple-element.50) | copy-start | bytes 27652
  74.7 5.7 %copy-start.7 = (bf16[1024,1536]{1,0:T(8,128)(2,1)S(1)}, bf16[1024,1536]{1,0:T(8,128)(2,1)}, u32[]{:S(2)}) copy-start(bf16[1024,1536]{1,0:T(8,128)(2,1)} %pad_maximum_fusion.1) | copy-start | bytes 9437188
  74.7 5.7 %copy-start.11 = (bf16[512,1536,1]{1,0,2:T(8,128)(2,1)S(1)}, bf16[512,1536,1]{1,0,2:T(8,128)(2,1)}, u32[]{:S(2)}) copy-start(bf16[512,1536,1]{1,0,2:T(8,128)(2,1)} %reshape.118) | copy-start | bytes 4718596
  85.2 1.7 copy-start.4
  85.2 1.7 copy-start.14
  92.1 3.9 %copy-start.9 = (f32[1,2,512,512]{3,2,1,0:T(8,128)S(1)}, f32[1,2,512,512]{3,2,1,0:T(8,128)}, u32[]{:S(2)}) copy-start(f32[1,2,512,512]{3,2,1,0:T(8,128)} %convolution_bitcast_fusion.2) | copy-start | bytes 6291460
  92.1 3.9 %copy-start.10 = (f32[1,2,512,512]{3,2,1,0:T(8,128)S(1)}, f32[1,2,512,512]{3,2,1,0:T(8,128)}, u32[]{:S(2)}) copy-start(f32[1,2,512,512]{3,2,1,0:T(8,128)} %convolution_bitcast_fusion.1) | copy-start | bytes 6291460
  97.3 4.6 %copy-start = (f32[3,2,512,512]{3,2,1,0:T(8,128)}, f32[3,2,512,512]{3,2,1,0:T(8,128)S(1)}, u32[]{:S(2)}) copy-start(f32[3,2,512,512]{3,2,1,0:T(8,128)S(1)} %maximum_multiply_fusion) | copy-start | bytes 18874372
  116.5 0.8 copy-start.19
Sparse Core Ops, SparseCore 0:
  116.6 111.3 reduce-scatter.1
where the time goes:
time: 246 us
  waiting for transfers between devices  79.6 us (32%)
  local copies, waits for them, and re-layouts  50.1 us (20%)
  blocking collectives  39.5 us (16%)
  other arithmetic  37.9 us (15%)
  between operations  18 us (7%)
  matrix products  13.7 us (6%)
  starting transfers between devices  6.74 us (3%)
    reduce_scatter x1, waiting for transfers between devices, on_device(): lax.psum_scatter(local_terms, ('wide', 'narrow'), scatter_dimension=2, ti...  79.6 us
    all_gather x1, blocking collectives, on_device(): piece = lax.all_gather(peram, 'wide', axis=1, tiled=True)  30.8 us
    mul x8, local copies, waits for them, and re-layouts, covariant_product(): out_real = jnp.sum(link_real * vec_real - link_imag * vec_imag, axis=2)  13.8 us
    dot_general x3, matrix products, on_device(): lax.dot_general(left_block, product, (((1,), (1,)), ((), ())), preferred_...  12.7 us
    unnamed x45, local copies, waits for them, and re-layouts  9.99 us
    all_gather x1, blocking collectives, on_device(): elementals = lax.all_gather(thin_rows, 'narrow', axis=2, tiled=True)  8.72 us
    another operation x2, other arithmetic, on_device(): jnp.stack([real_part - jnp.swapaxes(real_part, 1, 2), imag_part + jnp.swa...  8.68 us
    reduce_sum x3, other arithmetic, covariant_product(): out_real = jnp.sum(link_real * vec_real - link_imag * vec_imag, axis=2)  7.61 us
  transfers between devices with their start and end apart: 3, of which 1 were waited for; matrix products, arithmetic and copies ran while one was open for 7% of the time, Pallas kernels for 0%

commit v1 on v0

v1 whole, which is shorter than its diff:
```python
import functools
import math

import jax
import jax.numpy as jnp
from jax import lax
from jax.experimental import pallas as pl
from jax.experimental.pallas import tpu as pltpu
from jax.sharding import PartitionSpec as P

LZ = 16
COMP = 6
VMEM_BYTES = 40 * 1024 * 1024
FLOAT = jnp.float32
SHORT = jnp.bfloat16

VMEM_SPEC = pl.BlockSpec(memory_space=pltpu.VMEM)
SMEM_SPEC = pl.BlockSpec(memory_space=pltpu.SMEM)


def call(kernel, out_shape, in_specs, scratch=(), flops=0, size=0):
    return pl.pallas_call(
        kernel,
        out_shape=out_shape,
        in_specs=in_specs,
        out_specs=jax.tree.map(lambda _: VMEM_SPEC, out_shape),
        scratch_shapes=list(scratch),
        compiler_params=pltpu.CompilerParams(vmem_limit_bytes=VMEM_BYTES),
        cost_estimate=pl.CostEstimate(flops=flops, bytes_accessed=size, transcendentals=0),
    )


def from_behind(x, axis, by):
    length = lax.axis_size(axis)
    return lax.ppermute(x, axis, [(i, (i + by) % length) for i in range(length)])


def swap(x, axis, mask):
    length = lax.axis_size(axis)
    return lax.ppermute(x, axis, [(i, i ^ mask) for i in range(length)])


def split_kernel(planes, x_ref, all_ref, first_ref, edge_ref, wide_scr):
    count = all_ref.shape[0]
    length = x_ref.shape[1]
    per_tile = length // LZ
    wide_scr[...] = x_ref[...].astype(FLOAT)
    lane = lax.broadcasted_iota(jnp.int32, (count, length), 1)
    tiles = [jnp.zeros((count, length), FLOAT)] * (edge_ref.shape[1] // length)
    for plane in range(planes):
        for comp in range(COMP):
            values = wide_scr[pl.ds(comp * planes + plane, count, stride=COMP * planes), :]
            low = values.astype(SHORT)
            at = (plane * COMP + comp) * length
            all_ref[:, at : at + length] = low
            if plane == 0:
                first_ref[:, comp * length : (comp + 1) * length] = low
            tile, slot = divmod(plane * COMP + comp, per_tile)
            moved = values if slot == 0 else pltpu.roll(values, slot * LZ, 1)
            tiles[tile] = jnp.where(lane // LZ == slot, moved, tiles[tile])
    for tile, values in enumerate(tiles):
        edge_ref[:, tile * length : (tile + 1) * length] = values.astype(SHORT)


def split_vectors(vectors):
    count, _, _, planes, length = vectors.shape
    rows = COMP * planes
    edge_tiles = -(-rows // (length // LZ))
    block = 64
    shapes = [rows * length, COMP * length, edge_tiles * length]
    return pl.pallas_call(
        functools.partial(split_kernel, planes),
        grid=(count // block,),
        out_shape=[jax.ShapeDtypeStruct((count, s), SHORT) for s in shapes],
        in_specs=[pl.BlockSpec((block * rows, length), lambda i: (i, 0))],
        out_specs=[pl.BlockSpec((block, s), lambda i: (i, 0)) for s in shapes],
        scratch_shapes=[pltpu.VMEM((block * rows, length), FLOAT)],
        compiler_params=pltpu.CompilerParams(vmem_limit_bytes=VMEM_BYTES),
    )(vectors.reshape(count * rows, length))


def times_transposed(left, right):
    return lax.dot_general(left, right, (((1,), (1,)), ((), ())), preferred_element_type=FLOAT)


def direction_kernel(direction, chosen, planes, norm, has_more, has_halo, *refs):
    here_ref, links_ref, vec_ref = refs[:3]
    rest = list(refs[3:])
    halo_ref = rest.pop(0) if has_halo else None
    more_ref = rest.pop(0) if has_more is True else None
    if has_more == "first":
        whole_ref, fwd_scr, rot_scr = rest
        packed = whole_ref
    else:
        keep_ref, send_ref, fwd_scr, rot_scr, packed = rest
    count = vec_ref.shape[0]
    length = links_ref.shape[1]
    part = 3 * length
    per_tile = length // LZ
    group = 16
    lane = lax.broadcasted_iota(jnp.int32, (group, length), 1)

    def ahead(rows, plane, comp):
        at = (plane * COMP + comp) * length
        if direction == 0:
            if plane + 1 < planes:
                return vec_ref[rows, at + COMP * length : at + (COMP + 1) * length].astype(FLOAT)
            return halo_ref[rows, comp * length : (comp + 1) * length].astype(FLOAT)
        values = vec_ref[rows, at : at + length].astype(FLOAT)
        if direction == 1:
            tile, slot = divmod(plane * COMP + comp, per_tile)
            edge = halo_ref[rows, tile * length : (tile + 1) * length].astype(FLOAT)
            shift = length - LZ - slot * LZ
            edge = edge if shift == 0 else pltpu.roll(edge, shift, 1)
            return jnp.where(lane < length - LZ, pltpu.roll(values, length - LZ, 1), edge)
        return jnp.where(
            lane % LZ == LZ - 1, pltpu.roll(values, LZ - 1, 1), pltpu.roll(values, length - 1, 1)
        )

    for position, plane in enumerate(chosen):
        base = position * COMP * length

        def link(r, a, b):
            row = (((direction * 2 + r) * 3 + a) * 3 + b) * planes + plane
            return links_ref[row : row + 1, :]

        matrix = [[[link(r, a, b) for b in range(3)] for a in range(3)] for r in range(2)]

        def step(index, carry):
            rows = pl.ds(pl.multiple_of(index * group, group), group)
            real = [ahead(rows, plane, b) for b in range(3)]
            imag = [ahead(rows, plane, 3 + b) for b in range(3)]
            for a in range(3):
                out_real = sum(
                    matrix[0][a][b] * real[b] - matrix[1][a][b] * imag[b] for b in range(3)
                )
                out_imag = sum(
                    matrix[0][a][b] * imag[b] + matrix[1][a][b] * real[b] for b in range(3)
                )
                low_real = out_real.astype(SHORT)
                low_imag = out_imag.astype(SHORT)
                at = base + a * length
                fwd_scr[rows, at : at + length] = low_real
                fwd_scr[rows, at + part : at + part + length] = low_imag
                rot_scr[rows, at : at + length] = low_imag
                rot_scr[rows, at + part : at + part + length] = -low_real
            return carry

        lax.fori_loop(0, count // group, step, 0)

    here = here_ref[0]
    pieces = packed.shape[0]
    size = packed.shape[2]
    tile = min(256, count)
    first = chosen[0] * COMP * length
    depth = len(chosen) * COMP * length
    row = lax.broadcasted_iota(jnp.int32, (tile, tile), 0)
    col = lax.broadcasted_iota(jnp.int32, (tile, tile), 1)

    def vec(i):
        return vec_ref[i * tile : (i + 1) * tile, first : first + depth]

    def fwd(i):
        return fwd_scr[i * tile : (i + 1) * tile, :]

    def rot(i):
        return rot_scr[i * tile : (i + 1) * tile, :]

    for i in range(count // tile):
        for j in range(count // tile):
            if i < j:
                value = times_transposed(vec(i), fwd(j)) - times_transposed(fwd(i), vec(j))
            elif i > j:
                value = times_transposed(vec(i), rot(j)) + times_transposed(rot(i), vec(j))
            else:
                real = times_transposed(vec(i), fwd(i))
                imag = times_transposed(vec(i), rot(i))
                other = jnp.where(row > col, -real, imag)
                value = jnp.where(row < col, real, imag) + other.T
            value = value * norm
            for p in range(tile // size):
                for q in range(tile // size):
                    block_row = i * (tile // size) + p
                    block_col = j * (tile // size) + q
                    slot = here ^ (block_row ^ block_col)
                    block = value[p * size : (p + 1) * size, q * size : (q + 1) * size]
                    if more_ref is not None:
                        block = block + more_ref[slot, block_row]
                    packed[slot, block_row] = block
    if has_more != "first":
        for piece in range(pieces // 2):
            keep_ref[piece] = packed[2 * piece]
            send_ref[piece] = packed[2 * piece + 1].astype(SHORT)


def direction_part(direction, chosen, norm, pieces, here, links, vec, halo=None, more=None):
    planes = vec.shape[1] // (COMP * links.shape[1])
    count = vec.shape[0]
    size = count // pieces
    depth = len(chosen) * COMP * links.shape[1]
    whole = jax.ShapeDtypeStruct((pieces, pieces, size, size), FLOAT)
    if more == "first":
        out_shape = whole
    else:
        half = (pieces // 2, pieces, size, size)
        out_shape = [jax.ShapeDtypeStruct(half, FLOAT), jax.ShapeDtypeStruct(half, SHORT)]
    scratch = [pltpu.VMEM((count, depth), SHORT)] * 2
    if more != "first":
        scratch.append(pltpu.VMEM(whole.shape, FLOAT))
    operands = [here, links, vec]
    if halo is not None:
        operands.append(halo)
    has_more = more if more == "first" else more is not None
    if has_more is True:
        operands.append(more)
    return call(
        functools.partial(
            direction_kernel, direction, chosen, planes, norm, has_more, halo is not None
        ),
        out_shape,
        [SMEM_SPEC] + [VMEM_SPEC] * (len(operands) - 1),
        scratch,
        flops=4 * count * count * depth,
        size=8 * count * depth,
    )(*operands)


def expand_kernel(here_ref, keep_ref, came_ref, own_ref, *rest):
    send_refs, sum_scr, rows_scr = rest[:-2], rest[-2], rest[-1]
    narrow, wide = here_ref[0], here_ref[1]
    kinds, pieces, size, _ = keep_ref.shape
    rows = own_ref.shape[2]
    per_block = size // rows
    row = lax.broadcasted_iota(jnp.int32, (size, size), 0)
    col = lax.broadcasted_iota(jnp.int32, (size, size), 1)
    sum_scr[...] = keep_ref[...] + came_ref[...].astype(FLOAT)
    for kind in range(kinds):
        for block in range(pieces):
            across = narrow ^ block
            mine = sum_scr[kind, block]
            other = sum_scr[kind, across].T
            ahead = row + block * size - col - across * size
            real = jnp.where(ahead < 0, mine, jnp.where(ahead > 0, -other, 0.0))
            imag = jnp.where(ahead < 0, other, mine)
            for part in range(per_block):
                at = slice(part * rows, (part + 1) * rows)
                rows_scr[block * per_block + part, kind, 0] = real[at]
                rows_scr[block * per_block + part, kind, 1] = imag[at]
    own_ref[...] = rows_scr[wide]
    for index, ref in enumerate(send_refs):
        ref[...] = rows_scr[wide ^ (index + 1)].astype(SHORT)


def expand(here, keep, came, wide_count):
    kinds, pieces, size, _ = keep.shape
    rows = pieces * size // wide_count
    shape = (kinds, 2, rows, size)
    out_shape = [jax.ShapeDtypeStruct(shape, FLOAT)]
    out_shape += [jax.ShapeDtypeStruct(shape, SHORT)] * (wide_count - 1)
    return call(
        expand_kernel,
        out_shape,
        [SMEM_SPEC, VMEM_SPEC, VMEM_SPEC],
        [pltpu.VMEM(keep.shape, FLOAT), pltpu.VMEM((wide_count,) + shape, FLOAT)],
    )(here, keep, came)


def finish_kernel(here_ref, list_ref, rows_ref, peram_ref, elem_ref, prod_ref, left_scr, right_scr):
    narrow, wide = here_ref[0], here_ref[1]
    pieces, _, _, rows, size = rows_ref.shape
    slots = list_ref.shape[0]
    wide_count, _, share, cols = peram_ref.shape
    total = pieces * size
    mine = wide * rows // size
    for slot in range(slots):
        kind = list_ref[slot]
        for block in range(pieces):
            piece = rows_ref[narrow ^ block ^ mine, kind]
            at = slice(block * size, (block + 1) * size)
            elem_ref[slot, :, :, at] = piece.astype(FLOAT)
            for r in range(2):
                left_scr[
                    slot * rows : (slot + 1) * rows,
                    r * total + block * size : r * total + (block + 1) * size,
                ] = piece[r]
    for owner in range(wide_count):
        real = peram_ref[wide ^ owner, 0]
        imag = peram_ref[wide ^ owner, 1]
        up = slice(owner * share, (owner + 1) * share)
        down = slice(total + owner * share, total + (owner + 1) * share)
        right_scr[0, up, :] = real
        right_scr[0, down, :] = -imag
        right_scr[1, up, :] = imag
        right_scr[1, down, :] = real
    for r in range(2):
        product = jnp.dot(left_scr[...], right_scr[r], preferred_element_type=FLOAT)
        for slot in range(slots):
            prod_ref[slot, r] = product[slot * rows : (slot + 1) * rows]


def finish(here, directions, rows, peram):
    pieces, _, _, row_count, size = rows.shape
    slots = directions.shape[0]
    cols = peram.shape[-1]
    total = pieces * size
    return call(
        finish_kernel,
        [
            jax.ShapeDtypeStruct((slots, 2, row_count, total), FLOAT),
            jax.ShapeDtypeStruct((slots, 2, row_count, cols), FLOAT),
        ],
        [SMEM_SPEC, SMEM_SPEC, VMEM_SPEC, VMEM_SPEC],
        [
            pltpu.VMEM((slots * row_count, 2 * total), SHORT),
            pltpu.VMEM((2, 2 * total, cols), SHORT),
        ],
    )(here, directions, rows, peram)


def gather(x, axis, masks):
    stack = x[None]
    for mask in masks:
        stack = jnp.concatenate([stack, swap(stack, axis, mask)], 0)
    return stack


def on_device(vectors, links, directions, peram):
    planes = vectors.shape[3]
    length = vectors.shape[4]
    wide_count = lax.axis_size("wide")
    narrow_count = lax.axis_size("narrow")
    norm = 1.0 / math.sqrt(12.0 * planes * wide_count * length * narrow_count)
    here = jnp.stack([lax.axis_index("narrow"), lax.axis_index("wide")]).astype(jnp.int32)
    link_rows = links.reshape(-1, length)

    vec, first, edge = split_vectors(vectors)
    plane_halo = from_behind(first, "wide", -1)
    edge_halo = from_behind(edge, "narrow", -1)
    every = tuple(range(planes))
    part = functools.partial(
        direction_part, norm=norm, pieces=narrow_count, here=here, links=link_rows, vec=vec
    )
    third = part(2, every)
    second = part(1, every, halo=edge_halo)
    inner = part(0, every[:-1], more="first")
    whole = part(0, every[-1:], halo=plane_halo, more=inner)

    parts = [whole, second, third]
    keep = jnp.stack([k for k, _ in parts])
    send = jnp.stack([s for _, s in parts])
    came = swap(send, "narrow", 1)
    for stage in range(1, narrow_count.bit_length() - 1):
        total = keep + came.astype(FLOAT)
        keep = total[:, 0::2]
        came = swap(total[:, 1::2].astype(SHORT), "narrow", 1 << stage)
    own, *sends = expand(here, keep[:, 0], came[:, 0], wide_count)
    for index, piece in enumerate(sends):
        own = own + swap(piece, "wide", index + 1).astype(FLOAT)
    masks = [1 << stage for stage in range(narrow_count.bit_length() - 1)]
    low = own.astype(SHORT)
    stack = low[None]
    for mask in reversed(masks):
        stack = jnp.concatenate([stack, swap(stack, "narrow", mask)], 0)
    order = [0]
    for mask in reversed(masks):
        order = order + [o ^ mask for o in order]
    rows = jnp.stack([stack[order.index(j)] for j in range(narrow_count)])
    peram_all = gather(peram, "wide", [1 << s for s in range(wide_count.bit_length() - 1)])
    return tuple(finish(here, directions, rows, peram_all))


def solution(mesh):
    placed = (
        P("grp", None, None, "wide", "narrow"),
        P("grp", None, None, None, "wide", "narrow"),
        P(),
        P("grp", "wide", "narrow"),
    )
    return jax.shard_map(
        on_device,
        mesh=mesh,
        in_specs=placed,
        out_specs=(P("grp", None, "wide", None), P("grp", None, "wide", "narrow")),
        check_vma=False,
    )
```

time: 246 us -> 85.4 us (0.35)
  local copies, waits for them, and re-layouts: 50.1 us -> 1.58 us
  waiting for transfers between devices: 79.6 us -> 34.3 us
  blocking collectives: 39.5 us -> 0 us
  other arithmetic: 37.9 us -> 0.66 us
  Pallas kernels: 0 us -> 28 us
  between operations: 18 us -> 0.83 us
  matrix products: 13.7 us -> 0 us
  starting transfers between devices: 6.74 us -> 19.9 us
    reduce_scatter x1 -> x0, waiting for transfers between devices: 79.6 us -> none  [on_device(): lax.psum_scatter(local_terms, ('wide', 'narrow'), scatter_dimension=2, ti...]
    all_gather x2 -> x0, blocking collectives: 39.5 us -> none  [the longest x1 30.8 us: on_device(): piece = lax.all_gather(peram, 'wide', axis=1, tiled=True)]
    ppermute x0 -> x14, waiting for transfers between devices: none -> 34.3 us  [swap(): return lax.ppermute(x, axis, [(i, i ^ mask) for i in range(length)])]
    pallas_call x0 -> x7, Pallas kernels: none -> 28 us  [the longest x4 23.9 us: direction_part(): call(functools.partial(direction_kernel, direction, chosen, planes, norm,...]
    mul x8 -> x0, local copies, waits for them, and re-layouts: 13.8 us -> none  [covariant_product(): out_real = jnp.sum(link_real * vec_real - link_imag * vec_imag, axis=2)]
    dot_general x4 -> x0, matrix products: 13.7 us -> none  [the longest x3 12.7 us: on_device(): lax.dot_general(left_block, product, (((1,), (1,)), ((), ())), preferred_...]
    ppermute x0 -> x14, starting transfers between devices: none -> 13.1 us  [swap(): return lax.ppermute(x, axis, [(i, i ^ mask) for i in range(length)])]
    another operation x5 -> x3, other arithmetic: 9.12 us -> 0.22 us  [the longest x1 0.09 us: on_device(): send = jnp.stack([s for _, s in parts])]
  transfers between devices with their start and end apart: 3 -> 16, of which waited for: 1 -> 9; matrix products, arithmetic and copies ran while one was open for 7% -> 0% of each run, Pallas kernels for 0% -> 25%
where the time goes in v1:
time: 85.4 us; the launch traced here: 85.3 us
  waiting for transfers between devices  34.3 us (40%)
  Pallas kernels  28 us (33%)
  starting transfers between devices  19.9 us (23%)
  local copies, waits for them, and re-layouts  1.58 us (2%)
    ppermute x14, waiting for transfers between devices, swap(): return lax.ppermute(x, axis, [(i, i ^ mask) for i in range(length)])  34.3 us
    pallas_call x4, Pallas kernels, direction_part(): call(functools.partial(direction_kernel, direction, chosen, planes, norm,...  23.9 us
    ppermute x14, starting transfers between devices, swap(): return lax.ppermute(x, axis, [(i, i ^ mask) for i in range(length)])  13.1 us
    ppermute x2, starting transfers between devices, from_behind(): lax.ppermute(x, axis, [(i, (i + by) % length) for i in range(length)])  6.71 us
    pallas_call x1, Pallas kernels, finish(): call(finish_kernel, [jax.ShapeDtypeStruct((slots, 2, row_count, total), F...  1.73 us
  transfers between devices with their start and end apart: 16, of which 9 were waited for; matrix products, arithmetic and copies ran while one was open for 0% of the time, Pallas kernels for 25%

profile of v1, /device:TPU:0, one launch (start us, length us, event | category | flops | bytes accessed | tf_op | source)
XLA Modules:
  0.0 85.3 jit_solution(12730484007739594618)
XLA Ops:
  0.6 1.4 %copy-done = bf16[512,2,3,2,128]{4,3,2,1,0:T(2,128)(2,1)S(1)} copy-done((bf16[512,2,3,2,128]{4,3,2,1,0:T(2,128)(2,1)S(1)}, bf16[512,2,3,2,128]{4,3,2,1,0:T(2,128)(2,1)}, u32[]{:S(2)}) %copy-start) | copy-done | bytes 1572888
  2.0 1.4 %shard_map.59 = (bf16[512,1536]{1,0:T(8,128)(2,1)S(1)}, bf16[512,768]{1,0:T(8,128)(2,1)S(1)}, bf16[512,256]{1,0:T(8,128)(2,1)S(1)}) custom-call(bf16[6144,128]{1,0:T(8,128)(2,1)S(1)} %bitcast.15), custom_call_target="tpu_custom_call" | custom-call | tf_op jit(solution)/shard_map/pallas_call | solution.py:71
  3.4 6.1 %collective-permute-start = (bf16[512,768]{1,0:T(8,128)(2,1)S(1)}, bf16[512,768]{1,0:T(8,128)(2,1)S(1)}, u32[]{:S(2)}, u32[]{:S(2)}) collective-permute-start(bf16[512,768]{1,0:T(8,128)(2,1)S(1)} %get-tuple-element.20), channel_id=1, source_target_pairs={{0,28},{4,0},{8,4},{12,8},{16,12},{20,16},{24,20},{28,24},{1,29},{... | collective-permute-start | bytes 2359304 | tf_op jit(solution)/shard_map/ppermute | solution.py:35
  9.5 0.7 collective-permute-start.1
  10.1 0.1 pad_add_fusion.refs_0_.here_ref
  10.3 2.6 %shard_map.60.refs_4_ = f32[4,4,128,128]{3,2,1,0:T(8,128)S(1)} custom-call(s32[2]{0:T(128)S(1)} %pad_add_fusion.refs_0_.here_ref, f32[108,128]{1,0:T(8,128)S(1)} %reshape.10.refs_1_, bf16[512,1536]{1,0:T(8,128)(2,1)S(1)} %get-tuple-element.19.refs_2_), custom_call_target="tpu_custom_call" | custom-call | flops 805306368 | bytes 3145728 | tf_op jit(solution)/shard_map/pallas_call | solution.py:216
  12.9 9.1 %shard_map.63 = (f32[2,4,128,128]{3,2,1,0:T(8,128)S(1)}, bf16[2,4,128,128]{3,2,1,0:T(8,128)(2,1)S(1)}) custom-call(s32[2]{0:T(128)S(1)} %pad_add_fusion.refs_0_.here_ref, f32[108,128]{1,0:T(8,128)S(1)} %reshape.10.refs_1_, bf16[512,1536]{1,0:T(8,128)(2,1)S(1)} %get-tuple-element.19.refs_2_), custom_call_target="tpu_custom_call" | custom-call | flops 1610612736 | bytes 6291456 | tf_op jit(solution)/shard_map/pallas_call | solution.py:216
  22.0 9.5 %shard_map.62 = (f32[2,4,128,128]{3,2,1,0:T(8,128)S(1)}, bf16[2,4,128,128]{3,2,1,0:T(8,128)(2,1)S(1)}) custom-call(s32[2]{0:T(128)S(1)} %pad_add_fusion.refs_0_.here_ref, f32[108,128]{1,0:T(8,128)S(1)} %reshape.10.refs_1_, bf16[512,1536]{1,0:T(8,128)(2,1)S(1)} %get-tuple-element.19.refs_2_, bf16[512,256]{1,0:T(8,128)(2,1)} %collective-permute-done.1.refs_3_), custom_call_target="tpu_custom_call" | custom-call | flops 1610612736 | bytes 6291456 | tf_op jit(solution)/shard_map/pallas_call | solution.py:216
  31.6 2.7 %shard_map.61 = (f32[2,4,128,128]{3,2,1,0:T(8,128)S(1)}, bf16[2,4,128,128]{3,2,1,0:T(8,128)(2,1)S(1)}) custom-call(s32[2]{0:T(128)S(1)} %pad_add_fusion.refs_0_.here_ref, f32[108,128]{1,0:T(8,128)S(1)} %reshape.10.refs_1_, bf16[512,1536]{1,0:T(8,128)(2,1)S(1)} %get-tuple-element.19.refs_2_, bf16[512,768]{1,0:T(8,128)(2,1)S(1)} %collective-permute-done.refs_3_, ...), custom_call_target="tpu_custom_call" | custom-call | flops 805306368 | bytes 3145728 | tf_op jit(solution)/shard_map/pallas_call | solution.py:216
  34.2 0.1 pad_maximum_fusion
  34.4 2.3 %collective-permute-done.2 = bf16[3,2,4,128,128]{4,3,2,0,1:T(8,128)(2,1)S(1)} collective-permute-done((bf16[3,2,4,128,128]{4,3,2,0,1:T(8,128)(2,1)S(1)}, bf16[3,2,4,128,128]{4,3,2,0,1:T(8,128)(2,1)S(1)}, u32[]{:S(2)}, u32[]{:S(2)}) %collective-permute-start.2) | collective-permute-done | bytes 786464 | tf_op jit(solution)/shard_map/ppermute | solution.py:40
  36.7 0.2 maximum_add_fusion
  37.0 1.1 %collective-permute-start.3 = (bf16[3,1,4,128,128]{4,3,2,0,1:T(8,128)(2,1)S(1)}, bf16[3,1,4,128,128]{4,3,2,0,1:T(8,128)(2,1)S(1)}, u32[]{:S(2)}, u32[]{:S(2)}) collective-permute-start(bf16[3,1,4,128,128]{4,3,2,0,1:T(8,128)(2,1)S(1)} %slice.25), channel_id=1, source_target_pairs={{0,2},{1,3},{2,0},{3,1},{4,6},{5,7},{6,4},{7,5},{8,10},{9,11},{10,... | collective-permute-start | bytes 1179656 | tf_op jit(solution)/shard_map/ppermute | solution.py:40
  38.1 10.1 %collective-permute-done.3 = bf16[3,1,4,128,128]{4,3,2,0,1:T(8,128)(2,1)S(1)} collective-permute-done((bf16[3,1,4,128,128]{4,3,2,0,1:T(8,128)(2,1)S(1)}, bf16[3,1,4,128,128]{4,3,2,0,1:T(8,128)(2,1)S(1)}, u32[]{:S(2)}, u32[]{:S(2)}) %collective-permute-start.3) | collective-permute-done | bytes 393248 | tf_op jit(solution)/shard_map/ppermute | solution.py:40
  48.2 1.0 %shard_map.64 = (f32[3,2,64,128]{3,2,1,0:T(8,128)S(1)}, bf16[3,2,64,128]{3,2,1,0:T(8,128)(2,1)S(1)}, bf16[3,2,64,128]{3,2,1,0:T(8,128)(2,1)S(1)}, bf16[3,2,64,12...) custom-call(s32[2]{0:T(128)S(1)} %pad_add_fusion.refs_0_.here_ref, ...), custom_call_target="tpu_custom_call" | custom-call | tf_op jit(solution)/shard_map/pallas_call | solution.py:260
  49.2 0.6 collective-permute-start.10
  49.8 1.4 %collective-permute-start.4 = (bf16[3,2,64,128]{3,2,1,0:T(8,128)(2,1)S(1)}, bf16[3,2,64,128]{3,2,1,0:T(8,128)(2,1)S(1)}, u32[]{:S(2)}, u32[]{:S(2)}) collective-permute-start(bf16[3,2,64,128]{3,2,1,0:T(8,128)(2,1)S(1)} %get-tuple-element.29), channel_id=1, source_target_pairs={{0,4},{4,0},{8,12},{12,8},{16,20},{20,16},{24,28},{28,24},{1,5},{5... | collective-permute-start | bytes 294920 | tf_op jit(solution)/shard_map/ppermute | solution.py:40
  51.2 2.1 %collective-permute-start.6 = (bf16[3,2,64,128]{3,2,1,0:T(8,128)(2,1)S(1)}, bf16[3,2,64,128]{3,2,1,0:T(8,128)(2,1)S(1)}, u32[]{:S(2)}, u32[]{:S(2)}) collective-permute-start(bf16[3,2,64,128]{3,2,1,0:T(8,128)(2,1)S(1)} %get-tuple-element.31), channel_id=1, source_target_pairs={{0,12},{4,8},{8,4},{12,0},{16,28},{20,24},{24,20},{28,16},{1,13},{... | collective-permute-start | bytes 294920 | tf_op jit(solution)/shard_map/ppermute | solution.py:40
  53.2 1.9 %collective-permute-start.7 = (bf16[3,2,64,128]{3,2,1,0:T(8,128)(2,1)S(1)}, bf16[3,2,64,128]{3,2,1,0:T(8,128)(2,1)S(1)}, u32[]{:S(2)}, u32[]{:S(2)}) collective-permute-start(bf16[3,2,64,128]{3,2,1,0:T(8,128)(2,1)S(1)} %get-tuple-element.32), channel_id=1, source_target_pairs={{0,16},{4,20},{8,24},{12,28},{16,0},{20,4},{24,8},{28,12},{1,17},{... | collective-permute-start | bytes 294920 | tf_op jit(solution)/shard_map/ppermute | solution.py:40
  55.1 2.5 %collective-permute-done.10 = bf16[3,2,64,128]{3,2,1,0:T(8,128)(2,1)S(1)} collective-permute-done((bf16[3,2,64,128]{3,2,1,0:T(8,128)(2,1)S(1)}, bf16[3,2,64,128]{3,2,1,0:T(8,128)(2,1)S(1)}, u32[]{:S(2)}, u32[]{:S(2)}) %collective-permute-start.10) | collective-permute-done | bytes 98336 | tf_op jit(solution)/shard_map/ppermute | solution.py:40
  57.6 2.8 %collective-permute-start.9 = (bf16[3,2,64,128]{3,2,1,0:T(8,128)(2,1)S(1)}, bf16[3,2,64,128]{3,2,1,0:T(8,128)(2,1)S(1)}, u32[]{:S(2)}, u32[]{:S(2)}) collective-permute-start(bf16[3,2,64,128]{3,2,1,0:T(8,128)(2,1)S(1)} %get-tuple-element.34), channel_id=1, source_target_pairs={{0,24},{4,28},{8,16},{12,20},{16,8},{20,12},{24,0},{28,4},{1,25},{... | collective-permute-start | bytes 294920 | tf_op jit(solution)/shard_map/ppermute | solution.py:40
  60.4 1.1 %collective-permute-done.6 = bf16[3,2,64,128]{3,2,1,0:T(8,128)(2,1)S(1)} collective-permute-done((bf16[3,2,64,128]{3,2,1,0:T(8,128)(2,1)S(1)}, bf16[3,2,64,128]{3,2,1,0:T(8,128)(2,1)S(1)}, u32[]{:S(2)}, u32[]{:S(2)}) %collective-permute-start.6) | collective-permute-done | bytes 98336 | tf_op jit(solution)/shard_map/ppermute | solution.py:40
  61.5 4.2 %collective-permute-done.7 = bf16[3,2,64,128]{3,2,1,0:T(8,128)(2,1)S(1)} collective-permute-done((bf16[3,2,64,128]{3,2,1,0:T(8,128)(2,1)S(1)}, bf16[3,2,64,128]{3,2,1,0:T(8,128)(2,1)S(1)}, u32[]{:S(2)}, u32[]{:S(2)}) %collective-permute-start.7) | collective-permute-done | bytes 98336 | tf_op jit(solution)/shard_map/ppermute | solution.py:40
  65.6 3.1 %collective-permute-done.8 = bf16[3,2,64,128]{3,2,1,0:T(8,128)(2,1)S(1)} collective-permute-done((bf16[3,2,64,128]{3,2,1,0:T(8,128)(2,1)S(1)}, bf16[3,2,64,128]{3,2,1,0:T(8,128)(2,1)S(1)}, u32[]{:S(2)}, u32[]{:S(2)}) %collective-permute-start.8) | collective-permute-done | bytes 98336 | tf_op jit(solution)/shard_map/ppermute | solution.py:40
  68.8 0.1 fusion
  68.9 1.5 %collective-permute-start.11 = (bf16[1,3,2,64,128]{4,3,2,1,0:T(8,128)(2,1)S(1)}, bf16[1,3,2,64,128]{4,3,2,1,0:T(8,128)(2,1)S(1)}, u32[]{:S(2)}, u32[]{:S(2)}) collective-permute-start(bf16[1,3,2,64,128]{4,3,2,1,0:T(8,128)(2,1)S(1)} %fusion), channel_id=1, source_target_pairs={{0,2},{1,3},{2,0},{3,1},{4,6},{5,7},{6,4},{7,5},{8,10},{9,11},{10,... | collective-permute-start | bytes 294920 | tf_op jit(solution)/shard_map/ppermute | solution.py:40
  70.4 0.7 collective-permute-start.14
  71.1 2.5 %collective-permute-done.11 = bf16[1,3,2,64,128]{4,3,2,1,0:T(8,128)(2,1)S(1)} collective-permute-done((bf16[1,3,2,64,128]{4,3,2,1,0:T(8,128)(2,1)S(1)}, bf16[1,3,2,64,128]{4,3,2,1,0:T(8,128)(2,1)S(1)}, u32[]{:S(2)}, u32[]{:S(2)}) %collective-permute-start.11) | collective-permute-done | bytes 98336 | tf_op jit(solution)/shard_map/ppermute | solution.py:40
  73.7 1.1 %collective-permute-done.14 = bf16[2,2,64,64]{3,2,1,0:T(8,128)(2,1)S(1)} collective-permute-done((bf16[2,2,64,64]{3,2,1,0:T(8,128)(2,1)S(1)}, bf16[2,2,64,64]{3,2,1,0:T(8,128)(2,1)S(1)}, u32[]{:S(2)}, u32[]{:S(2)}) %collective-permute-start.14) | collective-permute-done | bytes 32800 | tf_op jit(solution)/shard_map/ppermute | solution.py:40
  74.8 1.0 %collective-permute-start.15 = (bf16[4,2,64,64]{3,2,1,0:T(8,128)(2,1)S(1)}, bf16[4,2,64,64]{3,2,1,0:T(8,128)(2,1)S(1)}, u32[]{:S(2)}, u32[]{:S(2)}) collective-permute-start(bf16[4,2,64,64]{3,2,1,0:T(8,128)(2,1)S(1)} %pad_maximum_fusion.4), channel_id=1, source_target_pairs={{0,16},{4,20},{8,24},{12,28},{16,0},{20,4},{24,8},{28,12},{1,17},{... | collective-permute-start | bytes 196616 | tf_op jit(solution)/shard_map/ppermute | solution.py:40
  75.8 7.6 %collective-permute-done.15 = bf16[4,2,64,64]{3,2,1,0:T(8,128)(2,1)S(1)} collective-permute-done((bf16[4,2,64,64]{3,2,1,0:T(8,128)(2,1)S(1)}, bf16[4,2,64,64]{3,2,1,0:T(8,128)(2,1)S(1)}, u32[]{:S(2)}, u32[]{:S(2)}) %collective-permute-start.15) | collective-permute-done | bytes 65568 | tf_op jit(solution)/shard_map/ppermute | solution.py:40
  83.5 1.7 %shard_map.65 = (f32[3,2,64,512]{3,2,1,0:T(8,128)}, f32[3,2,64,64]{3,2,1,0:T(8,128)}) custom-call(s32[2]{0:T(128)S(1)} %pad_add_fusion.refs_0_.here_ref, s32[3]{0:T(128)S(1)} %copy-done.1, bf16[4,3,2,64,128]{4,3,2,1,0:T(8,128)(2,1)S(1)} %pad_maximum_fusion.1.rows_ref, bf16[8,2,64,64]{3,2,1,0:T(8,128)(2,1)S(1)} %pad_maximum_fusion.2.peram_ref), custom_call_target="tpu_custom_call" | custom-call | tf_op jit(solution)/shard_map/pallas_call | solution.py:306
  (28 shorter events, 0.5 us)
Async XLA Ops:
  0.6 1.4 %copy-start = (bf16[512,2,3,2,128]{4,3,2,1,0:T(2,128)(2,1)S(1)}, bf16[512,2,3,2,128]{4,3,2,1,0:T(2,128)(2,1)}, u32[]{:S(2)}) copy-start(bf16[512,2,3,2,128]{4,3,2,1,0:T(2,128)(2,1)} %param.4) | copy-start | bytes 4718596
  2.0 8.2 %copy-start.3 = (f32[3,2,3,3,2,128]{5,4,3,2,1,0:T(2,128)S(1)}, f32[3,2,3,3,2,128]{5,4,3,2,1,0:T(2,128)}, u32[]{:S(2)}) copy-start(f32[3,2,3,3,2,128]{5,4,3,2,1,0:T(2,128)} %param.5) | copy-start | bytes 165892
  3.4 28.1 %collective-permute-start = (bf16[512,768]{1,0:T(8,128)(2,1)S(1)}, bf16[512,768]{1,0:T(8,128)(2,1)S(1)}, u32[]{:S(2)}, u32[]{:S(2)}) collective-permute-start(bf16[512,768]{1,0:T(8,128)(2,1)S(1)} %get-tuple-element.20), channel_id=1, source_target_pairs={{0,28},{4,0},{8,4},{12,8},{16,12},{20,16},{24,20},{28,24},{1,29},{... | collective-permute-start | bytes 2359304 | tf_op jit(solution)/shard_map/ppermute | solution.py:35
  9.5 12.6 %collective-permute-start.1 = (bf16[512,256]{1,0:T(8,128)(2,1)S(1)}, bf16[512,256]{1,0:T(8,128)(2,1)}, u32[]{:S(2)}, u32[]{:S(2)}) collective-permute-start(bf16[512,256]{1,0:T(8,128)(2,1)S(1)} %get-tuple-element.22), channel_id=1, source_target_pairs={{0,3},{1,0},{2,1},{3,2},{4,7},{5,4},{6,5},{7,6},{8,11},{9,8},{10,9... | collective-permute-start | bytes 786440 | tf_op jit(solution)/shard_map/ppermute | solution.py:35
  34.3 2.4 %collective-permute-start.2 = (bf16[3,2,4,128,128]{4,3,2,0,1:T(8,128)(2,1)S(1)}, bf16[3,2,4,128,128]{4,3,2,0,1:T(8,128)(2,1)S(1)}, u32[]{:S(2)}, u32[]{:S(2)}) collective-permute-start(bf16[3,2,4,128,128]{4,3,2,0,1:T(8,128)(2,1)S(1)} %pad_maximum_fusion), channel_id=1, source_target_pairs={{0,1},{1,0},{2,3},{3,2},{4,5},{5,4},{6,7},{7,6},{8,9},{9,8},{10,11... | collective-permute-start | bytes 2359304 | tf_op jit(solution)/shard_map/ppermute | solution.py:40
  37.0 23.4 %copy-start.2 = (bf16[2,64,64]{2,1,0:T(8,128)(2,1)S(1)}, bf16[2,64,64]{2,1,0:T(8,128)(2,1)}, u32[]{:S(2)}) copy-start(bf16[2,64,64]{2,1,0:T(8,128)(2,1)} %param.7) | copy-start | bytes 49156
  37.0 11.2 %collective-permute-start.3 = (bf16[3,1,4,128,128]{4,3,2,0,1:T(8,128)(2,1)S(1)}, bf16[3,1,4,128,128]{4,3,2,0,1:T(8,128)(2,1)S(1)}, u32[]{:S(2)}, u32[]{:S(2)}) collective-permute-start(bf16[3,1,4,128,128]{4,3,2,0,1:T(8,128)(2,1)S(1)} %slice.25), channel_id=1, source_target_pairs={{0,2},{1,3},{2,0},{3,1},{4,6},{5,7},{6,4},{7,5},{8,10},{9,11},{10,... | collective-permute-start | bytes 1179656 | tf_op jit(solution)/shard_map/ppermute | solution.py:40
  49.2 8.4 %collective-permute-start.10 = (bf16[3,2,64,128]{3,2,1,0:T(8,128)(2,1)S(1)}, bf16[3,2,64,128]{3,2,1,0:T(8,128)(2,1)S(1)}, u32[]{:S(2)}, u32[]{:S(2)}) collective-permute-start(bf16[3,2,64,128]{3,2,1,0:T(8,128)(2,1)S(1)} %get-tuple-element.35), channel_id=1, source_target_pairs={{0,28},{4,24},{8,20},{12,16},{16,12},{20,8},{24,4},{28,0},{1,29},{... | collective-permute-start | bytes 294920 | tf_op jit(solution)/shard_map/ppermute | solution.py:40
  49.8 7.8 %collective-permute-start.4 = (bf16[3,2,64,128]{3,2,1,0:T(8,128)(2,1)S(1)}, bf16[3,2,64,128]{3,2,1,0:T(8,128)(2,1)S(1)}, u32[]{:S(2)}, u32[]{:S(2)}) collective-permute-start(bf16[3,2,64,128]{3,2,1,0:T(8,128)(2,1)S(1)} %get-tuple-element.29), channel_id=1, source_target_pairs={{0,4},{4,0},{8,12},{12,8},{16,20},{20,16},{24,28},{28,24},{1,5},{5... | collective-permute-start | bytes 294920 | tf_op jit(solution)/shard_map/ppermute | solution.py:40
  51.2 9.2 %collective-permute-start.5 = (bf16[3,2,64,128]{3,2,1,0:T(8,128)(2,1)S(1)}, bf16[3,2,64,128]{3,2,1,0:T(8,128)(2,1)S(1)}, u32[]{:S(2)}, u32[]{:S(2)}) collective-permute-start(bf16[3,2,64,128]{3,2,1,0:T(8,128)(2,1)S(1)} %get-tuple-element.30), channel_id=1, source_target_pairs={{0,8},{4,12},{8,0},{12,4},{16,24},{20,28},{24,16},{28,20},{1,9},{5... | collective-permute-start | bytes 294920 | tf_op jit(solution)/shard_map/ppermute | solution.py:40
  51.2 10.3 %collective-permute-start.6 = (bf16[3,2,64,128]{3,2,1,0:T(8,128)(2,1)S(1)}, bf16[3,2,64,128]{3,2,1,0:T(8,128)(2,1)S(1)}, u32[]{:S(2)}, u32[]{:S(2)}) collective-permute-start(bf16[3,2,64,128]{3,2,1,0:T(8,128)(2,1)S(1)} %get-tuple-element.31), channel_id=1, source_target_pairs={{0,12},{4,8},{8,4},{12,0},{16,28},{20,24},{24,20},{28,16},{1,13},{... | collective-permute-start | bytes 294920 | tf_op jit(solution)/shard_map/ppermute | solution.py:40
  53.2 12.4 %collective-permute-start.7 = (bf16[3,2,64,128]{3,2,1,0:T(8,128)(2,1)S(1)}, bf16[3,2,64,128]{3,2,1,0:T(8,128)(2,1)S(1)}, u32[]{:S(2)}, u32[]{:S(2)}) collective-permute-start(bf16[3,2,64,128]{3,2,1,0:T(8,128)(2,1)S(1)} %get-tuple-element.32), channel_id=1, source_target_pairs={{0,16},{4,20},{8,24},{12,28},{16,0},{20,4},{24,8},{28,12},{1,17},{... | collective-permute-start | bytes 294920 | tf_op jit(solution)/shard_map/ppermute | solution.py:40
  57.6 11.2 %collective-permute-start.8 = (bf16[3,2,64,128]{3,2,1,0:T(8,128)(2,1)S(1)}, bf16[3,2,64,128]{3,2,1,0:T(8,128)(2,1)S(1)}, u32[]{:S(2)}, u32[]{:S(2)}) collective-permute-start(bf16[3,2,64,128]{3,2,1,0:T(8,128)(2,1)S(1)} %get-tuple-element.33), channel_id=1, source_target_pairs={{0,20},{4,16},{8,28},{12,24},{16,4},{20,0},{24,12},{28,8},{1,21},{... | collective-permute-start | bytes 294920 | tf_op jit(solution)/shard_map/ppermute | solution.py:40
  57.6 11.2 %collective-permute-start.9 = (bf16[3,2,64,128]{3,2,1,0:T(8,128)(2,1)S(1)}, bf16[3,2,64,128]{3,2,1,0:T(8,128)(2,1)S(1)}, u32[]{:S(2)}, u32[]{:S(2)}) collective-permute-start(bf16[3,2,64,128]{3,2,1,0:T(8,128)(2,1)S(1)} %get-tuple-element.34), channel_id=1, source_target_pairs={{0,24},{4,28},{8,16},{12,20},{16,8},{20,12},{24,0},{28,4},{1,25},{... | collective-permute-start | bytes 294920 | tf_op jit(solution)/shard_map/ppermute | solution.py:40
  60.4 10.0 %collective-permute-start.13 = (bf16[1,2,64,64]{3,2,1,0:T(8,128)(2,1)S(1)}, bf16[1,2,64,64]{3,2,1,0:T(8,128)(2,1)S(1)}, u32[]{:S(2)}, u32[]{:S(2)}) collective-permute-start(bf16[1,2,64,64]{3,2,1,0:T(8,128)(2,1)S(1)} %bitcast.23), channel_id=1, source_target_pairs={{0,4},{4,0},{8,12},{12,8},{16,20},{20,16},{24,28},{28,24},{1,5},{5... | collective-permute-start | bytes 49160 | tf_op jit(solution)/shard_map/ppermute | solution.py:40
  68.8 14.8 %copy-start.1 = (s32[3]{0:T(128)S(1)}, s32[3]{0:T(128)}, u32[]{:S(2)}) copy-start(s32[3]{0:T(128)} %list_ref.1) | copy-start | bytes 40
  68.9 4.7 %collective-permute-start.11 = (bf16[1,3,2,64,128]{4,3,2,1,0:T(8,128)(2,1)S(1)}, bf16[1,3,2,64,128]{4,3,2,1,0:T(8,128)(2,1)S(1)}, u32[]{:S(2)}, u32[]{:S(2)}) collective-permute-start(bf16[1,3,2,64,128]{4,3,2,1,0:T(8,128)(2,1)S(1)} %fusion), channel_id=1, source_target_pairs={{0,2},{1,3},{2,0},{3,1},{4,6},{5,7},{6,4},{7,5},{8,10},{9,11},{10,... | collective-permute-start | bytes 294920 | tf_op jit(solution)/shard_map/ppermute | solution.py:40
  70.4 4.3 %collective-permute-start.14 = (bf16[2,2,64,64]{3,2,1,0:T(8,128)(2,1)S(1)}, bf16[2,2,64,64]{3,2,1,0:T(8,128)(2,1)S(1)}, u32[]{:S(2)}, u32[]{:S(2)}) collective-permute-start(bf16[2,2,64,64]{3,2,1,0:T(8,128)(2,1)S(1)} %pad_maximum_fusion.5), channel_id=1, source_target_pairs={{0,8},{4,12},{8,0},{12,4},{16,24},{20,28},{24,16},{28,20},{1,9},{5... | collective-permute-start | bytes 98312 | tf_op jit(solution)/shard_map/ppermute | solution.py:40
  73.6 9.9 %collective-permute-start.12 = (bf16[2,3,2,64,128]{4,3,2,1,0:T(8,128)(2,1)S(1)}, bf16[2,3,2,64,128]{4,3,2,1,0:T(8,128)(2,1)S(1)}, u32[]{:S(2)}, u32[]{:S(2)}) collective-permute-start(bf16[2,3,2,64,128]{4,3,2,1,0:T(8,128)(2,1)S(1)} %pad_maximum_fusion.3), channel_id=1, source_target_pairs={{0,1},{1,0},{2,3},{3,2},{4,5},{5,4},{6,7},{7,6},{8,9},{9,8},{10,11... | collective-permute-start | bytes 589832 | tf_op jit(solution)/shard_map/ppermute | solution.py:40
  74.8 8.6 %collective-permute-start.15 = (bf16[4,2,64,64]{3,2,1,0:T(8,128)(2,1)S(1)}, bf16[4,2,64,64]{3,2,1,0:T(8,128)(2,1)S(1)}, u32[]{:S(2)}, u32[]{:S(2)}) collective-permute-start(bf16[4,2,64,64]{3,2,1,0:T(8,128)(2,1)S(1)} %pad_maximum_fusion.4), channel_id=1, source_target_pairs={{0,16},{4,20},{8,24},{12,28},{16,0},{20,4},{24,8},{28,12},{1,17},{... | collective-permute-start | bytes 196616 | tf_op jit(solution)/shard_map/ppermute | solution.py:40

commit v2 on v1

--- a/solution.py
+++ b/solution.py
@@ -10,7 +10,7 @@
 
 LZ = 16
 COMP = 6
-VMEM_BYTES = 40 * 1024 * 1024
+VMEM_BYTES = 16 * 1024 * 1024
 FLOAT = jnp.float32
 SHORT = jnp.bfloat16
 
@@ -40,42 +40,53 @@
     return lax.ppermute(x, axis, [(i, i ^ mask) for i in range(length)])
 
 
-def split_kernel(planes, x_ref, all_ref, first_ref, edge_ref, wide_scr):
-    count = all_ref.shape[0]
+def split_kernel(planes, x_ref, all_ref, first_ref, edge_ref, held, wide_scr, sems):
+    blocks = sems.shape[0]
+    count = all_ref.shape[0] // blocks
+    rows = count * COMP * planes
     length = x_ref.shape[1]
     per_tile = length // LZ
-    wide_scr[...] = x_ref[...].astype(FLOAT)
     lane = lax.broadcasted_iota(jnp.int32, (count, length), 1)
-    tiles = [jnp.zeros((count, length), FLOAT)] * (edge_ref.shape[1] // length)
-    for plane in range(planes):
-        for comp in range(COMP):
-            values = wide_scr[pl.ds(comp * planes + plane, count, stride=COMP * planes), :]
-            low = values.astype(SHORT)
-            at = (plane * COMP + comp) * length
-            all_ref[:, at : at + length] = low
-            if plane == 0:
-                first_ref[:, comp * length : (comp + 1) * length] = low
-            tile, slot = divmod(plane * COMP + comp, per_tile)
-            moved = values if slot == 0 else pltpu.roll(values, slot * LZ, 1)
-            tiles[tile] = jnp.where(lane // LZ == slot, moved, tiles[tile])
-    for tile, values in enumerate(tiles):
-        edge_ref[:, tile * length : (tile + 1) * length] = values.astype(SHORT)
+    copies = []
+    for block in range(blocks):
+        at = pl.ds(block * rows, rows)
+        copies.append(pltpu.make_async_copy(x_ref.at[at], held.at[at], sems.at[block]))
+        copies[-1].start()
+    for block in range(blocks):
+        copies[block].wait()
+        here = slice(block * count, (block + 1) * count)
+        wide_scr[...] = held[block * rows : (block + 1) * rows].astype(FLOAT)
+        tiles = [jnp.zeros((count, length), FLOAT)] * (edge_ref.shape[1] // length)
+        for plane in range(planes):
+            for comp in range(COMP):
+                values = wide_scr[pl.ds(comp * planes + plane, count, stride=COMP * planes), :]
+                low = values.astype(SHORT)
+                at = (plane * COMP + comp) * length
+                all_ref[here, at : at + length] = low
+                if plane == 0:
+                    first_ref[here, comp * length : (comp + 1) * length] = low
+                tile, slot = divmod(plane * COMP + comp, per_tile)
+                moved = values if slot == 0 else pltpu.roll(values, slot * LZ, 1)
+                tiles[tile] = jnp.where(lane // LZ == slot, moved, tiles[tile])
+        for tile, values in enumerate(tiles):
+            edge_ref[here, tile * length : (tile + 1) * length] = values.astype(SHORT)
 
 
 def split_vectors(vectors):
     count, _, _, planes, length = vectors.shape
     rows = COMP * planes
     edge_tiles = -(-rows // (length // LZ))
-    block = 64
+    blocks = 8
     shapes = [rows * length, COMP * length, edge_tiles * length]
-    return pl.pallas_call(
+    return call(
         functools.partial(split_kernel, planes),
-        grid=(count // block,),
-        out_shape=[jax.ShapeDtypeStruct((count, s), SHORT) for s in shapes],
-        in_specs=[pl.BlockSpec((block * rows, length), lambda i: (i, 0))],
-        out_specs=[pl.BlockSpec((block, s), lambda i: (i, 0)) for s in shapes],
-        scratch_shapes=[pltpu.VMEM((block * rows, length), FLOAT)],
-        compiler_params=pltpu.CompilerParams(vmem_limit_bytes=VMEM_BYTES),
+        [jax.ShapeDtypeStruct((count, s), SHORT) for s in shapes],
+        [pl.BlockSpec(memory_space=pltpu.HBM)],
+        [
+            pltpu.VMEM((count * rows, length), SHORT),
+            pltpu.VMEM((count // blocks * rows, length), FLOAT),
+            pltpu.SemaphoreType.DMA((blocks,)),
+        ],
     )(vectors.reshape(count * rows, length))
 
 
@@ -146,7 +157,7 @@
                 rot_scr[rows, at + part : at + part + length] = -low_real
             return carry
 
-        lax.fori_loop(0, count // group, step, 0)
+        lax.fori_loop(0, count // group, step, 0, unroll=8)
 
     here = here_ref[0]
     pieces = packed.shape[0]
@@ -220,108 +231,203 @@
         out_shape,
         [SMEM_SPEC] + [VMEM_SPEC] * (len(operands) - 1),
         scratch,
-        flops=4 * count * count * depth,
-        size=8 * count * depth,
+        flops=1,
+        size=1,
     )(*operands)
 
 
-def expand_kernel(here_ref, keep_ref, came_ref, own_ref, *rest):
-    send_refs, sum_scr, rows_scr = rest[:-2], rest[-2], rest[-1]
+def halve_kernel(sources, *refs):
+    keep_ref, send_ref = refs[-2:]
+    kind = 0
+    for source in range(sources):
+        held, came = refs[2 * source], refs[2 * source + 1]
+        for k in range(held.shape[0]):
+            for piece in range(held.shape[1] // 2):
+                even, odd = 2 * piece, 2 * piece + 1
+                keep_ref[kind, piece] = held[k, even] + came[k, even].astype(FLOAT)
+                send_ref[kind, piece] = (held[k, odd] + came[k, odd].astype(FLOAT)).astype(SHORT)
+            kind += 1
+
+
+def halve(*pairs):
+    shape = pairs[0][0].shape
+    shape = (sum(held.shape[0] for held, _ in pairs), shape[1] // 2) + shape[2:]
+    return call(
+        functools.partial(halve_kernel, len(pairs)),
+        [jax.ShapeDtypeStruct(shape, FLOAT), jax.ShapeDtypeStruct(shape, SHORT)],
+        [VMEM_SPEC] * (2 * len(pairs)),
+    )(*[x for pair in pairs for x in pair])
+
+
+def expand_kernel(has_extra, here_ref, keep_ref, came_ref, *refs):
+    refs = list(refs)
+    extra_ref = refs.pop(0) if has_extra else None
+    own_ref, send_ref, sum_scr, rows_scr = refs
     narrow, wide = here_ref[0], here_ref[1]
-    kinds, pieces, size, _ = keep_ref.shape
-    rows = own_ref.shape[2]
+    kinds, _, pieces, size, _ = keep_ref.shape
+    half, height, _ = own_ref.shape
+    rows = height // (2 * kinds)
     per_block = size // rows
     row = lax.broadcasted_iota(jnp.int32, (size, size), 0)
     col = lax.broadcasted_iota(jnp.int32, (size, size), 1)
-    sum_scr[...] = keep_ref[...] + came_ref[...].astype(FLOAT)
     for kind in range(kinds):
+        sum_scr[...] = keep_ref[kind, 0] + came_ref[kind, 0].astype(FLOAT)
         for block in range(pieces):
             across = narrow ^ block
-            mine = sum_scr[kind, block]
-            other = sum_scr[kind, across].T
+            mine = sum_scr[block]
+            other = sum_scr[across].T
             ahead = row + block * size - col - across * size
             real = jnp.where(ahead < 0, mine, jnp.where(ahead > 0, -other, 0.0))
             imag = jnp.where(ahead < 0, other, mine)
             for part in range(per_block):
                 at = slice(part * rows, (part + 1) * rows)
-                rows_scr[block * per_block + part, kind, 0] = real[at]
-                rows_scr[block * per_block + part, kind, 1] = imag[at]
-    own_ref[...] = rows_scr[wide]
-    for index, ref in enumerate(send_refs):
-        ref[...] = rows_scr[wide ^ (index + 1)].astype(SHORT)
-
-
-def expand(here, keep, came, wide_count):
-    kinds, pieces, size, _ = keep.shape
-    rows = pieces * size // wide_count
-    shape = (kinds, 2, rows, size)
-    out_shape = [jax.ShapeDtypeStruct(shape, FLOAT)]
-    out_shape += [jax.ShapeDtypeStruct(shape, SHORT)] * (wide_count - 1)
-    return call(
-        expand_kernel,
-        out_shape,
-        [SMEM_SPEC, VMEM_SPEC, VMEM_SPEC],
-        [pltpu.VMEM(keep.shape, FLOAT), pltpu.VMEM((wide_count,) + shape, FLOAT)],
-    )(here, keep, came)
-
-
-def finish_kernel(here_ref, list_ref, rows_ref, peram_ref, elem_ref, prod_ref, left_scr, right_scr):
+                first = 2 * kind * rows
+                rows_scr[block * per_block + part, first : first + rows] = real[at]
+                rows_scr[block * per_block + part, first + rows : first + 2 * rows] = imag[at]
+    for index in range(half):
+        own_ref[index] = rows_scr[wide ^ (2 * index)]
+        send_ref[index * height : (index + 1) * height] = rows_scr[wide ^ (2 * index + 1)].astype(
+            SHORT
+        )
+    if has_extra:
+        send_ref[half * height :] = extra_ref[...]
+
+
+def expand(here, keep, came, wide_count, extra=None):
+    kinds, _, pieces, size, _ = keep.shape
+    height = kinds * 2 * pieces * size // wide_count
+    half = wide_count // 2
+    more = 0 if extra is None else extra.shape[0]
+    operands = [here, keep, came] + ([] if extra is None else [extra])
+    return call(
+        functools.partial(expand_kernel, extra is not None),
+        [
+            jax.ShapeDtypeStruct((half, height, size), FLOAT),
+            jax.ShapeDtypeStruct((half * height + more, size), SHORT),
+        ],
+        [SMEM_SPEC] + [VMEM_SPEC] * (len(operands) - 1),
+        [
+            pltpu.VMEM((pieces, size, size), FLOAT),
+            pltpu.VMEM((wide_count, height, size), FLOAT),
+        ],
+    )(*operands)
+
+
+def spread_kernel(has_extra, own_ref, came_ref, *refs):
+    refs = list(refs)
+    extra_ref = refs.pop(0) if has_extra else None
+    keep_ref, sends = refs[0], refs[1:]
+    half, height, _ = own_ref.shape
+    keep_ref[...] = own_ref[0] + came_ref[:height].astype(FLOAT)
+    for index in range(1, half):
+        came = came_ref[index * height : (index + 1) * height].astype(FLOAT)
+        sends[index - 1][:height] = (own_ref[index] + came).astype(SHORT)
+        if has_extra:
+            more = extra_ref.shape[0]
+            sends[index - 1][height : height + more] = extra_ref[...]
+            sends[index - 1][height + more :] = came_ref[half * height :]
+
+
+def spread(own, came, extra=None):
+    half, height, size = own.shape
+    more = 0 if extra is None else 2 * extra.shape[0]
+    operands = [own, came] + ([] if extra is None else [extra])
+    return call(
+        functools.partial(spread_kernel, extra is not None),
+        [jax.ShapeDtypeStruct((height, size), FLOAT)]
+        + [jax.ShapeDtypeStruct((height + more, size), SHORT)] * (half - 1),
+        [VMEM_SPEC] * len(operands),
+    )(*operands)
+
+
+def total_kernel(sources, *refs):
+    own_ref, came, rest = refs[0], refs[1 : 1 + sources], refs[1 + sources :]
+    out_ref = rest[-1]
+    height = own_ref.shape[0]
+    total = own_ref[...]
+    for ref in came:
+        total = total + ref[:height].astype(FLOAT)
+    out_ref[:height] = total.astype(SHORT)
+    if len(rest) > 1:
+        out_ref[height:] = rest[0][...]
+
+
+def total(own, came, behind=None):
+    height, size = own.shape
+    more = 0 if behind is None else behind.shape[0]
+    operands = [own, *came] + ([] if behind is None else [behind])
+    return call(
+        functools.partial(total_kernel, len(came)),
+        jax.ShapeDtypeStruct((height + more, size), SHORT),
+        [VMEM_SPEC] * len(operands),
+    )(*operands)
+
+
+def finish_kernel(order, here_ref, list_ref, *refs):
+    pieces = len(order)
+    row_refs = refs[:pieces]
+    pair_ref, last_refs = refs[pieces], refs[pieces + 1 : -5]
+    elem_ref, prod_ref, rows_scr, left_scr, right_scr = refs[-5:]
     narrow, wide = here_ref[0], here_ref[1]
-    pieces, _, _, rows, size = rows_ref.shape
-    slots = list_ref.shape[0]
-    wide_count, _, share, cols = peram_ref.shape
-    total = pieces * size
+    slots, _, rows, total = elem_ref.shape
+    size = row_refs[0].shape[1]
+    share = pair_ref.shape[0] // 2
+    cols = pair_ref.shape[1] // 2
+    height = row_refs[0].shape[0]
     mine = wide * rows // size
+    for position, ref in zip(order, row_refs):
+        rows_scr[position] = ref[...].reshape(slots, 2 * rows, size)
     for slot in range(slots):
         kind = list_ref[slot]
         for block in range(pieces):
-            piece = rows_ref[narrow ^ block ^ mine, kind]
+            piece = rows_scr[narrow ^ block ^ mine, kind]
             at = slice(block * size, (block + 1) * size)
-            elem_ref[slot, :, :, at] = piece.astype(FLOAT)
             for r in range(2):
+                part = piece[r * rows : (r + 1) * rows]
+                elem_ref[slot, r, :, at] = part.astype(FLOAT)
                 left_scr[
                     slot * rows : (slot + 1) * rows,
                     r * total + block * size : r * total + (block + 1) * size,
-                ] = piece[r]
-    for owner in range(wide_count):
-        real = peram_ref[wide ^ owner, 0]
-        imag = peram_ref[wide ^ owner, 1]
-        up = slice(owner * share, (owner + 1) * share)
-        down = slice(total + owner * share, total + (owner + 1) * share)
-        right_scr[0, up, :] = real
-        right_scr[0, down, :] = -imag
-        right_scr[1, up, :] = imag
-        right_scr[1, down, :] = real
-    for r in range(2):
-        product = jnp.dot(left_scr[...], right_scr[r], preferred_element_type=FLOAT)
-        for slot in range(slots):
-            prod_ref[slot, r] = product[slot * rows : (slot + 1) * rows]
-
-
-def finish(here, directions, rows, peram):
-    pieces, _, _, row_count, size = rows.shape
+                ] = part
+    held = [pair_ref[...]]
+    held += [ref[ref.shape[0] - 2 * share :, :] for ref in last_refs]
+    for index, values in enumerate(held):
+        for low in range(2):
+            block = values[low * share : (low + 1) * share]
+            turned = jnp.concatenate([-block[:, cols:], block[:, :cols]], 1)
+            owner = wide ^ (2 * index + low)
+            right_scr[0, owner] = block
+            right_scr[1, owner] = turned
+    right = right_scr[...].reshape(2 * total, 2 * cols)
+    product = jnp.dot(left_scr[...], right, preferred_element_type=FLOAT)
+    for slot in range(slots):
+        for r in range(2):
+            prod_ref[slot, r] = product[
+                slot * rows : (slot + 1) * rows, r * cols : (r + 1) * cols
+            ]
+
+
+def finish(here, directions, order, rows, pair, last):
+    pieces = len(rows)
     slots = directions.shape[0]
-    cols = peram.shape[-1]
+    height, size = rows[0].shape
+    row_count = height // (2 * slots)
+    share, cols = pair.shape[0] // 2, pair.shape[1] // 2
     total = pieces * size
-    return call(
-        finish_kernel,
+    operands = [*rows, pair, *last]
+    return call(
+        functools.partial(finish_kernel, order),
         [
             jax.ShapeDtypeStruct((slots, 2, row_count, total), FLOAT),
             jax.ShapeDtypeStruct((slots, 2, row_count, cols), FLOAT),
         ],
-        [SMEM_SPEC, SMEM_SPEC, VMEM_SPEC, VMEM_SPEC],
+        [SMEM_SPEC, SMEM_SPEC] + [VMEM_SPEC] * len(operands),
         [
+            pltpu.VMEM((pieces, slots, 2 * row_count, size), SHORT),
             pltpu.VMEM((slots * row_count, 2 * total), SHORT),
-            pltpu.VMEM((2, 2 * total, cols), SHORT),
+            pltpu.VMEM((2, total // share, share, 2 * cols), SHORT),
         ],
-    )(here, directions, rows, peram)
-
-
-def gather(x, axis, masks):
-    stack = x[None]
-    for mask in masks:
-        stack = jnp.concatenate([stack, swap(stack, axis, mask)], 0)
-    return stack
+    )(here, directions, *operands)
 
 
 def on_device(vectors, links, directions, peram):
@@ -332,6 +438,7 @@
     norm = 1.0 / math.sqrt(12.0 * planes * wide_count * length * narrow_count)
     here = jnp.stack([lax.axis_index("narrow"), lax.axis_index("wide")]).astype(jnp.int32)
     link_rows = links.reshape(-1, length)
+    pair = jnp.concatenate([peram[0], peram[1]], 1)
 
     vec, first, edge = split_vectors(vectors)
     plane_halo = from_behind(first, "wide", -1)
@@ -340,33 +447,39 @@
     part = functools.partial(
         direction_part, norm=norm, pieces=narrow_count, here=here, links=link_rows, vec=vec
     )
+
+    def over_narrow(parts, tie=None):
+        keep, send = halve(*[(k[None], swap(s, "narrow", 1)[None]) for k, s in parts])
+        if tie is not None:
+            keep, send, tie = lax.optimization_barrier((keep, send, tie))
+        for stage in range(1, narrow_count.bit_length() - 1):
+            came = swap(send, "narrow", 1 << stage)
+            if keep.shape[1] > 1:
+                keep, send = halve((keep, came))
+        return keep, came, tie
+
+    def over_wide(own, send, extra=None):
+        came = swap(send, "wide", 1)
+        own, *sends = spread(own, came, extra)
+        return own, came, [swap(x, "wide", 2 * (i + 1)) for i, x in enumerate(sends)]
+
     third = part(2, every)
     second = part(1, every, halo=edge_halo)
     inner = part(0, every[:-1], more="first")
+    keep, came, plane_halo = over_narrow([second, third], plane_halo)
+    own, near, far = over_wide(*expand(here, keep, came, wide_count, pair), pair)
+    early = total(own, far)
+    pairs = jnp.concatenate([pair, near[near.shape[0] - pair.shape[0] :]], 0)
+
     whole = part(0, every[-1:], halo=plane_halo, more=inner)
-
-    parts = [whole, second, third]
-    keep = jnp.stack([k for k, _ in parts])
-    send = jnp.stack([s for _, s in parts])
-    came = swap(send, "narrow", 1)
-    for stage in range(1, narrow_count.bit_length() - 1):
-        total = keep + came.astype(FLOAT)
-        keep = total[:, 0::2]
-        came = swap(total[:, 1::2].astype(SHORT), "narrow", 1 << stage)
-    own, *sends = expand(here, keep[:, 0], came[:, 0], wide_count)
-    for index, piece in enumerate(sends):
-        own = own + swap(piece, "wide", index + 1).astype(FLOAT)
-    masks = [1 << stage for stage in range(narrow_count.bit_length() - 1)]
-    low = own.astype(SHORT)
-    stack = low[None]
-    for mask in reversed(masks):
-        stack = jnp.concatenate([stack, swap(stack, "narrow", mask)], 0)
+    keep, came, _ = over_narrow([whole])
+    own, _, late = over_wide(*expand(here, keep, came, wide_count))
+    rows = [total(own, late, early)]
     order = [0]
-    for mask in reversed(masks):
-        order = order + [o ^ mask for o in order]
-    rows = jnp.stack([stack[order.index(j)] for j in range(narrow_count)])
-    peram_all = gather(peram, "wide", [1 << s for s in range(wide_count.bit_length() - 1)])
-    return tuple(finish(here, directions, rows, peram_all))
+    for stage in reversed(range(narrow_count.bit_length() - 1)):
+        rows = rows + [swap(x, "narrow", 1 << stage) for x in rows]
+        order = order + [o ^ (1 << stage) for o in order]
+    return tuple(finish(here, directions, order, rows, pairs, far))
 
 
 def solution(mesh):

time: 85.4 us -> 68 us (0.80)
  waiting for transfers between devices: 34.3 us -> 18.2 us
  Pallas kernels: 28 us -> 22.5 us
  starting transfers between devices: 19.9 us -> 24.6 us
    ppermute x14 -> x16, waiting for transfers between devices: 34.3 us -> 15.2 us  [swap(): return lax.ppermute(x, axis, [(i, i ^ mask) for i in range(length)])]
    pallas_call x4, Pallas kernels: 23.9 us -> 14.7 us  [direction_part(): call(functools.partial(direction_kernel, direction, chosen, planes, norm,...]
    ppermute x14 -> x16, starting transfers between devices: 13.1 us -> 17.9 us  [swap(): return lax.ppermute(x, axis, [(i, i ^ mask) for i in range(length)])]
    pallas_call x3 -> x10, Pallas kernels: 4.09 us -> 7.73 us  [the longest x1 4.09 us: split_vectors(): call(functools.partial(split_kernel, planes), [jax.ShapeDtypeStruct((coun...]
    ppermute x2, waiting for transfers between devices: 0.01 us -> 3.09 us  [from_behind(): lax.ppermute(x, axis, [(i, (i + by) % length) for i in range(length)])]
  transfers between devices with their start and end apart: 16 -> 18, of which waited for: 9 -> 8; matrix products, arithmetic and copies ran while one was open for 0% -> 0% of each run, Pallas kernels for 25% -> 24%
where the time goes in v2:
time: 68 us; the launch traced here: 67.8 us
  starting transfers between devices  24.6 us (36%)
  Pallas kernels  22.5 us (33%)
  waiting for transfers between devices  18.2 us (27%)
  local copies, waits for them, and re-layouts  1.46 us (2%)
  between operations  0.81 us (1%)
    ppermute x16, starting transfers between devices, swap(): return lax.ppermute(x, axis, [(i, i ^ mask) for i in range(length)])  17.9 us
    ppermute x16, waiting for transfers between devices, swap(): return lax.ppermute(x, axis, [(i, i ^ mask) for i in range(length)])  15.2 us
    pallas_call x4, Pallas kernels, direction_part(): call(functools.partial(direction_kernel, direction, chosen, planes, norm,...  14.7 us
    ppermute x2, starting transfers between devices, from_behind(): lax.ppermute(x, axis, [(i, (i + by) % length) for i in range(length)])  6.71 us
    pallas_call x1, Pallas kernels, split_vectors(): call(functools.partial(split_kernel, planes), [jax.ShapeDtypeStruct((coun...  4.09 us
    ppermute x2, waiting for transfers between devices, from_behind(): lax.ppermute(x, axis, [(i, (i + by) % length) for i in range(length)])  3.09 us
    pallas_call x1, Pallas kernels, finish(): call(functools.partial(finish_kernel, order), [jax.ShapeDtypeStruct((slot...  1.75 us
    pallas_call x2, Pallas kernels, expand(): call(functools.partial(expand_kernel, extra is not None), [jax.ShapeDtype...  1.59 us
  transfers between devices with their start and end apart: 18, of which 8 were waited for; matrix products, arithmetic and copies ran while one was open for 0% of the time, Pallas kernels for 24%

profile of v2, /device:TPU:0, one launch (start us, length us, event | category | flops | bytes accessed | tf_op | source)
XLA Modules:
  0.0 67.8 jit_solution(3638272332906117708)
XLA Ops:
  0.6 1.4 %copy-done = bf16[512,2,3,2,128]{4,3,2,1,0:T(2,128)(2,1)S(1)} copy-done((bf16[512,2,3,2,128]{4,3,2,1,0:T(2,128)(2,1)S(1)}, bf16[512,2,3,2,128]{4,3,2,1,0:T(2,128)(2,1)}, u32[]{:S(2)}) %copy-start) | copy-done | bytes 1572888
  2.0 4.1 %shard_map.59 = (bf16[512,1536]{1,0:T(8,128)(2,1)S(1)}, bf16[512,768]{1,0:T(8,128)(2,1)S(1)}, bf16[512,256]{1,0:T(8,128)(2,1)}) custom-call(bf16[6144,128]{1,0:T(8,128)(2,1)S(1)} %bitcast.13), custom_call_target="tpu_custom_call" | custom-call | tf_op jit(solution)/shard_map/pallas_call | solution.py:81
  6.1 6.1 %collective-permute-start.3 = (bf16[512,768]{1,0:T(8,128)(2,1)S(1)}, bf16[512,768]{1,0:T(8,128)(2,1)S(1)}, u32[]{:S(2)}, u32[]{:S(2)}) collective-permute-start(bf16[512,768]{1,0:T(8,128)(2,1)S(1)} %get-tuple-element.38), channel_id=1, source_target_pairs={{0,28},{4,0},{8,4},{12,8},{16,12},{20,16},{24,20},{28,24},{1,29},{... | collective-permute-start | bytes 2359304 | tf_op jit(solution)/shard_map/ppermute | solution.py:35
  12.2 0.7 collective-permute-start
  13.0 4.8 %shard_map.61 = (f32[2,4,128,128]{3,2,1,0:T(8,128)S(1)}, bf16[2,4,128,128]{3,2,1,0:T(8,128)(2,1)S(1)}) custom-call(s32[2]{0:T(128)S(1)} %pad_add_fusion.refs_0_.here_ref, f32[108,128]{1,0:T(8,128)S(1)} %reshape.10.refs_1_, bf16[512,1536]{1,0:T(8,128)(2,1)S(1)} %get-tuple-element.30.refs_2_), custom_call_target="tpu_custom_call" | custom-call | flops 1 | bytes 1 | tf_op jit(solution)/shard_map/pallas_call | solution.py:227
  17.9 4.8 %shard_map.60 = (f32[2,4,128,128]{3,2,1,0:T(8,128)S(1)}, bf16[2,4,128,128]{3,2,1,0:T(8,128)(2,1)S(1)}) custom-call(s32[2]{0:T(128)S(1)} %pad_add_fusion.refs_0_.here_ref, f32[108,128]{1,0:T(8,128)S(1)} %reshape.10.refs_1_, bf16[512,1536]{1,0:T(8,128)(2,1)S(1)} %get-tuple-element.30.refs_2_, bf16[512,256]{1,0:T(8,128)(2,1)S(1)} %collective-permute-done.refs_3_), custom_call_target="tpu_custom_call" | custom-call | flops 1 | bytes 1 | tf_op jit(solution)/shard_map/pallas_call | solution.py:227
  22.7 0.6 collective-permute-start.1
  23.3 2.5 %shard_map.63.refs_4_ = f32[4,4,128,128]{3,2,1,0:T(8,128)S(1)} custom-call(s32[2]{0:T(128)S(1)} %pad_add_fusion.refs_0_.here_ref, f32[108,128]{1,0:T(8,128)S(1)} %reshape.10.refs_1_, bf16[512,1536]{1,0:T(8,128)(2,1)S(1)} %get-tuple-element.30.refs_2_), custom_call_target="tpu_custom_call" | custom-call | flops 1 | bytes 1 | tf_op jit(solution)/shard_map/pallas_call | solution.py:227
  25.8 0.1 shard_map.62
  25.9 3.1 %collective-permute-done.3.refs_3_ = bf16[512,768]{1,0:T(8,128)(2,1)S(1)} collective-permute-done((bf16[512,768]{1,0:T(8,128)(2,1)S(1)}, bf16[512,768]{1,0:T(8,128)(2,1)S(1)}, u32[]{:S(2)}, u32[]{:S(2)}) %collective-permute-start.3) | collective-permute-done | bytes 786464 | tf_op jit(solution)/shard_map/ppermute | solution.py:35
  29.0 1.5 %collective-permute-start.10 = (bf16[2,1,4,128,128]{4,3,2,1,0:T(8,128)(2,1)S(1)}, bf16[2,1,4,128,128]{4,3,2,1,0:T(8,128)(2,1)S(1)}, u32[]{:S(2)}, u32[]{:S(2)}) collective-permute-start(bf16[2,1,4,128,128]{4,3,2,1,0:T(8,128)(2,1)S(1)} %get-tuple-element.51), channel_id=1, source_target_pairs={{0,2},{1,3},{2,0},{3,1},{4,6},{5,7},{6,4},{7,5},{8,10},{9,11},{10,... | collective-permute-start | bytes 786440 | tf_op jit(solution)/shard_map/ppermute | solution.py:40
  30.5 2.6 %shard_map.64 = (f32[2,4,128,128]{3,2,1,0:T(8,128)S(1)}, bf16[2,4,128,128]{3,2,1,0:T(8,128)(2,1)S(1)}) custom-call(s32[2]{0:T(128)S(1)} %pad_add_fusion.refs_0_.here_ref, f32[108,128]{1,0:T(8,128)S(1)} %reshape.10.refs_1_, bf16[512,1536]{1,0:T(8,128)(2,1)S(1)} %get-tuple-element.30.refs_2_, bf16[512,768]{1,0:T(8,128)(2,1)S(1)} %collective-permute-done.3.refs_3_, ...), custom_call_target="tpu_custom_call" | custom-call | flops 1 | bytes 1 | tf_op jit(solution)/shard_map/pallas_call | solution.py:227
  33.2 0.1 pad_maximum_fusion.1.refs_0_
  33.3 2.9 %collective-permute-done.10.came_ref = bf16[2,1,4,128,128]{4,3,2,1,0:T(8,128)(2,1)S(1)} collective-permute-done((bf16[2,1,4,128,128]{4,3,2,1,0:T(8,128)(2,1)S(1)}, bf16[2,1,4,128,128]{4,3,2,1,0:T(8,128)(2,1)S(1)}, u32[]{:S(2)}, u32[]{:S(2)}) %collective-permute-start.10) | collective-permute-done | bytes 262176 | tf_op jit(solution)/shard_map/ppermute | solution.py:40
  36.2 0.9 %shard_map.68 = (f32[4,256,128]{2,1,0:T(8,128)S(1)}, bf16[1088,128]{1,0:T(8,128)(2,1)S(1)}) custom-call(s32[2]{0:T(128)S(1)} %pad_add_fusion.refs_0_.here_ref, f32[2,1,4,128,128]{4,3,2,1,0:T(8,128)S(1)} %get-tuple-element.50.keep_ref, bf16[2,1,4,128,128]{4,3,2,1,0:T(8,128)(2,1)S(1)} %collective-permute-done.10.came_ref, ...), custom_call_target="tpu_custom_call" | custom-call | tf_op jit(solution)/shard_map/pallas_call | solution.py:302
  37.0 0.4 collective-permute-start.11
  37.5 1.6 %collective-permute-start.5 = (bf16[1,1,4,128,128]{4,3,2,1,0:T(8,128)(2,1)S(1)}, bf16[1,1,4,128,128]{4,3,2,1,0:T(8,128)(2,1)S(1)}, u32[]{:S(2)}, u32[]{:S(2)}) collective-permute-start(bf16[1,1,4,128,128]{4,3,2,1,0:T(8,128)(2,1)S(1)} %get-tuple-element.43), channel_id=1, source_target_pairs={{0,2},{1,3},{2,0},{3,1},{4,6},{5,7},{6,4},{7,5},{8,10},{9,11},{10,... | collective-permute-start | bytes 393224 | tf_op jit(solution)/shard_map/ppermute | solution.py:40
  39.1 3.5 %collective-permute-done.5.came_ref = bf16[1,1,4,128,128]{4,3,2,1,0:T(8,128)(2,1)S(1)} collective-permute-done((bf16[1,1,4,128,128]{4,3,2,1,0:T(8,128)(2,1)S(1)}, bf16[1,1,4,128,128]{4,3,2,1,0:T(8,128)(2,1)S(1)}, u32[]{:S(2)}, u32[]{:S(2)}) %collective-permute-start.5) | collective-permute-done | bytes 131104 | tf_op jit(solution)/shard_map/ppermute | solution.py:40
  42.5 0.7 %shard_map.66 = (f32[4,128,128]{2,1,0:T(8,128)S(1)}, bf16[512,128]{1,0:T(8,128)(2,1)S(1)}) custom-call(s32[2]{0:T(128)S(1)} %pad_add_fusion.refs_0_.here_ref, f32[1,1,4,128,128]{4,3,2,1,0:T(8,128)S(1)} %get-tuple-element.42.keep_ref, bf16[1,1,4,128,128]{4,3,2,1,0:T(8,128)(2,1)S(1)} %collective-permute-done.5.came_ref), custom_call_target="tpu_custom_call" | custom-call | tf_op jit(solution)/shard_map/pallas_call | solution.py:302
  43.3 1.8 %collective-permute-start.6 = (bf16[512,128]{1,0:T(8,128)(2,1)S(1)}, bf16[512,128]{1,0:T(8,128)(2,1)S(1)}, u32[]{:S(2)}, u32[]{:S(2)}) collective-permute-start(bf16[512,128]{1,0:T(8,128)(2,1)S(1)} %get-tuple-element.45), channel_id=1, source_target_pairs={{0,4},{4,0},{8,12},{12,8},{16,20},{20,16},{24,28},{28,24},{1,5},{5... | collective-permute-start | bytes 393224 | tf_op jit(solution)/shard_map/ppermute | solution.py:40
  45.2 4.3 %collective-permute-start.13 = (bf16[384,128]{1,0:T(8,128)(2,1)S(1)}, bf16[384,128]{1,0:T(8,128)(2,1)S(1)}, u32[]{:S(2)}, u32[]{:S(2)}) collective-permute-start(bf16[384,128]{1,0:T(8,128)(2,1)S(1)} %get-tuple-element.56), channel_id=1, source_target_pairs={{0,16},{4,20},{8,24},{12,28},{16,0},{20,4},{24,8},{28,12},{1,17},{... | collective-permute-start | bytes 294920 | tf_op jit(solution)/shard_map/ppermute | solution.py:40
  49.6 0.6 collective-permute-start.7
  50.2 4.2 %collective-permute-start.8 = (bf16[128,128]{1,0:T(8,128)(2,1)S(1)}, bf16[128,128]{1,0:T(8,128)(2,1)S(1)}, u32[]{:S(2)}, u32[]{:S(2)}) collective-permute-start(bf16[128,128]{1,0:T(8,128)(2,1)S(1)} %get-tuple-element.48), channel_id=1, source_target_pairs={{0,16},{4,20},{8,24},{12,28},{16,0},{20,4},{24,8},{28,12},{1,17},{... | collective-permute-start | bytes 98312 | tf_op jit(solution)/shard_map/ppermute | solution.py:40
  54.4 1.2 %collective-permute-start.9 = (bf16[128,128]{1,0:T(8,128)(2,1)S(1)}, bf16[128,128]{1,0:T(8,128)(2,1)S(1)}, u32[]{:S(2)}, u32[]{:S(2)}) collective-permute-start(bf16[128,128]{1,0:T(8,128)(2,1)S(1)} %get-tuple-element.49), channel_id=1, source_target_pairs={{0,24},{4,28},{8,16},{12,20},{16,8},{20,12},{24,0},{28,4},{1,25},{... | collective-permute-start | bytes 98312 | tf_op jit(solution)/shard_map/ppermute | solution.py:40
  55.6 0.3 collective-permute-done.13.refs_2_.refs_6_
  56.0 1.7 %collective-permute-done.8.refs_2_ = bf16[128,128]{1,0:T(8,128)(2,1)S(1)} collective-permute-done((bf16[128,128]{1,0:T(8,128)(2,1)S(1)}, bf16[128,128]{1,0:T(8,128)(2,1)S(1)}, u32[]{:S(2)}, u32[]{:S(2)}) %collective-permute-start.8) | collective-permute-done | bytes 32800 | tf_op jit(solution)/shard_map/ppermute | solution.py:40
  57.7 2.4 %collective-permute-done.9.refs_3_ = bf16[128,128]{1,0:T(8,128)(2,1)S(1)} collective-permute-done((bf16[128,128]{1,0:T(8,128)(2,1)S(1)}, bf16[128,128]{1,0:T(8,128)(2,1)S(1)}, u32[]{:S(2)}, u32[]{:S(2)}) %collective-permute-start.9) | collective-permute-done | bytes 32800 | tf_op jit(solution)/shard_map/ppermute | solution.py:40
  60.1 1.6 %collective-permute-start.15 = (bf16[384,128]{1,0:T(8,128)(2,1)S(1)}, bf16[384,128]{1,0:T(8,128)(2,1)S(1)}, u32[]{:S(2)}, u32[]{:S(2)}) collective-permute-start(bf16[384,128]{1,0:T(8,128)(2,1)S(1)} %shard_map.71.refs_0_), channel_id=1, source_target_pairs={{0,2},{1,3},{2,0},{3,1},{4,6},{5,7},{6,4},{7,5},{8,10},{9,11},{10,... | collective-permute-start | bytes 294920 | tf_op jit(solution)/shard_map/ppermute | solution.py:40
  61.7 3.1 %collective-permute-done.15.refs_1_ = bf16[384,128]{1,0:T(8,128)(2,1)S(1)} collective-permute-done((bf16[384,128]{1,0:T(8,128)(2,1)S(1)}, bf16[384,128]{1,0:T(8,128)(2,1)S(1)}, u32[]{:S(2)}, u32[]{:S(2)}) %collective-permute-start.15) | collective-permute-done | bytes 98336 | tf_op jit(solution)/shard_map/ppermute | solution.py:40
  64.8 0.1 pad_maximum_fusion.refs_4_
  64.9 1.2 %collective-permute-done.17.refs_3_ = bf16[384,128]{1,0:T(8,128)(2,1)S(1)} collective-permute-done((bf16[384,128]{1,0:T(8,128)(2,1)S(1)}, bf16[384,128]{1,0:T(8,128)(2,1)S(1)}, u32[]{:S(2)}, u32[]{:S(2)}) %collective-permute-start.17) | collective-permute-done | bytes 98336 | tf_op jit(solution)/shard_map/ppermute | solution.py:40
  66.1 1.8 %shard_map.72 = (f32[3,2,64,512]{3,2,1,0:T(8,128)}, f32[3,2,64,64]{3,2,1,0:T(8,128)}) custom-call(s32[2]{0:T(128)S(1)} %pad_add_fusion.refs_0_.here_ref, s32[3]{0:T(128)S(1)} %copy-done.1, bf16[384,128]{1,0:T(8,128)(2,1)S(1)} %shard_map.71.refs_0_, bf16[384,128]{1,0:T(8,128)(2,1)S(1)} %collective-permute-done.15.refs_1_, ...), custom_call_target="tpu_custom_call" | custom-call | tf_op jit(solution)/shard_map/pallas_call | solution.py:418
  (32 shorter events, 0.6 us)
Async XLA Ops:
  0.6 1.4 %copy-start = (bf16[512,2,3,2,128]{4,3,2,1,0:T(2,128)(2,1)S(1)}, bf16[512,2,3,2,128]{4,3,2,1,0:T(2,128)(2,1)}, u32[]{:S(2)}) copy-start(bf16[512,2,3,2,128]{4,3,2,1,0:T(2,128)(2,1)} %param.4) | copy-start | bytes 4718596
  2.0 10.8 %copy-start.2 = (f32[3,2,3,3,2,128]{5,4,3,2,1,0:T(2,128)S(1)}, f32[3,2,3,3,2,128]{5,4,3,2,1,0:T(2,128)}, u32[]{:S(2)}) copy-start(f32[3,2,3,3,2,128]{5,4,3,2,1,0:T(2,128)} %param.5) | copy-start | bytes 165892
  6.1 22.9 %collective-permute-start.3 = (bf16[512,768]{1,0:T(8,128)(2,1)S(1)}, bf16[512,768]{1,0:T(8,128)(2,1)S(1)}, u32[]{:S(2)}, u32[]{:S(2)}) collective-permute-start(bf16[512,768]{1,0:T(8,128)(2,1)S(1)} %get-tuple-element.38), channel_id=1, source_target_pairs={{0,28},{4,0},{8,4},{12,8},{16,12},{20,16},{24,20},{28,24},{1,29},{... | collective-permute-start | bytes 2359304 | tf_op jit(solution)/shard_map/ppermute | solution.py:35
  12.2 5.7 %collective-permute-start = (bf16[512,256]{1,0:T(8,128)(2,1)}, bf16[512,256]{1,0:T(8,128)(2,1)S(1)}, u32[]{:S(2)}, u32[]{:S(2)}) collective-permute-start(bf16[512,256]{1,0:T(8,128)(2,1)} %get-tuple-element.31), channel_id=1, source_target_pairs={{0,3},{1,0},{2,1},{3,2},{4,7},{5,4},{6,5},{7,6},{8,11},{9,8},{10,9... | collective-permute-start | bytes 786440 | tf_op jit(solution)/shard_map/ppermute | solution.py:35
  17.8 8.0 %collective-permute-start.2 = (bf16[2,4,128,128]{3,2,1,0:T(8,128)(2,1)S(1)}, bf16[2,4,128,128]{3,2,1,0:T(8,128)(2,1)S(1)}, u32[]{:S(2)}, u32[]{:S(2)}) collective-permute-start(bf16[2,4,128,128]{3,2,1,0:T(8,128)(2,1)S(1)} %get-tuple-element.35), channel_id=1, source_target_pairs={{0,1},{1,0},{2,3},{3,2},{4,5},{5,4},{6,7},{7,6},{8,9},{9,8},{10,11... | collective-permute-start | bytes 786440 | tf_op jit(solution)/shard_map/ppermute | solution.py:40
  22.7 3.1 %collective-permute-start.1 = (bf16[2,4,128,128]{3,2,1,0:T(8,128)(2,1)S(1)}, bf16[2,4,128,128]{3,2,1,0:T(8,128)(2,1)S(1)}, u32[]{:S(2)}, u32[]{:S(2)}) collective-permute-start(bf16[2,4,128,128]{3,2,1,0:T(8,128)(2,1)S(1)} %get-tuple-element.33), channel_id=1, source_target_pairs={{0,1},{1,0},{2,3},{3,2},{4,5},{5,4},{6,7},{7,6},{8,9},{9,8},{10,11... | collective-permute-start | bytes 786440 | tf_op jit(solution)/shard_map/ppermute | solution.py:40
  29.0 4.2 %copy-start.3 = (bf16[2,64,64]{2,1,0:T(8,128)(2,1)S(1)}, bf16[2,64,64]{2,1,0:T(8,128)(2,1)}, u32[]{:S(2)}) copy-start(bf16[2,64,64]{2,1,0:T(8,128)(2,1)} %param.7) | copy-start | bytes 49156
  29.0 7.2 %collective-permute-start.10 = (bf16[2,1,4,128,128]{4,3,2,1,0:T(8,128)(2,1)S(1)}, bf16[2,1,4,128,128]{4,3,2,1,0:T(8,128)(2,1)S(1)}, u32[]{:S(2)}, u32[]{:S(2)}) collective-permute-start(bf16[2,1,4,128,128]{4,3,2,1,0:T(8,128)(2,1)S(1)} %get-tuple-element.51), channel_id=1, source_target_pairs={{0,2},{1,3},{2,0},{3,1},{4,6},{5,7},{6,4},{7,5},{8,10},{9,11},{10,... | collective-permute-start | bytes 786440 | tf_op jit(solution)/shard_map/ppermute | solution.py:40
  33.1 4.4 %collective-permute-start.4 = (bf16[2,4,128,128]{3,2,1,0:T(8,128)(2,1)S(1)}, bf16[2,4,128,128]{3,2,1,0:T(8,128)(2,1)S(1)}, u32[]{:S(2)}, u32[]{:S(2)}) collective-permute-start(bf16[2,4,128,128]{3,2,1,0:T(8,128)(2,1)S(1)} %get-tuple-element.41), channel_id=1, source_target_pairs={{0,1},{1,0},{2,3},{3,2},{4,5},{5,4},{6,7},{7,6},{8,9},{9,8},{10,11... | collective-permute-start | bytes 786440 | tf_op jit(solution)/shard_map/ppermute | solution.py:40
  37.0 8.0 %collective-permute-start.11 = (bf16[1088,128]{1,0:T(8,128)(2,1)S(1)}, bf16[1088,128]{1,0:T(8,128)(2,1)S(1)}, u32[]{:S(2)}, u32[]{:S(2)}) collective-permute-start(bf16[1088,128]{1,0:T(8,128)(2,1)S(1)} %get-tuple-element.53), channel_id=1, source_target_pairs={{0,4},{4,0},{8,12},{12,8},{16,20},{20,16},{24,28},{28,24},{1,5},{5... | collective-permute-start | bytes 835592 | tf_op jit(solution)/shard_map/ppermute | solution.py:40
  37.4 28.6 %copy-start.1 = (s32[3]{0:T(128)S(1)}, s32[3]{0:T(128)}, u32[]{:S(2)}) copy-start(s32[3]{0:T(128)} %list_ref.1) | copy-start | bytes 40
  37.5 5.0 %collective-permute-start.5 = (bf16[1,1,4,128,128]{4,3,2,1,0:T(8,128)(2,1)S(1)}, bf16[1,1,4,128,128]{4,3,2,1,0:T(8,128)(2,1)S(1)}, u32[]{:S(2)}, u32[]{:S(2)}) collective-permute-start(bf16[1,1,4,128,128]{4,3,2,1,0:T(8,128)(2,1)S(1)} %get-tuple-element.43), channel_id=1, source_target_pairs={{0,2},{1,3},{2,0},{3,1},{4,6},{5,7},{6,4},{7,5},{8,10},{9,11},{10,... | collective-permute-start | bytes 393224 | tf_op jit(solution)/shard_map/ppermute | solution.py:40
  43.3 6.3 %collective-permute-start.6 = (bf16[512,128]{1,0:T(8,128)(2,1)S(1)}, bf16[512,128]{1,0:T(8,128)(2,1)S(1)}, u32[]{:S(2)}, u32[]{:S(2)}) collective-permute-start(bf16[512,128]{1,0:T(8,128)(2,1)S(1)} %get-tuple-element.45), channel_id=1, source_target_pairs={{0,4},{4,0},{8,12},{12,8},{16,20},{20,16},{24,28},{28,24},{1,5},{5... | collective-permute-start | bytes 393224 | tf_op jit(solution)/shard_map/ppermute | solution.py:40
  45.1 9.3 %collective-permute-start.12 = (bf16[384,128]{1,0:T(8,128)(2,1)S(1)}, bf16[384,128]{1,0:T(8,128)(2,1)S(1)}, u32[]{:S(2)}, u32[]{:S(2)}) collective-permute-start(bf16[384,128]{1,0:T(8,128)(2,1)S(1)} %get-tuple-element.55), channel_id=1, source_target_pairs={{0,8},{4,12},{8,0},{12,4},{16,24},{20,28},{24,16},{28,20},{1,9},{5... | collective-permute-start | bytes 294920 | tf_op jit(solution)/shard_map/ppermute | solution.py:40
  45.2 10.8 %collective-permute-start.13 = (bf16[384,128]{1,0:T(8,128)(2,1)S(1)}, bf16[384,128]{1,0:T(8,128)(2,1)S(1)}, u32[]{:S(2)}, u32[]{:S(2)}) collective-permute-start(bf16[384,128]{1,0:T(8,128)(2,1)S(1)} %get-tuple-element.56), channel_id=1, source_target_pairs={{0,16},{4,20},{8,24},{12,28},{16,0},{20,4},{24,8},{28,12},{1,17},{... | collective-permute-start | bytes 294920 | tf_op jit(solution)/shard_map/ppermute | solution.py:40
  49.5 6.4 %collective-permute-start.14 = (bf16[384,128]{1,0:T(8,128)(2,1)S(1)}, bf16[384,128]{1,0:T(8,128)(2,1)S(1)}, u32[]{:S(2)}, u32[]{:S(2)}) collective-permute-start(bf16[384,128]{1,0:T(8,128)(2,1)S(1)} %get-tuple-element.57), channel_id=1, source_target_pairs={{0,24},{4,28},{8,16},{12,20},{16,8},{20,12},{24,0},{28,4},{1,25},{... | collective-permute-start | bytes 294920 | tf_op jit(solution)/shard_map/ppermute | solution.py:40
  49.6 6.4 %collective-permute-start.7 = (bf16[128,128]{1,0:T(8,128)(2,1)S(1)}, bf16[128,128]{1,0:T(8,128)(2,1)S(1)}, u32[]{:S(2)}, u32[]{:S(2)}) collective-permute-start(bf16[128,128]{1,0:T(8,128)(2,1)S(1)} %get-tuple-element.47), channel_id=1, source_target_pairs={{0,8},{4,12},{8,0},{12,4},{16,24},{20,28},{24,16},{28,20},{1,9},{5... | collective-permute-start | bytes 98312 | tf_op jit(solution)/shard_map/ppermute | solution.py:40
  50.2 7.5 %collective-permute-start.8 = (bf16[128,128]{1,0:T(8,128)(2,1)S(1)}, bf16[128,128]{1,0:T(8,128)(2,1)S(1)}, u32[]{:S(2)}, u32[]{:S(2)}) collective-permute-start(bf16[128,128]{1,0:T(8,128)(2,1)S(1)} %get-tuple-element.48), channel_id=1, source_target_pairs={{0,16},{4,20},{8,24},{12,28},{16,0},{20,4},{24,8},{28,12},{1,17},{... | collective-permute-start | bytes 98312 | tf_op jit(solution)/shard_map/ppermute | solution.py:40
  54.4 5.7 %collective-permute-start.9 = (bf16[128,128]{1,0:T(8,128)(2,1)S(1)}, bf16[128,128]{1,0:T(8,128)(2,1)S(1)}, u32[]{:S(2)}, u32[]{:S(2)}) collective-permute-start(bf16[128,128]{1,0:T(8,128)(2,1)S(1)} %get-tuple-element.49), channel_id=1, source_target_pairs={{0,24},{4,28},{8,16},{12,20},{16,8},{20,12},{24,0},{28,4},{1,25},{... | collective-permute-start | bytes 98312 | tf_op jit(solution)/shard_map/ppermute | solution.py:40
  60.1 4.7 %collective-permute-start.15 = (bf16[384,128]{1,0:T(8,128)(2,1)S(1)}, bf16[384,128]{1,0:T(8,128)(2,1)S(1)}, u32[]{:S(2)}, u32[]{:S(2)}) collective-permute-start(bf16[384,128]{1,0:T(8,128)(2,1)S(1)} %shard_map.71.refs_0_), channel_id=1, source_target_pairs={{0,2},{1,3},{2,0},{3,1},{4,6},{5,7},{6,4},{7,5},{8,10},{9,11},{10,... | collective-permute-start | bytes 294920 | tf_op jit(solution)/shard_map/ppermute | solution.py:40
  61.7 3.2 %collective-permute-start.16 = (bf16[384,128]{1,0:T(8,128)(2,1)S(1)}, bf16[384,128]{1,0:T(8,128)(2,1)S(1)}, u32[]{:S(2)}, u32[]{:S(2)}) collective-permute-start(bf16[384,128]{1,0:T(8,128)(2,1)S(1)} %shard_map.71.refs_0_), channel_id=1, source_target_pairs={{0,1},{1,0},{2,3},{3,2},{4,5},{5,4},{6,7},{7,6},{8,9},{9,8},{10,11... | collective-permute-start | bytes 294920 | tf_op jit(solution)/shard_map/ppermute | solution.py:40
  64.8 1.3 %collective-permute-start.17 = (bf16[384,128]{1,0:T(8,128)(2,1)S(1)}, bf16[384,128]{1,0:T(8,128)(2,1)S(1)}, u32[]{:S(2)}, u32[]{:S(2)}) collective-permute-start(bf16[384,128]{1,0:T(8,128)(2,1)S(1)} %collective-permute-done.15.refs_1_), channel_id=1, source_target_pairs={{0,1},{1,0},{2,3},{3,2},{4,5},{5,4},{6,7},{7,6},{8,9},{9,8},{10,11... | collective-permute-start | bytes 294920 | tf_op jit(solution)/shard_map/ppermute | solution.py:40

commit v3 on v2

--- a/solution.py
+++ b/solution.py
@@ -18,7 +18,7 @@
 SMEM_SPEC = pl.BlockSpec(memory_space=pltpu.SMEM)
 
 
-def call(kernel, out_shape, in_specs, scratch=(), flops=0, size=0):
+def call(kernel, out_shape, in_specs, scratch=()):
     return pl.pallas_call(
         kernel,
         out_shape=out_shape,
@@ -26,7 +26,7 @@
         out_specs=jax.tree.map(lambda _: VMEM_SPEC, out_shape),
         scratch_shapes=list(scratch),
         compiler_params=pltpu.CompilerParams(vmem_limit_bytes=VMEM_BYTES),
-        cost_estimate=pl.CostEstimate(flops=flops, bytes_accessed=size, transcendentals=0),
+        cost_estimate=pl.CostEstimate(flops=1, bytes_accessed=1, transcendentals=0),
     )
 
 
@@ -40,54 +40,58 @@
     return lax.ppermute(x, axis, [(i, i ^ mask) for i in range(length)])
 
 
-def split_kernel(planes, x_ref, all_ref, first_ref, edge_ref, held, wide_scr, sems):
-    blocks = sems.shape[0]
-    count = all_ref.shape[0] // blocks
-    rows = count * COMP * planes
+def front_kernel(planes, x_ref, first_ref, wide_scr):
+    count = first_ref.shape[0]
+    length = x_ref.shape[1]
+    wide_scr[...] = x_ref[...].astype(FLOAT)
+    for comp in range(COMP):
+        values = wide_scr[pl.ds(comp * planes, count, stride=COMP * planes), :]
+        first_ref[:, comp * length : (comp + 1) * length] = values.astype(SHORT)
+
+
+def split_kernel(planes, x_ref, all_ref, edge_ref, wide_scr):
+    count = all_ref.shape[0]
     length = x_ref.shape[1]
     per_tile = length // LZ
+    wide_scr[...] = x_ref[...].astype(FLOAT)
     lane = lax.broadcasted_iota(jnp.int32, (count, length), 1)
-    copies = []
-    for block in range(blocks):
-        at = pl.ds(block * rows, rows)
-        copies.append(pltpu.make_async_copy(x_ref.at[at], held.at[at], sems.at[block]))
-        copies[-1].start()
-    for block in range(blocks):
-        copies[block].wait()
-        here = slice(block * count, (block + 1) * count)
-        wide_scr[...] = held[block * rows : (block + 1) * rows].astype(FLOAT)
-        tiles = [jnp.zeros((count, length), FLOAT)] * (edge_ref.shape[1] // length)
-        for plane in range(planes):
-            for comp in range(COMP):
-                values = wide_scr[pl.ds(comp * planes + plane, count, stride=COMP * planes), :]
-                low = values.astype(SHORT)
-                at = (plane * COMP + comp) * length
-                all_ref[here, at : at + length] = low
-                if plane == 0:
-                    first_ref[here, comp * length : (comp + 1) * length] = low
-                tile, slot = divmod(plane * COMP + comp, per_tile)
-                moved = values if slot == 0 else pltpu.roll(values, slot * LZ, 1)
-                tiles[tile] = jnp.where(lane // LZ == slot, moved, tiles[tile])
-        for tile, values in enumerate(tiles):
-            edge_ref[here, tile * length : (tile + 1) * length] = values.astype(SHORT)
+    tiles = [jnp.zeros((count, length), FLOAT)] * (edge_ref.shape[1] // length)
+    for plane in range(planes):
+        for comp in range(COMP):
+            values = wide_scr[pl.ds(comp * planes + plane, count, stride=COMP * planes), :]
+            at = (plane * COMP + comp) * length
+            all_ref[:, at : at + length] = values.astype(SHORT)
+            tile, slot = divmod(plane * COMP + comp, per_tile)
+            moved = values if slot == 0 else pltpu.roll(values, slot * LZ, 1)
+            tiles[tile] = jnp.where(lane // LZ == slot, moved, tiles[tile])
+    for tile, values in enumerate(tiles):
+        edge_ref[:, tile * length : (tile + 1) * length] = values.astype(SHORT)
+
+
+def by_rows(kernel, flat, count, planes, widths, block):
+    rows = COMP * planes
+    length = flat.shape[1]
+    return pl.pallas_call(
+        functools.partial(kernel, planes),
+        grid=(count // block,),
+        out_shape=[jax.ShapeDtypeStruct((count, width), SHORT) for width in widths],
+        in_specs=[pl.BlockSpec((block * rows, length), lambda i: (i, 0))],
+        out_specs=[pl.BlockSpec((block, width), lambda i: (i, 0)) for width in widths],
+        scratch_shapes=[pltpu.VMEM((block * rows, length), FLOAT)],
+        compiler_params=pltpu.CompilerParams(vmem_limit_bytes=VMEM_BYTES),
+        cost_estimate=pl.CostEstimate(flops=1, bytes_accessed=1, transcendentals=0),
+    )(flat)
 
 
 def split_vectors(vectors):
     count, _, _, planes, length = vectors.shape
-    rows = COMP * planes
-    edge_tiles = -(-rows // (length // LZ))
-    blocks = 8
-    shapes = [rows * length, COMP * length, edge_tiles * length]
-    return call(
-        functools.partial(split_kernel, planes),
-        [jax.ShapeDtypeStruct((count, s), SHORT) for s in shapes],
-        [pl.BlockSpec(memory_space=pltpu.HBM)],
-        [
-            pltpu.VMEM((count * rows, length), SHORT),
-            pltpu.VMEM((count // blocks * rows, length), FLOAT),
-            pltpu.SemaphoreType.DMA((blocks,)),
-        ],
-    )(vectors.reshape(count * rows, length))
+    flat = vectors.reshape(-1, length)
+    edge_tiles = -(-COMP * planes // (length // LZ))
+    (first,) = by_rows(front_kernel, flat, count, planes, [COMP * length], 64)
+    _, flat = lax.optimization_barrier((first, flat))
+    widths = [COMP * planes * length, edge_tiles * length]
+    vec, edge = by_rows(split_kernel, flat, count, planes, widths, 256)
+    return vec, first, edge
 
 
 def times_transposed(left, right):
@@ -231,8 +235,6 @@
         out_shape,
         [SMEM_SPEC] + [VMEM_SPEC] * (len(operands) - 1),
         scratch,
-        flops=1,
-        size=1,
     )(*operands)
 
 
@@ -451,7 +453,7 @@
     def over_narrow(parts, tie=None):
         keep, send = halve(*[(k[None], swap(s, "narrow", 1)[None]) for k, s in parts])
         if tie is not None:
-            keep, send, tie = lax.optimization_barrier((keep, send, tie))
+            _, tie = lax.optimization_barrier((keep, tie))
         for stage in range(1, narrow_count.bit_length() - 1):
             came = swap(send, "narrow", 1 << stage)
             if keep.shape[1] > 1:
@@ -467,14 +469,14 @@
     second = part(1, every, halo=edge_halo)
     inner = part(0, every[:-1], more="first")
     keep, came, plane_halo = over_narrow([second, third], plane_halo)
-    own, near, far = over_wide(*expand(here, keep, came, wide_count, pair), pair)
-    early = total(own, far)
-    pairs = jnp.concatenate([pair, near[near.shape[0] - pair.shape[0] :]], 0)
-
+    early, near, far = over_wide(*expand(here, keep, came, wide_count, pair), pair)
     whole = part(0, every[-1:], halo=plane_halo, more=inner)
     keep, came, _ = over_narrow([whole])
-    own, _, late = over_wide(*expand(here, keep, came, wide_count))
-    rows = [total(own, late, early)]
+    _, came = lax.optimization_barrier((early, came))
+    late, _, rest = over_wide(*expand(here, keep, came, wide_count))
+    pairs = jnp.concatenate([pair, near[near.shape[0] - pair.shape[0] :]], 0)
+
+    rows = [total(late, rest, total(early, far))]
     order = [0]
     for stage in reversed(range(narrow_count.bit_length() - 1)):
         rows = rows + [swap(x, "narrow", 1 << stage) for x in rows]

time: 68 us -> 64.1 us (0.943)
  starting transfers between devices: 24.6 us -> 20.8 us
  Pallas kernels: 22.5 us -> 20.3 us
  waiting for transfers between devices: 18.2 us -> 20.2 us
    ppermute x16, waiting for transfers between devices: 15.2 us -> 19.9 us  [swap(): return lax.ppermute(x, axis, [(i, i ^ mask) for i in range(length)])]
    ppermute x16, starting transfers between devices: 17.9 us -> 14.1 us  [swap(): return lax.ppermute(x, axis, [(i, i ^ mask) for i in range(length)])]
    ppermute x2, waiting for transfers between devices: 3.09 us -> 0.32 us  [from_behind(): lax.ppermute(x, axis, [(i, (i + by) % length) for i in range(length)])]
    pallas_call x1 -> x2, Pallas kernels: 4.09 us -> 1.98 us  [by_rows(): pl.pallas_call(functools.partial(kernel, planes), grid=(count // block,),...]
  transfers between devices with their start and end apart: 18 -> 18, of which waited for: 8 -> 8; matrix products, arithmetic and copies ran while one was open for 0% -> 0% of each run, Pallas kernels for 24% -> 27%
where the time goes in v3:
time: 64.1 us; the launch traced here: 63.9 us
  starting transfers between devices  20.8 us (32%)
  Pallas kernels  20.3 us (32%)
  waiting for transfers between devices  20.2 us (32%)
  local copies, waits for them, and re-layouts  1.46 us (2%)
  between operations  0.85 us (1%)
    ppermute x16, waiting for transfers between devices, swap(): return lax.ppermute(x, axis, [(i, i ^ mask) for i in range(length)])  19.9 us
    pallas_call x4, Pallas kernels, direction_part(): call(functools.partial(direction_kernel, direction, chosen, planes, norm,...  14.7 us
    ppermute x16, starting transfers between devices, swap(): return lax.ppermute(x, axis, [(i, i ^ mask) for i in range(length)])  14.1 us
    ppermute x2, starting transfers between devices, from_behind(): lax.ppermute(x, axis, [(i, (i + by) % length) for i in range(length)])  6.71 us
    pallas_call x2, Pallas kernels, by_rows(): pl.pallas_call(functools.partial(kernel, planes), grid=(count // block,),...  1.98 us
    pallas_call x1, Pallas kernels, finish(): call(functools.partial(finish_kernel, order), [jax.ShapeDtypeStruct((slot...  1.75 us
    pallas_call x2, Pallas kernels, expand(): call(functools.partial(expand_kernel, extra is not None), [jax.ShapeDtype...  1.59 us
    unnamed x8, local copies, waits for them, and re-layouts  1.41 us
  transfers between devices with their start and end apart: 18, of which 8 were waited for; matrix products, arithmetic and copies ran while one was open for 0% of the time, Pallas kernels for 27%

profile of v3, /device:TPU:0, one launch (start us, length us, event | category | flops | bytes accessed | tf_op | source)
XLA Modules:
  0.0 63.9 jit_solution(12316617377712904929)
XLA Ops:
  0.6 1.4 %copy-done = bf16[512,2,3,2,128]{4,3,2,1,0:T(2,128)(2,1)S(1)} copy-done((bf16[512,2,3,2,128]{4,3,2,1,0:T(2,128)(2,1)S(1)}, bf16[512,2,3,2,128]{4,3,2,1,0:T(2,128)(2,1)}, u32[]{:S(2)}) %copy-start) | copy-done | bytes 1572888
  2.0 0.4 shard_map.59
  2.5 6.1 %collective-permute-start.3 = (bf16[512,768]{1,0:T(8,128)(2,1)S(1)}, bf16[512,768]{1,0:T(8,128)(2,1)S(1)}, u32[]{:S(2)}, u32[]{:S(2)}) collective-permute-start(bf16[512,768]{1,0:T(8,128)(2,1)S(1)} %shard_map.59), channel_id=1, source_target_pairs={{0,28},{4,0},{8,4},{12,8},{16,12},{20,16},{24,20},{28,24},{1,29},{... | collective-permute-start | bytes 2359304 | tf_op jit(solution)/shard_map/ppermute | solution.py:35
  8.5 1.5 %shard_map.60 = (bf16[512,1536]{1,0:T(8,128)(2,1)S(1)}, bf16[512,256]{1,0:T(8,128)(2,1)}) custom-call(bf16[6144,128]{1,0:T(8,128)(2,1)S(1)} %bitcast.14), custom_call_target="tpu_custom_call" | custom-call | flops 1 | bytes 1 | tf_op jit(solution)/shard_map/pallas_call | solution.py:74
  10.1 0.7 %collective-permute-start = (bf16[512,256]{1,0:T(8,128)(2,1)}, bf16[512,256]{1,0:T(8,128)(2,1)S(1)}, u32[]{:S(2)}, u32[]{:S(2)}) collective-permute-start(bf16[512,256]{1,0:T(8,128)(2,1)} %get-tuple-element.31), channel_id=1, source_target_pairs={{0,3},{1,0},{2,1},{3,2},{4,7},{5,4},{6,5},{7,6},{8,11},{9,8},{10,9... | collective-permute-start | bytes 786440 | tf_op jit(solution)/shard_map/ppermute | solution.py:35
  10.9 4.8 %shard_map.62 = (f32[2,4,128,128]{3,2,1,0:T(8,128)S(1)}, bf16[2,4,128,128]{3,2,1,0:T(8,128)(2,1)S(1)}) custom-call(s32[2]{0:T(128)S(1)} %pad_add_fusion.refs_0_.here_ref, f32[108,128]{1,0:T(8,128)S(1)} %reshape.10.refs_1_, bf16[512,1536]{1,0:T(8,128)(2,1)S(1)} %get-tuple-element.30.refs_2_), custom_call_target="tpu_custom_call" | custom-call | flops 1 | bytes 1 | tf_op jit(solution)/shard_map/pallas_call | solution.py:231
  15.8 4.8 %shard_map.61 = (f32[2,4,128,128]{3,2,1,0:T(8,128)S(1)}, bf16[2,4,128,128]{3,2,1,0:T(8,128)(2,1)S(1)}) custom-call(s32[2]{0:T(128)S(1)} %pad_add_fusion.refs_0_.here_ref, f32[108,128]{1,0:T(8,128)S(1)} %reshape.10.refs_1_, bf16[512,1536]{1,0:T(8,128)(2,1)S(1)} %get-tuple-element.30.refs_2_, bf16[512,256]{1,0:T(8,128)(2,1)S(1)} %collective-permute-done.refs_3_), custom_call_target="tpu_custom_call" | custom-call | flops 1 | bytes 1 | tf_op jit(solution)/shard_map/pallas_call | solution.py:231
  20.6 0.6 collective-permute-start.1
  21.2 2.5 %shard_map.64.refs_4_ = f32[4,4,128,128]{3,2,1,0:T(8,128)S(1)} custom-call(s32[2]{0:T(128)S(1)} %pad_add_fusion.refs_0_.here_ref, f32[108,128]{1,0:T(8,128)S(1)} %reshape.10.refs_1_, bf16[512,1536]{1,0:T(8,128)(2,1)S(1)} %get-tuple-element.30.refs_2_), custom_call_target="tpu_custom_call" | custom-call | flops 1 | bytes 1 | tf_op jit(solution)/shard_map/pallas_call | solution.py:231
  23.7 0.1 shard_map.63
  23.8 1.2 %collective-permute-start.5 = (bf16[2,1,4,128,128]{4,3,2,1,0:T(8,128)(2,1)S(1)}, bf16[2,1,4,128,128]{4,3,2,1,0:T(8,128)(2,1)S(1)}, u32[]{:S(2)}, u32[]{:S(2)}) collective-permute-start(bf16[2,1,4,128,128]{4,3,2,1,0:T(8,128)(2,1)S(1)} %get-tuple-element.41), channel_id=1, source_target_pairs={{0,2},{1,3},{2,0},{3,1},{4,6},{5,7},{6,4},{7,5},{8,10},{9,11},{10,... | collective-permute-start | bytes 786440 | tf_op jit(solution)/shard_map/ppermute | solution.py:40
  25.0 0.3 collective-permute-done.3.refs_3_
  25.3 2.6 %shard_map.65 = (f32[2,4,128,128]{3,2,1,0:T(8,128)S(1)}, bf16[2,4,128,128]{3,2,1,0:T(8,128)(2,1)S(1)}) custom-call(s32[2]{0:T(128)S(1)} %pad_add_fusion.refs_0_.here_ref, f32[108,128]{1,0:T(8,128)S(1)} %reshape.10.refs_1_, bf16[512,1536]{1,0:T(8,128)(2,1)S(1)} %get-tuple-element.30.refs_2_, bf16[512,768]{1,0:T(8,128)(2,1)S(1)} %collective-permute-done.3.refs_3_, ...), custom_call_target="tpu_custom_call" | custom-call | flops 1 | bytes 1 | tf_op jit(solution)/shard_map/pallas_call | solution.py:231
  28.1 0.1 pad_maximum_fusion.1.refs_0_
  28.1 4.0 %collective-permute-done.5.came_ref = bf16[2,1,4,128,128]{4,3,2,1,0:T(8,128)(2,1)S(1)} collective-permute-done((bf16[2,1,4,128,128]{4,3,2,1,0:T(8,128)(2,1)S(1)}, bf16[2,1,4,128,128]{4,3,2,1,0:T(8,128)(2,1)S(1)}, u32[]{:S(2)}, u32[]{:S(2)}) %collective-permute-start.5) | collective-permute-done | bytes 262176 | tf_op jit(solution)/shard_map/ppermute | solution.py:40
  32.1 0.9 %shard_map.67 = (f32[4,256,128]{2,1,0:T(8,128)S(1)}, bf16[1088,128]{1,0:T(8,128)(2,1)S(1)}) custom-call(s32[2]{0:T(128)S(1)} %pad_add_fusion.refs_0_.here_ref, f32[2,1,4,128,128]{4,3,2,1,0:T(8,128)S(1)} %get-tuple-element.36.keep_ref, bf16[2,1,4,128,128]{4,3,2,1,0:T(8,128)(2,1)S(1)} %collective-permute-done.5.came_ref, ...), custom_call_target="tpu_custom_call" | custom-call | flops 1 | bytes 1 | tf_op jit(solution)/shard_map/pallas_call | solution.py:304
  33.1 1.4 %collective-permute-start.7 = (bf16[1,1,4,128,128]{4,3,2,1,0:T(8,128)(2,1)S(1)}, bf16[1,1,4,128,128]{4,3,2,1,0:T(8,128)(2,1)S(1)}, u32[]{:S(2)}, u32[]{:S(2)}) collective-permute-start(bf16[1,1,4,128,128]{4,3,2,1,0:T(8,128)(2,1)S(1)} %get-tuple-element.45), channel_id=1, source_target_pairs={{0,2},{1,3},{2,0},{3,1},{4,6},{5,7},{6,4},{7,5},{8,10},{9,11},{10,... | collective-permute-start | bytes 393224 | tf_op jit(solution)/shard_map/ppermute | solution.py:40
  34.5 6.2 %collective-permute-done.6.came_ref = bf16[1088,128]{1,0:T(8,128)(2,1)S(1)} collective-permute-done((bf16[1088,128]{1,0:T(8,128)(2,1)S(1)}, bf16[1088,128]{1,0:T(8,128)(2,1)S(1)}, u32[]{:S(2)}, u32[]{:S(2)}) %collective-permute-start.6) | collective-permute-done | bytes 278560 | tf_op jit(solution)/shard_map/ppermute | solution.py:40
  40.8 0.7 %shard_map.69 = (f32[4,128,128]{2,1,0:T(8,128)S(1)}, bf16[512,128]{1,0:T(8,128)(2,1)S(1)}) custom-call(s32[2]{0:T(128)S(1)} %pad_add_fusion.refs_0_.here_ref, f32[1,1,4,128,128]{4,3,2,1,0:T(8,128)S(1)} %get-tuple-element.40.keep_ref, bf16[1,1,4,128,128]{4,3,2,1,0:T(8,128)(2,1)S(1)} %collective-permute-done.7.came_ref), custom_call_target="tpu_custom_call" | custom-call | flops 1 | bytes 1 | tf_op jit(solution)/shard_map/pallas_call | solution.py:304
  41.6 0.4 collective-permute-start.8
  41.9 3.4 %collective-permute-start.13 = (bf16[384,128]{1,0:T(8,128)(2,1)S(1)}, bf16[384,128]{1,0:T(8,128)(2,1)S(1)}, u32[]{:S(2)}, u32[]{:S(2)}) collective-permute-start(bf16[384,128]{1,0:T(8,128)(2,1)S(1)} %get-tuple-element.54), channel_id=1, source_target_pairs={{0,16},{4,20},{8,24},{12,28},{16,0},{20,4},{24,8},{28,12},{1,17},{... | collective-permute-start | bytes 294920 | tf_op jit(solution)/shard_map/ppermute | solution.py:40
  45.3 1.0 %collective-permute-start.14 = (bf16[384,128]{1,0:T(8,128)(2,1)S(1)}, bf16[384,128]{1,0:T(8,128)(2,1)S(1)}, u32[]{:S(2)}, u32[]{:S(2)}) collective-permute-start(bf16[384,128]{1,0:T(8,128)(2,1)S(1)} %get-tuple-element.55), channel_id=1, source_target_pairs={{0,24},{4,28},{8,16},{12,20},{16,8},{20,12},{24,0},{28,4},{1,25},{... | collective-permute-start | bytes 294920 | tf_op jit(solution)/shard_map/ppermute | solution.py:40
  46.3 0.3 collective-permute-done.8.came_ref
  46.7 3.1 %collective-permute-start.10 = (bf16[128,128]{1,0:T(8,128)(2,1)S(1)}, bf16[128,128]{1,0:T(8,128)(2,1)S(1)}, u32[]{:S(2)}, u32[]{:S(2)}) collective-permute-start(bf16[128,128]{1,0:T(8,128)(2,1)S(1)} %get-tuple-element.51), channel_id=1, source_target_pairs={{0,16},{4,20},{8,24},{12,28},{16,0},{20,4},{24,8},{28,12},{1,17},{... | collective-permute-start | bytes 98312 | tf_op jit(solution)/shard_map/ppermute | solution.py:40
  49.8 1.3 %collective-permute-start.11 = (bf16[128,128]{1,0:T(8,128)(2,1)S(1)}, bf16[128,128]{1,0:T(8,128)(2,1)S(1)}, u32[]{:S(2)}, u32[]{:S(2)}) collective-permute-start(bf16[128,128]{1,0:T(8,128)(2,1)S(1)} %get-tuple-element.52), channel_id=1, source_target_pairs={{0,24},{4,28},{8,16},{12,20},{16,8},{20,12},{24,0},{28,4},{1,25},{... | collective-permute-start | bytes 98312 | tf_op jit(solution)/shard_map/ppermute | solution.py:40
  51.1 2.7 %collective-permute-done.13.refs_2_.refs_6_ = bf16[384,128]{1,0:T(8,128)(2,1)S(1)} collective-permute-done((bf16[384,128]{1,0:T(8,128)(2,1)S(1)}, bf16[384,128]{1,0:T(8,128)(2,1)S(1)}, u32[]{:S(2)}, u32[]{:S(2)}) %collective-permute-start.13) | collective-permute-done | bytes 98336 | tf_op jit(solution)/shard_map/ppermute | solution.py:40
  53.8 2.4 %collective-permute-done.10.refs_2_ = bf16[128,128]{1,0:T(8,128)(2,1)S(1)} collective-permute-done((bf16[128,128]{1,0:T(8,128)(2,1)S(1)}, bf16[128,128]{1,0:T(8,128)(2,1)S(1)}, u32[]{:S(2)}, u32[]{:S(2)}) %collective-permute-start.10) | collective-permute-done | bytes 32800 | tf_op jit(solution)/shard_map/ppermute | solution.py:40
  56.2 1.6 %collective-permute-start.15 = (bf16[384,128]{1,0:T(8,128)(2,1)S(1)}, bf16[384,128]{1,0:T(8,128)(2,1)S(1)}, u32[]{:S(2)}, u32[]{:S(2)}) collective-permute-start(bf16[384,128]{1,0:T(8,128)(2,1)S(1)} %shard_map.72.refs_0_), channel_id=1, source_target_pairs={{0,2},{1,3},{2,0},{3,1},{4,6},{5,7},{6,4},{7,5},{8,10},{9,11},{10,... | collective-permute-start | bytes 294920 | tf_op jit(solution)/shard_map/ppermute | solution.py:40
  57.8 3.1 %collective-permute-done.15.refs_1_ = bf16[384,128]{1,0:T(8,128)(2,1)S(1)} collective-permute-done((bf16[384,128]{1,0:T(8,128)(2,1)S(1)}, bf16[384,128]{1,0:T(8,128)(2,1)S(1)}, u32[]{:S(2)}, u32[]{:S(2)}) %collective-permute-start.15) | collective-permute-done | bytes 98336 | tf_op jit(solution)/shard_map/ppermute | solution.py:40
  60.9 0.1 pad_maximum_fusion.refs_4_
  61.0 1.2 %collective-permute-done.17.refs_3_ = bf16[384,128]{1,0:T(8,128)(2,1)S(1)} collective-permute-done((bf16[384,128]{1,0:T(8,128)(2,1)S(1)}, bf16[384,128]{1,0:T(8,128)(2,1)S(1)}, u32[]{:S(2)}, u32[]{:S(2)}) %collective-permute-start.17) | collective-permute-done | bytes 98336 | tf_op jit(solution)/shard_map/ppermute | solution.py:40
  62.2 1.8 %shard_map.73 = (f32[3,2,64,512]{3,2,1,0:T(8,128)}, f32[3,2,64,64]{3,2,1,0:T(8,128)}) custom-call(s32[2]{0:T(128)S(1)} %pad_add_fusion.refs_0_.here_ref, s32[3]{0:T(128)S(1)} %copy-done.1, bf16[384,128]{1,0:T(8,128)(2,1)S(1)} %shard_map.72.refs_0_, bf16[384,128]{1,0:T(8,128)(2,1)S(1)} %collective-permute-done.15.refs_1_, ...), custom_call_target="tpu_custom_call" | custom-call | flops 1 | bytes 1 | tf_op jit(solution)/shard_map/pallas_call | solution.py:420
  (33 shorter events, 0.6 us)
Async XLA Ops:
  0.6 1.4 %copy-start = (bf16[512,2,3,2,128]{4,3,2,1,0:T(2,128)(2,1)S(1)}, bf16[512,2,3,2,128]{4,3,2,1,0:T(2,128)(2,1)}, u32[]{:S(2)}) copy-start(bf16[512,2,3,2,128]{4,3,2,1,0:T(2,128)(2,1)} %param.4) | copy-start | bytes 4718596
  2.0 8.7 %copy-start.2 = (f32[3,2,3,3,2,128]{5,4,3,2,1,0:T(2,128)S(1)}, f32[3,2,3,3,2,128]{5,4,3,2,1,0:T(2,128)}, u32[]{:S(2)}) copy-start(f32[3,2,3,3,2,128]{5,4,3,2,1,0:T(2,128)} %param.5) | copy-start | bytes 165892
  2.5 22.9 %collective-permute-start.3 = (bf16[512,768]{1,0:T(8,128)(2,1)S(1)}, bf16[512,768]{1,0:T(8,128)(2,1)S(1)}, u32[]{:S(2)}, u32[]{:S(2)}) collective-permute-start(bf16[512,768]{1,0:T(8,128)(2,1)S(1)} %shard_map.59), channel_id=1, source_target_pairs={{0,28},{4,0},{8,4},{12,8},{16,12},{20,16},{24,20},{28,24},{1,29},{... | collective-permute-start | bytes 2359304 | tf_op jit(solution)/shard_map/ppermute | solution.py:35
  10.1 5.7 %collective-permute-start = (bf16[512,256]{1,0:T(8,128)(2,1)}, bf16[512,256]{1,0:T(8,128)(2,1)S(1)}, u32[]{:S(2)}, u32[]{:S(2)}) collective-permute-start(bf16[512,256]{1,0:T(8,128)(2,1)} %get-tuple-element.31), channel_id=1, source_target_pairs={{0,3},{1,0},{2,1},{3,2},{4,7},{5,4},{6,5},{7,6},{8,11},{9,8},{10,9... | collective-permute-start | bytes 786440 | tf_op jit(solution)/shard_map/ppermute | solution.py:35
  15.7 8.0 %collective-permute-start.2 = (bf16[2,4,128,128]{3,2,1,0:T(8,128)(2,1)S(1)}, bf16[2,4,128,128]{3,2,1,0:T(8,128)(2,1)S(1)}, u32[]{:S(2)}, u32[]{:S(2)}) collective-permute-start(bf16[2,4,128,128]{3,2,1,0:T(8,128)(2,1)S(1)} %get-tuple-element.35), channel_id=1, source_target_pairs={{0,1},{1,0},{2,3},{3,2},{4,5},{5,4},{6,7},{7,6},{8,9},{9,8},{10,11... | collective-permute-start | bytes 786440 | tf_op jit(solution)/shard_map/ppermute | solution.py:40
  20.6 3.1 %collective-permute-start.1 = (bf16[2,4,128,128]{3,2,1,0:T(8,128)(2,1)S(1)}, bf16[2,4,128,128]{3,2,1,0:T(8,128)(2,1)S(1)}, u32[]{:S(2)}, u32[]{:S(2)}) collective-permute-start(bf16[2,4,128,128]{3,2,1,0:T(8,128)(2,1)S(1)} %get-tuple-element.33), channel_id=1, source_target_pairs={{0,1},{1,0},{2,3},{3,2},{4,5},{5,4},{6,7},{7,6},{8,9},{9,8},{10,11... | collective-permute-start | bytes 786440 | tf_op jit(solution)/shard_map/ppermute | solution.py:40
  23.8 8.3 %collective-permute-start.5 = (bf16[2,1,4,128,128]{4,3,2,1,0:T(8,128)(2,1)S(1)}, bf16[2,1,4,128,128]{4,3,2,1,0:T(8,128)(2,1)S(1)}, u32[]{:S(2)}, u32[]{:S(2)}) collective-permute-start(bf16[2,1,4,128,128]{4,3,2,1,0:T(8,128)(2,1)S(1)} %get-tuple-element.41), channel_id=1, source_target_pairs={{0,2},{1,3},{2,0},{3,1},{4,6},{5,7},{6,4},{7,5},{8,10},{9,11},{10,... | collective-permute-start | bytes 786440 | tf_op jit(solution)/shard_map/ppermute | solution.py:40
  25.3 2.7 %copy-start.3 = (bf16[2,64,64]{2,1,0:T(8,128)(2,1)S(1)}, bf16[2,64,64]{2,1,0:T(8,128)(2,1)}, u32[]{:S(2)}) copy-start(bf16[2,64,64]{2,1,0:T(8,128)(2,1)} %param.7) | copy-start | bytes 49156
  27.9 5.1 %collective-permute-start.4 = (bf16[2,4,128,128]{3,2,1,0:T(8,128)(2,1)S(1)}, bf16[2,4,128,128]{3,2,1,0:T(8,128)(2,1)S(1)}, u32[]{:S(2)}, u32[]{:S(2)}) collective-permute-start(bf16[2,4,128,128]{3,2,1,0:T(8,128)(2,1)S(1)} %get-tuple-element.39), channel_id=1, source_target_pairs={{0,1},{1,0},{2,3},{3,2},{4,5},{5,4},{6,7},{7,6},{8,9},{9,8},{10,11... | collective-permute-start | bytes 786440 | tf_op jit(solution)/shard_map/ppermute | solution.py:40
  33.0 7.8 %collective-permute-start.6 = (bf16[1088,128]{1,0:T(8,128)(2,1)S(1)}, bf16[1088,128]{1,0:T(8,128)(2,1)S(1)}, u32[]{:S(2)}, u32[]{:S(2)}) collective-permute-start(bf16[1088,128]{1,0:T(8,128)(2,1)S(1)} %get-tuple-element.43), channel_id=1, source_target_pairs={{0,4},{4,0},{8,12},{12,8},{16,20},{20,16},{24,28},{28,24},{1,5},{5... | collective-permute-start | bytes 835592 | tf_op jit(solution)/shard_map/ppermute | solution.py:40
  33.0 29.1 %copy-start.1 = (s32[3]{0:T(128)S(1)}, s32[3]{0:T(128)}, u32[]{:S(2)}) copy-start(s32[3]{0:T(128)} %list_ref.1) | copy-start | bytes 40
  33.1 7.7 %collective-permute-start.7 = (bf16[1,1,4,128,128]{4,3,2,1,0:T(8,128)(2,1)S(1)}, bf16[1,1,4,128,128]{4,3,2,1,0:T(8,128)(2,1)S(1)}, u32[]{:S(2)}, u32[]{:S(2)}) collective-permute-start(bf16[1,1,4,128,128]{4,3,2,1,0:T(8,128)(2,1)S(1)} %get-tuple-element.45), channel_id=1, source_target_pairs={{0,2},{1,3},{2,0},{3,1},{4,6},{5,7},{6,4},{7,5},{8,10},{9,11},{10,... | collective-permute-start | bytes 393224 | tf_op jit(solution)/shard_map/ppermute | solution.py:40
  41.6 5.0 %collective-permute-start.8 = (bf16[512,128]{1,0:T(8,128)(2,1)S(1)}, bf16[512,128]{1,0:T(8,128)(2,1)S(1)}, u32[]{:S(2)}, u32[]{:S(2)}) collective-permute-start(bf16[512,128]{1,0:T(8,128)(2,1)S(1)} %get-tuple-element.48), channel_id=1, source_target_pairs={{0,4},{4,0},{8,12},{12,8},{16,20},{20,16},{24,28},{28,24},{1,5},{5... | collective-permute-start | bytes 393224 | tf_op jit(solution)/shard_map/ppermute | solution.py:40
  41.9 7.9 %collective-permute-start.12 = (bf16[384,128]{1,0:T(8,128)(2,1)S(1)}, bf16[384,128]{1,0:T(8,128)(2,1)S(1)}, u32[]{:S(2)}, u32[]{:S(2)}) collective-permute-start(bf16[384,128]{1,0:T(8,128)(2,1)S(1)} %get-tuple-element.53), channel_id=1, source_target_pairs={{0,8},{4,12},{8,0},{12,4},{16,24},{20,28},{24,16},{28,20},{1,9},{5... | collective-permute-start | bytes 294920 | tf_op jit(solution)/shard_map/ppermute | solution.py:40
  41.9 11.8 %collective-permute-start.13 = (bf16[384,128]{1,0:T(8,128)(2,1)S(1)}, bf16[384,128]{1,0:T(8,128)(2,1)S(1)}, u32[]{:S(2)}, u32[]{:S(2)}) collective-permute-start(bf16[384,128]{1,0:T(8,128)(2,1)S(1)} %get-tuple-element.54), channel_id=1, source_target_pairs={{0,16},{4,20},{8,24},{12,28},{16,0},{20,4},{24,8},{28,12},{1,17},{... | collective-permute-start | bytes 294920 | tf_op jit(solution)/shard_map/ppermute | solution.py:40
  45.3 8.5 %collective-permute-start.14 = (bf16[384,128]{1,0:T(8,128)(2,1)S(1)}, bf16[384,128]{1,0:T(8,128)(2,1)S(1)}, u32[]{:S(2)}, u32[]{:S(2)}) collective-permute-start(bf16[384,128]{1,0:T(8,128)(2,1)S(1)} %get-tuple-element.55), channel_id=1, source_target_pairs={{0,24},{4,28},{8,16},{12,20},{16,8},{20,12},{24,0},{28,4},{1,25},{... | collective-permute-start | bytes 294920 | tf_op jit(solution)/shard_map/ppermute | solution.py:40
  46.6 7.2 %collective-permute-start.9 = (bf16[128,128]{1,0:T(8,128)(2,1)S(1)}, bf16[128,128]{1,0:T(8,128)(2,1)S(1)}, u32[]{:S(2)}, u32[]{:S(2)}) collective-permute-start(bf16[128,128]{1,0:T(8,128)(2,1)S(1)} %get-tuple-element.50), channel_id=1, source_target_pairs={{0,8},{4,12},{8,0},{12,4},{16,24},{20,28},{24,16},{28,20},{1,9},{5... | collective-permute-start | bytes 98312 | tf_op jit(solution)/shard_map/ppermute | solution.py:40
  46.7 9.5 %collective-permute-start.10 = (bf16[128,128]{1,0:T(8,128)(2,1)S(1)}, bf16[128,128]{1,0:T(8,128)(2,1)S(1)}, u32[]{:S(2)}, u32[]{:S(2)}) collective-permute-start(bf16[128,128]{1,0:T(8,128)(2,1)S(1)} %get-tuple-element.51), channel_id=1, source_target_pairs={{0,16},{4,20},{8,24},{12,28},{16,0},{20,4},{24,8},{28,12},{1,17},{... | collective-permute-start | bytes 98312 | tf_op jit(solution)/shard_map/ppermute | solution.py:40
  49.8 6.4 %collective-permute-start.11 = (bf16[128,128]{1,0:T(8,128)(2,1)S(1)}, bf16[128,128]{1,0:T(8,128)(2,1)S(1)}, u32[]{:S(2)}, u32[]{:S(2)}) collective-permute-start(bf16[128,128]{1,0:T(8,128)(2,1)S(1)} %get-tuple-element.52), channel_id=1, source_target_pairs={{0,24},{4,28},{8,16},{12,20},{16,8},{20,12},{24,0},{28,4},{1,25},{... | collective-permute-start | bytes 98312 | tf_op jit(solution)/shard_map/ppermute | solution.py:40
  56.2 4.7 %collective-permute-start.15 = (bf16[384,128]{1,0:T(8,128)(2,1)S(1)}, bf16[384,128]{1,0:T(8,128)(2,1)S(1)}, u32[]{:S(2)}, u32[]{:S(2)}) collective-permute-start(bf16[384,128]{1,0:T(8,128)(2,1)S(1)} %shard_map.72.refs_0_), channel_id=1, source_target_pairs={{0,2},{1,3},{2,0},{3,1},{4,6},{5,7},{6,4},{7,5},{8,10},{9,11},{10,... | collective-permute-start | bytes 294920 | tf_op jit(solution)/shard_map/ppermute | solution.py:40
  57.8 3.2 %collective-permute-start.16 = (bf16[384,128]{1,0:T(8,128)(2,1)S(1)}, bf16[384,128]{1,0:T(8,128)(2,1)S(1)}, u32[]{:S(2)}, u32[]{:S(2)}) collective-permute-start(bf16[384,128]{1,0:T(8,128)(2,1)S(1)} %shard_map.72.refs_0_), channel_id=1, source_target_pairs={{0,1},{1,0},{2,3},{3,2},{4,5},{5,4},{6,7},{7,6},{8,9},{9,8},{10,11... | collective-permute-start | bytes 294920 | tf_op jit(solution)/shard_map/ppermute | solution.py:40
  60.9 1.3 %collective-permute-start.17 = (bf16[384,128]{1,0:T(8,128)(2,1)S(1)}, bf16[384,128]{1,0:T(8,128)(2,1)S(1)}, u32[]{:S(2)}, u32[]{:S(2)}) collective-permute-start(bf16[384,128]{1,0:T(8,128)(2,1)S(1)} %collective-permute-done.15.refs_1_), channel_id=1, source_target_pairs={{0,1},{1,0},{2,3},{3,2},{4,5},{5,4},{6,7},{7,6},{8,9},{9,8},{10,11... | collective-permute-start | bytes 294920 | tf_op jit(solution)/shard_map/ppermute | solution.py:40

commit v4 on v3

--- a/solution.py
+++ b/solution.py
@@ -472,7 +472,6 @@
     early, near, far = over_wide(*expand(here, keep, came, wide_count, pair), pair)
     whole = part(0, every[-1:], halo=plane_halo, more=inner)
     keep, came, _ = over_narrow([whole])
-    _, came = lax.optimization_barrier((early, came))
     late, _, rest = over_wide(*expand(here, keep, came, wide_count))
     pairs = jnp.concatenate([pair, near[near.shape[0] - pair.shape[0] :]], 0)
 

time: 64.1 us -> 61.9 us (0.966)
  waiting for transfers between devices: 20.2 us -> 17 us
  starting transfers between devices: 20.8 us -> 21.9 us
    ppermute x16, waiting for transfers between devices: 19.9 us -> 16.6 us  [swap(): return lax.ppermute(x, axis, [(i, i ^ mask) for i in range(length)])]
    ppermute x16, starting transfers between devices: 14.1 us -> 15.2 us  [swap(): return lax.ppermute(x, axis, [(i, i ^ mask) for i in range(length)])]
  transfers between devices with their start and end apart: 18 -> 18, of which waited for: 8 -> 10; matrix products, arithmetic and copies ran while one was open for 0% -> 0% of each run, Pallas kernels for 27% -> 29%
where the time goes in v4:
time: 61.9 us; the launch traced here: 61.8 us
  starting transfers between devices  21.9 us (35%)
  Pallas kernels  20.4 us (33%)
  waiting for transfers between devices  17 us (27%)
  local copies, waits for them, and re-layouts  1.46 us (2%)
  between operations  0.85 us (1%)
    ppermute x16, waiting for transfers between devices, swap(): return lax.ppermute(x, axis, [(i, i ^ mask) for i in range(length)])  16.6 us
    ppermute x16, starting transfers between devices, swap(): return lax.ppermute(x, axis, [(i, i ^ mask) for i in range(length)])  15.2 us
    pallas_call x4, Pallas kernels, direction_part(): call(functools.partial(direction_kernel, direction, chosen, planes, norm,...  14.7 us
    ppermute x2, starting transfers between devices, from_behind(): lax.ppermute(x, axis, [(i, (i + by) % length) for i in range(length)])  6.71 us
    pallas_call x2, Pallas kernels, by_rows(): pl.pallas_call(functools.partial(kernel, planes), grid=(count // block,),...  1.98 us
    pallas_call x1, Pallas kernels, finish(): call(functools.partial(finish_kernel, order), [jax.ShapeDtypeStruct((slot...  1.75 us
    pallas_call x2, Pallas kernels, expand(): call(functools.partial(expand_kernel, extra is not None), [jax.ShapeDtype...  1.59 us
    unnamed x8, local copies, waits for them, and re-layouts  1.41 us
  transfers between devices with their start and end apart: 18, of which 10 were waited for; matrix products, arithmetic and copies ran while one was open for 0% of the time, Pallas kernels for 29%

profile of v4, /device:TPU:0, one launch (start us, length us, event | category | flops | bytes accessed | tf_op | source)
XLA Modules:
  0.0 61.8 jit_solution(13490261784182904399)
XLA Ops:
  0.6 1.4 %copy-done = bf16[512,2,3,2,128]{4,3,2,1,0:T(2,128)(2,1)S(1)} copy-done((bf16[512,2,3,2,128]{4,3,2,1,0:T(2,128)(2,1)S(1)}, bf16[512,2,3,2,128]{4,3,2,1,0:T(2,128)(2,1)}, u32[]{:S(2)}) %copy-start) | copy-done | bytes 1572888
  2.0 0.4 shard_map.59
  2.5 6.1 %collective-permute-start.3 = (bf16[512,768]{1,0:T(8,128)(2,1)S(1)}, bf16[512,768]{1,0:T(8,128)(2,1)S(1)}, u32[]{:S(2)}, u32[]{:S(2)}) collective-permute-start(bf16[512,768]{1,0:T(8,128)(2,1)S(1)} %shard_map.59), channel_id=1, source_target_pairs={{0,28},{4,0},{8,4},{12,8},{16,12},{20,16},{24,20},{28,24},{1,29},{... | collective-permute-start | bytes 2359304 | tf_op jit(solution)/shard_map/ppermute | solution.py:35
  8.5 1.5 %shard_map.60 = (bf16[512,1536]{1,0:T(8,128)(2,1)S(1)}, bf16[512,256]{1,0:T(8,128)(2,1)}) custom-call(bf16[6144,128]{1,0:T(8,128)(2,1)S(1)} %bitcast.14), custom_call_target="tpu_custom_call" | custom-call | flops 1 | bytes 1 | tf_op jit(solution)/shard_map/pallas_call | solution.py:74
  10.1 0.7 %collective-permute-start = (bf16[512,256]{1,0:T(8,128)(2,1)}, bf16[512,256]{1,0:T(8,128)(2,1)S(1)}, u32[]{:S(2)}, u32[]{:S(2)}) collective-permute-start(bf16[512,256]{1,0:T(8,128)(2,1)} %get-tuple-element.30), channel_id=1, source_target_pairs={{0,3},{1,0},{2,1},{3,2},{4,7},{5,4},{6,5},{7,6},{8,11},{9,8},{10,9... | collective-permute-start | bytes 786440 | tf_op jit(solution)/shard_map/ppermute | solution.py:35
  10.9 4.8 %shard_map.62 = (f32[2,4,128,128]{3,2,1,0:T(8,128)S(1)}, bf16[2,4,128,128]{3,2,1,0:T(8,128)(2,1)S(1)}) custom-call(s32[2]{0:T(128)S(1)} %pad_add_fusion.refs_0_.here_ref, f32[108,128]{1,0:T(8,128)S(1)} %reshape.10.refs_1_, bf16[512,1536]{1,0:T(8,128)(2,1)S(1)} %get-tuple-element.29.refs_2_), custom_call_target="tpu_custom_call" | custom-call | flops 1 | bytes 1 | tf_op jit(solution)/shard_map/pallas_call | solution.py:231
  15.8 4.8 %shard_map.61 = (f32[2,4,128,128]{3,2,1,0:T(8,128)S(1)}, bf16[2,4,128,128]{3,2,1,0:T(8,128)(2,1)S(1)}) custom-call(s32[2]{0:T(128)S(1)} %pad_add_fusion.refs_0_.here_ref, f32[108,128]{1,0:T(8,128)S(1)} %reshape.10.refs_1_, bf16[512,1536]{1,0:T(8,128)(2,1)S(1)} %get-tuple-element.29.refs_2_, bf16[512,256]{1,0:T(8,128)(2,1)S(1)} %collective-permute-done.refs_3_), custom_call_target="tpu_custom_call" | custom-call | flops 1 | bytes 1 | tf_op jit(solution)/shard_map/pallas_call | solution.py:231
  20.6 0.6 collective-permute-start.1
  21.2 2.5 %shard_map.64.refs_4_ = f32[4,4,128,128]{3,2,1,0:T(8,128)S(1)} custom-call(s32[2]{0:T(128)S(1)} %pad_add_fusion.refs_0_.here_ref, f32[108,128]{1,0:T(8,128)S(1)} %reshape.10.refs_1_, bf16[512,1536]{1,0:T(8,128)(2,1)S(1)} %get-tuple-element.29.refs_2_), custom_call_target="tpu_custom_call" | custom-call | flops 1 | bytes 1 | tf_op jit(solution)/shard_map/pallas_call | solution.py:231
  23.7 0.1 shard_map.63
  23.8 1.2 %collective-permute-start.10 = (bf16[2,1,4,128,128]{4,3,2,1,0:T(8,128)(2,1)S(1)}, bf16[2,1,4,128,128]{4,3,2,1,0:T(8,128)(2,1)S(1)}, u32[]{:S(2)}, u32[]{:S(2)}) collective-permute-start(bf16[2,1,4,128,128]{4,3,2,1,0:T(8,128)(2,1)S(1)} %get-tuple-element.47), channel_id=1, source_target_pairs={{0,2},{1,3},{2,0},{3,1},{4,6},{5,7},{6,4},{7,5},{8,10},{9,11},{10,... | collective-permute-start | bytes 786440 | tf_op jit(solution)/shard_map/ppermute | solution.py:40
  25.0 0.3 collective-permute-done.3.refs_3_
  25.3 2.6 %shard_map.65 = (f32[2,4,128,128]{3,2,1,0:T(8,128)S(1)}, bf16[2,4,128,128]{3,2,1,0:T(8,128)(2,1)S(1)}) custom-call(s32[2]{0:T(128)S(1)} %pad_add_fusion.refs_0_.here_ref, f32[108,128]{1,0:T(8,128)S(1)} %reshape.10.refs_1_, bf16[512,1536]{1,0:T(8,128)(2,1)S(1)} %get-tuple-element.29.refs_2_, bf16[512,768]{1,0:T(8,128)(2,1)S(1)} %collective-permute-done.3.refs_3_, ...), custom_call_target="tpu_custom_call" | custom-call | flops 1 | bytes 1 | tf_op jit(solution)/shard_map/pallas_call | solution.py:231
  28.1 4.0 %collective-permute-done.10.came_ref = bf16[2,1,4,128,128]{4,3,2,1,0:T(8,128)(2,1)S(1)} collective-permute-done((bf16[2,1,4,128,128]{4,3,2,1,0:T(8,128)(2,1)S(1)}, bf16[2,1,4,128,128]{4,3,2,1,0:T(8,128)(2,1)S(1)}, u32[]{:S(2)}, u32[]{:S(2)}) %collective-permute-start.10) | collective-permute-done | bytes 262176 | tf_op jit(solution)/shard_map/ppermute | solution.py:40
  32.1 0.9 %shard_map.69 = (f32[4,256,128]{2,1,0:T(8,128)S(1)}, bf16[1088,128]{1,0:T(8,128)(2,1)S(1)}) custom-call(s32[2]{0:T(128)S(1)} %pad_add_fusion.refs_0_.here_ref, f32[2,1,4,128,128]{4,3,2,1,0:T(8,128)S(1)} %get-tuple-element.35.keep_ref, bf16[2,1,4,128,128]{4,3,2,1,0:T(8,128)(2,1)S(1)} %collective-permute-done.10.came_ref, ...), custom_call_target="tpu_custom_call" | custom-call | flops 1 | bytes 1 | tf_op jit(solution)/shard_map/pallas_call | solution.py:304
  33.1 1.4 %collective-permute-start.5 = (bf16[1,1,4,128,128]{4,3,2,1,0:T(8,128)(2,1)S(1)}, bf16[1,1,4,128,128]{4,3,2,1,0:T(8,128)(2,1)S(1)}, u32[]{:S(2)}, u32[]{:S(2)}) collective-permute-start(bf16[1,1,4,128,128]{4,3,2,1,0:T(8,128)(2,1)S(1)} %get-tuple-element.40), channel_id=1, source_target_pairs={{0,2},{1,3},{2,0},{3,1},{4,6},{5,7},{6,4},{7,5},{8,10},{9,11},{10,... | collective-permute-start | bytes 393224 | tf_op jit(solution)/shard_map/ppermute | solution.py:40
  34.5 3.6 %collective-permute-done.5.came_ref = bf16[1,1,4,128,128]{4,3,2,1,0:T(8,128)(2,1)S(1)} collective-permute-done((bf16[1,1,4,128,128]{4,3,2,1,0:T(8,128)(2,1)S(1)}, bf16[1,1,4,128,128]{4,3,2,1,0:T(8,128)(2,1)S(1)}, u32[]{:S(2)}, u32[]{:S(2)}) %collective-permute-start.5) | collective-permute-done | bytes 131104 | tf_op jit(solution)/shard_map/ppermute | solution.py:40
  38.2 0.7 %shard_map.67 = (f32[4,128,128]{2,1,0:T(8,128)S(1)}, bf16[512,128]{1,0:T(8,128)(2,1)S(1)}) custom-call(s32[2]{0:T(128)S(1)} %pad_add_fusion.refs_0_.here_ref, f32[1,1,4,128,128]{4,3,2,1,0:T(8,128)S(1)} %get-tuple-element.39.keep_ref, bf16[1,1,4,128,128]{4,3,2,1,0:T(8,128)(2,1)S(1)} %collective-permute-done.5.came_ref), custom_call_target="tpu_custom_call" | custom-call | flops 1 | bytes 1 | tf_op jit(solution)/shard_map/pallas_call | solution.py:304
  38.9 2.1 %collective-permute-start.6 = (bf16[512,128]{1,0:T(8,128)(2,1)S(1)}, bf16[512,128]{1,0:T(8,128)(2,1)S(1)}, u32[]{:S(2)}, u32[]{:S(2)}) collective-permute-start(bf16[512,128]{1,0:T(8,128)(2,1)S(1)} %get-tuple-element.42), channel_id=1, source_target_pairs={{0,4},{4,0},{8,12},{12,8},{16,20},{20,16},{24,28},{28,24},{1,5},{5... | collective-permute-start | bytes 393224 | tf_op jit(solution)/shard_map/ppermute | solution.py:40
  40.9 0.7 %collective-permute-done.11.came_ref = bf16[1088,128]{1,0:T(8,128)(2,1)S(1)} collective-permute-done((bf16[1088,128]{1,0:T(8,128)(2,1)S(1)}, bf16[1088,128]{1,0:T(8,128)(2,1)S(1)}, u32[]{:S(2)}, u32[]{:S(2)}) %collective-permute-start.11) | collective-permute-done | bytes 278560 | tf_op jit(solution)/shard_map/ppermute | solution.py:40
  41.8 1.1 %collective-permute-start.13 = (bf16[384,128]{1,0:T(8,128)(2,1)S(1)}, bf16[384,128]{1,0:T(8,128)(2,1)S(1)}, u32[]{:S(2)}, u32[]{:S(2)}) collective-permute-start(bf16[384,128]{1,0:T(8,128)(2,1)S(1)} %get-tuple-element.52), channel_id=1, source_target_pairs={{0,16},{4,20},{8,24},{12,28},{16,0},{20,4},{24,8},{28,12},{1,17},{... | collective-permute-start | bytes 294920 | tf_op jit(solution)/shard_map/ppermute | solution.py:40
  42.8 3.3 %collective-permute-start.14 = (bf16[384,128]{1,0:T(8,128)(2,1)S(1)}, bf16[384,128]{1,0:T(8,128)(2,1)S(1)}, u32[]{:S(2)}, u32[]{:S(2)}) collective-permute-start(bf16[384,128]{1,0:T(8,128)(2,1)S(1)} %get-tuple-element.53), channel_id=1, source_target_pairs={{0,24},{4,28},{8,16},{12,20},{16,8},{20,12},{24,0},{28,4},{1,25},{... | collective-permute-start | bytes 294920 | tf_op jit(solution)/shard_map/ppermute | solution.py:40
  46.3 1.1 %collective-permute-start.8 = (bf16[128,128]{1,0:T(8,128)(2,1)S(1)}, bf16[128,128]{1,0:T(8,128)(2,1)S(1)}, u32[]{:S(2)}, u32[]{:S(2)}) collective-permute-start(bf16[128,128]{1,0:T(8,128)(2,1)S(1)} %get-tuple-element.45), channel_id=1, source_target_pairs={{0,16},{4,20},{8,24},{12,28},{16,0},{20,4},{24,8},{28,12},{1,17},{... | collective-permute-start | bytes 98312 | tf_op jit(solution)/shard_map/ppermute | solution.py:40
  47.3 0.9 %collective-permute-done.12.refs_1_.refs_5_ = bf16[384,128]{1,0:T(8,128)(2,1)S(1)} collective-permute-done((bf16[384,128]{1,0:T(8,128)(2,1)S(1)}, bf16[384,128]{1,0:T(8,128)(2,1)S(1)}, u32[]{:S(2)}, u32[]{:S(2)}) %collective-permute-start.12) | collective-permute-done | bytes 98336 | tf_op jit(solution)/shard_map/ppermute | solution.py:40
  48.2 2.4 %collective-permute-start.9 = (bf16[128,128]{1,0:T(8,128)(2,1)S(1)}, bf16[128,128]{1,0:T(8,128)(2,1)S(1)}, u32[]{:S(2)}, u32[]{:S(2)}) collective-permute-start(bf16[128,128]{1,0:T(8,128)(2,1)S(1)} %get-tuple-element.46), channel_id=1, source_target_pairs={{0,24},{4,28},{8,16},{12,20},{16,8},{20,12},{24,0},{28,4},{1,25},{... | collective-permute-start | bytes 98312 | tf_op jit(solution)/shard_map/ppermute | solution.py:40
  50.6 1.0 %collective-permute-done.13.refs_2_.refs_6_ = bf16[384,128]{1,0:T(8,128)(2,1)S(1)} collective-permute-done((bf16[384,128]{1,0:T(8,128)(2,1)S(1)}, bf16[384,128]{1,0:T(8,128)(2,1)S(1)}, u32[]{:S(2)}, u32[]{:S(2)}) %collective-permute-start.13) | collective-permute-done | bytes 98336 | tf_op jit(solution)/shard_map/ppermute | solution.py:40
  51.7 1.7 %collective-permute-done.8.refs_2_ = bf16[128,128]{1,0:T(8,128)(2,1)S(1)} collective-permute-done((bf16[128,128]{1,0:T(8,128)(2,1)S(1)}, bf16[128,128]{1,0:T(8,128)(2,1)S(1)}, u32[]{:S(2)}, u32[]{:S(2)}) %collective-permute-start.8) | collective-permute-done | bytes 32800 | tf_op jit(solution)/shard_map/ppermute | solution.py:40
  53.4 0.6 %collective-permute-done.9.refs_3_ = bf16[128,128]{1,0:T(8,128)(2,1)S(1)} collective-permute-done((bf16[128,128]{1,0:T(8,128)(2,1)S(1)}, bf16[128,128]{1,0:T(8,128)(2,1)S(1)}, u32[]{:S(2)}, u32[]{:S(2)}) %collective-permute-start.9) | collective-permute-done | bytes 32800 | tf_op jit(solution)/shard_map/ppermute | solution.py:40
  54.0 1.7 %collective-permute-start.15 = (bf16[384,128]{1,0:T(8,128)(2,1)S(1)}, bf16[384,128]{1,0:T(8,128)(2,1)S(1)}, u32[]{:S(2)}, u32[]{:S(2)}) collective-permute-start(bf16[384,128]{1,0:T(8,128)(2,1)S(1)} %shard_map.72.refs_0_), channel_id=1, source_target_pairs={{0,2},{1,3},{2,0},{3,1},{4,6},{5,7},{6,4},{7,5},{8,10},{9,11},{10,... | collective-permute-start | bytes 294920 | tf_op jit(solution)/shard_map/ppermute | solution.py:40
  55.8 2.9 %collective-permute-done.15.refs_1_ = bf16[384,128]{1,0:T(8,128)(2,1)S(1)} collective-permute-done((bf16[384,128]{1,0:T(8,128)(2,1)S(1)}, bf16[384,128]{1,0:T(8,128)(2,1)S(1)}, u32[]{:S(2)}, u32[]{:S(2)}) %collective-permute-start.15) | collective-permute-done | bytes 98336 | tf_op jit(solution)/shard_map/ppermute | solution.py:40
  58.8 1.2 %collective-permute-done.17.refs_3_ = bf16[384,128]{1,0:T(8,128)(2,1)S(1)} collective-permute-done((bf16[384,128]{1,0:T(8,128)(2,1)S(1)}, bf16[384,128]{1,0:T(8,128)(2,1)S(1)}, u32[]{:S(2)}, u32[]{:S(2)}) %collective-permute-start.17) | collective-permute-done | bytes 98336 | tf_op jit(solution)/shard_map/ppermute | solution.py:40
  60.0 1.8 %shard_map.73 = (f32[3,2,64,512]{3,2,1,0:T(8,128)}, f32[3,2,64,64]{3,2,1,0:T(8,128)}) custom-call(s32[2]{0:T(128)S(1)} %pad_add_fusion.refs_0_.here_ref, s32[3]{0:T(128)S(1)} %copy-done.1, bf16[384,128]{1,0:T(8,128)(2,1)S(1)} %shard_map.72.refs_0_, bf16[384,128]{1,0:T(8,128)(2,1)S(1)} %collective-permute-done.15.refs_1_, ...), custom_call_target="tpu_custom_call" | custom-call | flops 1 | bytes 1 | tf_op jit(solution)/shard_map/pallas_call | solution.py:420
  (33 shorter events, 0.9 us)
Async XLA Ops:
  0.6 1.4 %copy-start = (bf16[512,2,3,2,128]{4,3,2,1,0:T(2,128)(2,1)S(1)}, bf16[512,2,3,2,128]{4,3,2,1,0:T(2,128)(2,1)}, u32[]{:S(2)}) copy-start(bf16[512,2,3,2,128]{4,3,2,1,0:T(2,128)(2,1)} %param.4) | copy-start | bytes 4718596
  2.0 8.7 %copy-start.2 = (f32[3,2,3,3,2,128]{5,4,3,2,1,0:T(2,128)S(1)}, f32[3,2,3,3,2,128]{5,4,3,2,1,0:T(2,128)}, u32[]{:S(2)}) copy-start(f32[3,2,3,3,2,128]{5,4,3,2,1,0:T(2,128)} %param.5) | copy-start | bytes 165892
  2.5 22.9 %collective-permute-start.3 = (bf16[512,768]{1,0:T(8,128)(2,1)S(1)}, bf16[512,768]{1,0:T(8,128)(2,1)S(1)}, u32[]{:S(2)}, u32[]{:S(2)}) collective-permute-start(bf16[512,768]{1,0:T(8,128)(2,1)S(1)} %shard_map.59), channel_id=1, source_target_pairs={{0,28},{4,0},{8,4},{12,8},{16,12},{20,16},{24,20},{28,24},{1,29},{... | collective-permute-start | bytes 2359304 | tf_op jit(solution)/shard_map/ppermute | solution.py:35
  10.1 5.7 %collective-permute-start = (bf16[512,256]{1,0:T(8,128)(2,1)}, bf16[512,256]{1,0:T(8,128)(2,1)S(1)}, u32[]{:S(2)}, u32[]{:S(2)}) collective-permute-start(bf16[512,256]{1,0:T(8,128)(2,1)} %get-tuple-element.30), channel_id=1, source_target_pairs={{0,3},{1,0},{2,1},{3,2},{4,7},{5,4},{6,5},{7,6},{8,11},{9,8},{10,9... | collective-permute-start | bytes 786440 | tf_op jit(solution)/shard_map/ppermute | solution.py:35
  15.7 8.0 %collective-permute-start.2 = (bf16[2,4,128,128]{3,2,1,0:T(8,128)(2,1)S(1)}, bf16[2,4,128,128]{3,2,1,0:T(8,128)(2,1)S(1)}, u32[]{:S(2)}, u32[]{:S(2)}) collective-permute-start(bf16[2,4,128,128]{3,2,1,0:T(8,128)(2,1)S(1)} %get-tuple-element.34), channel_id=1, source_target_pairs={{0,1},{1,0},{2,3},{3,2},{4,5},{5,4},{6,7},{7,6},{8,9},{9,8},{10,11... | collective-permute-start | bytes 786440 | tf_op jit(solution)/shard_map/ppermute | solution.py:40
  20.6 3.1 %collective-permute-start.1 = (bf16[2,4,128,128]{3,2,1,0:T(8,128)(2,1)S(1)}, bf16[2,4,128,128]{3,2,1,0:T(8,128)(2,1)S(1)}, u32[]{:S(2)}, u32[]{:S(2)}) collective-permute-start(bf16[2,4,128,128]{3,2,1,0:T(8,128)(2,1)S(1)} %get-tuple-element.32), channel_id=1, source_target_pairs={{0,1},{1,0},{2,3},{3,2},{4,5},{5,4},{6,7},{7,6},{8,9},{9,8},{10,11... | collective-permute-start | bytes 786440 | tf_op jit(solution)/shard_map/ppermute | solution.py:40
  23.8 8.3 %collective-permute-start.10 = (bf16[2,1,4,128,128]{4,3,2,1,0:T(8,128)(2,1)S(1)}, bf16[2,1,4,128,128]{4,3,2,1,0:T(8,128)(2,1)S(1)}, u32[]{:S(2)}, u32[]{:S(2)}) collective-permute-start(bf16[2,1,4,128,128]{4,3,2,1,0:T(8,128)(2,1)S(1)} %get-tuple-element.47), channel_id=1, source_target_pairs={{0,2},{1,3},{2,0},{3,1},{4,6},{5,7},{6,4},{7,5},{8,10},{9,11},{10,... | collective-permute-start | bytes 786440 | tf_op jit(solution)/shard_map/ppermute | solution.py:40
  25.3 2.7 %copy-start.3 = (bf16[2,64,64]{2,1,0:T(8,128)(2,1)S(1)}, bf16[2,64,64]{2,1,0:T(8,128)(2,1)}, u32[]{:S(2)}) copy-start(bf16[2,64,64]{2,1,0:T(8,128)(2,1)} %param.7) | copy-start | bytes 49156
  27.9 5.1 %collective-permute-start.4 = (bf16[2,4,128,128]{3,2,1,0:T(8,128)(2,1)S(1)}, bf16[2,4,128,128]{3,2,1,0:T(8,128)(2,1)S(1)}, u32[]{:S(2)}, u32[]{:S(2)}) collective-permute-start(bf16[2,4,128,128]{3,2,1,0:T(8,128)(2,1)S(1)} %get-tuple-element.38), channel_id=1, source_target_pairs={{0,1},{1,0},{2,3},{3,2},{4,5},{5,4},{6,7},{7,6},{8,9},{9,8},{10,11... | collective-permute-start | bytes 786440 | tf_op jit(solution)/shard_map/ppermute | solution.py:40
  33.0 8.7 %collective-permute-start.11 = (bf16[1088,128]{1,0:T(8,128)(2,1)S(1)}, bf16[1088,128]{1,0:T(8,128)(2,1)S(1)}, u32[]{:S(2)}, u32[]{:S(2)}) collective-permute-start(bf16[1088,128]{1,0:T(8,128)(2,1)S(1)} %get-tuple-element.49), channel_id=1, source_target_pairs={{0,4},{4,0},{8,12},{12,8},{16,20},{20,16},{24,28},{28,24},{1,5},{5... | collective-permute-start | bytes 835592 | tf_op jit(solution)/shard_map/ppermute | solution.py:40
  33.0 27.0 %copy-start.1 = (s32[3]{0:T(128)S(1)}, s32[3]{0:T(128)}, u32[]{:S(2)}) copy-start(s32[3]{0:T(128)} %list_ref.1) | copy-start | bytes 40
  33.1 5.0 %collective-permute-start.5 = (bf16[1,1,4,128,128]{4,3,2,1,0:T(8,128)(2,1)S(1)}, bf16[1,1,4,128,128]{4,3,2,1,0:T(8,128)(2,1)S(1)}, u32[]{:S(2)}, u32[]{:S(2)}) collective-permute-start(bf16[1,1,4,128,128]{4,3,2,1,0:T(8,128)(2,1)S(1)} %get-tuple-element.40), channel_id=1, source_target_pairs={{0,2},{1,3},{2,0},{3,1},{4,6},{5,7},{6,4},{7,5},{8,10},{9,11},{10,... | collective-permute-start | bytes 393224 | tf_op jit(solution)/shard_map/ppermute | solution.py:40
  38.9 7.3 %collective-permute-start.6 = (bf16[512,128]{1,0:T(8,128)(2,1)S(1)}, bf16[512,128]{1,0:T(8,128)(2,1)S(1)}, u32[]{:S(2)}, u32[]{:S(2)}) collective-permute-start(bf16[512,128]{1,0:T(8,128)(2,1)S(1)} %get-tuple-element.42), channel_id=1, source_target_pairs={{0,4},{4,0},{8,12},{12,8},{16,20},{20,16},{24,28},{28,24},{1,5},{5... | collective-permute-start | bytes 393224 | tf_op jit(solution)/shard_map/ppermute | solution.py:40
  41.7 6.5 %collective-permute-start.12 = (bf16[384,128]{1,0:T(8,128)(2,1)S(1)}, bf16[384,128]{1,0:T(8,128)(2,1)S(1)}, u32[]{:S(2)}, u32[]{:S(2)}) collective-permute-start(bf16[384,128]{1,0:T(8,128)(2,1)S(1)} %get-tuple-element.51), channel_id=1, source_target_pairs={{0,8},{4,12},{8,0},{12,4},{16,24},{20,28},{24,16},{28,20},{1,9},{5... | collective-permute-start | bytes 294920 | tf_op jit(solution)/shard_map/ppermute | solution.py:40
  41.8 9.9 %collective-permute-start.13 = (bf16[384,128]{1,0:T(8,128)(2,1)S(1)}, bf16[384,128]{1,0:T(8,128)(2,1)S(1)}, u32[]{:S(2)}, u32[]{:S(2)}) collective-permute-start(bf16[384,128]{1,0:T(8,128)(2,1)S(1)} %get-tuple-element.52), channel_id=1, source_target_pairs={{0,16},{4,20},{8,24},{12,28},{16,0},{20,4},{24,8},{28,12},{1,17},{... | collective-permute-start | bytes 294920 | tf_op jit(solution)/shard_map/ppermute | solution.py:40
  42.8 8.8 %collective-permute-start.14 = (bf16[384,128]{1,0:T(8,128)(2,1)S(1)}, bf16[384,128]{1,0:T(8,128)(2,1)S(1)}, u32[]{:S(2)}, u32[]{:S(2)}) collective-permute-start(bf16[384,128]{1,0:T(8,128)(2,1)S(1)} %get-tuple-element.53), channel_id=1, source_target_pairs={{0,24},{4,28},{8,16},{12,20},{16,8},{20,12},{24,0},{28,4},{1,25},{... | collective-permute-start | bytes 294920 | tf_op jit(solution)/shard_map/ppermute | solution.py:40
  46.2 5.5 %collective-permute-start.7 = (bf16[128,128]{1,0:T(8,128)(2,1)S(1)}, bf16[128,128]{1,0:T(8,128)(2,1)S(1)}, u32[]{:S(2)}, u32[]{:S(2)}) collective-permute-start(bf16[128,128]{1,0:T(8,128)(2,1)S(1)} %get-tuple-element.44), channel_id=1, source_target_pairs={{0,8},{4,12},{8,0},{12,4},{16,24},{20,28},{24,16},{28,20},{1,9},{5... | collective-permute-start | bytes 98312 | tf_op jit(solution)/shard_map/ppermute | solution.py:40
  46.3 7.1 %collective-permute-start.8 = (bf16[128,128]{1,0:T(8,128)(2,1)S(1)}, bf16[128,128]{1,0:T(8,128)(2,1)S(1)}, u32[]{:S(2)}, u32[]{:S(2)}) collective-permute-start(bf16[128,128]{1,0:T(8,128)(2,1)S(1)} %get-tuple-element.45), channel_id=1, source_target_pairs={{0,16},{4,20},{8,24},{12,28},{16,0},{20,4},{24,8},{28,12},{1,17},{... | collective-permute-start | bytes 98312 | tf_op jit(solution)/shard_map/ppermute | solution.py:40
  48.2 5.8 %collective-permute-start.9 = (bf16[128,128]{1,0:T(8,128)(2,1)S(1)}, bf16[128,128]{1,0:T(8,128)(2,1)S(1)}, u32[]{:S(2)}, u32[]{:S(2)}) collective-permute-start(bf16[128,128]{1,0:T(8,128)(2,1)S(1)} %get-tuple-element.46), channel_id=1, source_target_pairs={{0,24},{4,28},{8,16},{12,20},{16,8},{20,12},{24,0},{28,4},{1,25},{... | collective-permute-start | bytes 98312 | tf_op jit(solution)/shard_map/ppermute | solution.py:40
  54.0 4.7 %collective-permute-start.15 = (bf16[384,128]{1,0:T(8,128)(2,1)S(1)}, bf16[384,128]{1,0:T(8,128)(2,1)S(1)}, u32[]{:S(2)}, u32[]{:S(2)}) collective-permute-start(bf16[384,128]{1,0:T(8,128)(2,1)S(1)} %shard_map.72.refs_0_), channel_id=1, source_target_pairs={{0,2},{1,3},{2,0},{3,1},{4,6},{5,7},{6,4},{7,5},{8,10},{9,11},{10,... | collective-permute-start | bytes 294920 | tf_op jit(solution)/shard_map/ppermute | solution.py:40
  55.8 3.0 %collective-permute-start.16 = (bf16[384,128]{1,0:T(8,128)(2,1)S(1)}, bf16[384,128]{1,0:T(8,128)(2,1)S(1)}, u32[]{:S(2)}, u32[]{:S(2)}) collective-permute-start(bf16[384,128]{1,0:T(8,128)(2,1)S(1)} %shard_map.72.refs_0_), channel_id=1, source_target_pairs={{0,1},{1,0},{2,3},{3,2},{4,5},{5,4},{6,7},{7,6},{8,9},{9,8},{10,11... | collective-permute-start | bytes 294920 | tf_op jit(solution)/shard_map/ppermute | solution.py:40
  58.7 1.3 %collective-permute-start.17 = (bf16[384,128]{1,0:T(8,128)(2,1)S(1)}, bf16[384,128]{1,0:T(8,128)(2,1)S(1)}, u32[]{:S(2)}, u32[]{:S(2)}) collective-permute-start(bf16[384,128]{1,0:T(8,128)(2,1)S(1)} %collective-permute-done.15.refs_1_), channel_id=1, source_target_pairs={{0,1},{1,0},{2,3},{3,2},{4,5},{5,4},{6,7},{7,6},{8,9},{9,8},{10,11... | collective-permute-start | bytes 294920 | tf_op jit(solution)/shard_map/ppermute | solution.py:40

commit v5 on v4

--- a/solution.py
+++ b/solution.py
@@ -15,7 +15,6 @@
 SHORT = jnp.bfloat16
 
 VMEM_SPEC = pl.BlockSpec(memory_space=pltpu.VMEM)
-SMEM_SPEC = pl.BlockSpec(memory_space=pltpu.SMEM)
 
 
 def call(kernel, out_shape, in_specs, scratch=()):
@@ -99,8 +98,8 @@
 
 
 def direction_kernel(direction, chosen, planes, norm, has_more, has_halo, *refs):
-    here_ref, links_ref, vec_ref = refs[:3]
-    rest = list(refs[3:])
+    links_ref, vec_ref = refs[:2]
+    rest = list(refs[2:])
     halo_ref = rest.pop(0) if has_halo else None
     more_ref = rest.pop(0) if has_more is True else None
     if has_more == "first":
@@ -163,7 +162,7 @@
 
         lax.fori_loop(0, count // group, step, 0, unroll=8)
 
-    here = here_ref[0]
+    here = lax.axis_index("narrow")
     pieces = packed.shape[0]
     size = packed.shape[2]
     tile = min(256, count)
@@ -208,7 +207,7 @@
             send_ref[piece] = packed[2 * piece + 1].astype(SHORT)
 
 
-def direction_part(direction, chosen, norm, pieces, here, links, vec, halo=None, more=None):
+def direction_part(direction, chosen, norm, pieces, links, vec, halo=None, more=None):
     planes = vec.shape[1] // (COMP * links.shape[1])
     count = vec.shape[0]
     size = count // pieces
@@ -222,7 +221,7 @@
     scratch = [pltpu.VMEM((count, depth), SHORT)] * 2
     if more != "first":
         scratch.append(pltpu.VMEM(whole.shape, FLOAT))
-    operands = [here, links, vec]
+    operands = [links, vec]
     if halo is not None:
         operands.append(halo)
     has_more = more if more == "first" else more is not None
@@ -233,7 +232,7 @@
             direction_kernel, direction, chosen, planes, norm, has_more, halo is not None
         ),
         out_shape,
-        [SMEM_SPEC] + [VMEM_SPEC] * (len(operands) - 1),
+        [VMEM_SPEC] * len(operands),
         scratch,
     )(*operands)
 
@@ -261,11 +260,11 @@
     )(*[x for pair in pairs for x in pair])
 
 
-def expand_kernel(has_extra, here_ref, keep_ref, came_ref, *refs):
+def expand_kernel(has_extra, keep_ref, came_ref, *refs):
     refs = list(refs)
     extra_ref = refs.pop(0) if has_extra else None
     own_ref, send_ref, sum_scr, rows_scr = refs
-    narrow, wide = here_ref[0], here_ref[1]
+    narrow, wide = lax.axis_index("narrow"), lax.axis_index("wide")
     kinds, _, pieces, size, _ = keep_ref.shape
     half, height, _ = own_ref.shape
     rows = height // (2 * kinds)
@@ -295,19 +294,19 @@
         send_ref[half * height :] = extra_ref[...]
 
 
-def expand(here, keep, came, wide_count, extra=None):
+def expand(keep, came, wide_count, extra=None):
     kinds, _, pieces, size, _ = keep.shape
     height = kinds * 2 * pieces * size // wide_count
     half = wide_count // 2
     more = 0 if extra is None else extra.shape[0]
-    operands = [here, keep, came] + ([] if extra is None else [extra])
+    operands = [keep, came] + ([] if extra is None else [extra])
     return call(
         functools.partial(expand_kernel, extra is not None),
         [
             jax.ShapeDtypeStruct((half, height, size), FLOAT),
             jax.ShapeDtypeStruct((half * height + more, size), SHORT),
         ],
-        [SMEM_SPEC] + [VMEM_SPEC] * (len(operands) - 1),
+        [VMEM_SPEC] * len(operands),
         [
             pltpu.VMEM((pieces, size, size), FLOAT),
             pltpu.VMEM((wide_count, height, size), FLOAT),
@@ -365,12 +364,12 @@
     )(*operands)
 
 
-def finish_kernel(order, here_ref, list_ref, *refs):
+def finish_kernel(order, list_ref, *refs):
     pieces = len(order)
     row_refs = refs[:pieces]
     pair_ref, last_refs = refs[pieces], refs[pieces + 1 : -5]
     elem_ref, prod_ref, rows_scr, left_scr, right_scr = refs[-5:]
-    narrow, wide = here_ref[0], here_ref[1]
+    narrow, wide = lax.axis_index("narrow"), lax.axis_index("wide")
     slots, _, rows, total = elem_ref.shape
     size = row_refs[0].shape[1]
     share = pair_ref.shape[0] // 2
@@ -379,18 +378,20 @@
     mine = wide * rows // size
     for position, ref in zip(order, row_refs):
         rows_scr[position] = ref[...].reshape(slots, 2 * rows, size)
-    for slot in range(slots):
-        kind = list_ref[slot]
-        for block in range(pieces):
-            piece = rows_scr[narrow ^ block ^ mine, kind]
-            at = slice(block * size, (block + 1) * size)
+    for block in range(pieces):
+        piece = rows_scr[narrow ^ block ^ mine].astype(FLOAT)
+        at = slice(block * size, (block + 1) * size)
+        for slot in range(slots):
+            chosen = piece[0]
+            for kind in range(1, slots):
+                chosen = jnp.where(list_ref[slot] == kind, piece[kind], chosen)
             for r in range(2):
-                part = piece[r * rows : (r + 1) * rows]
-                elem_ref[slot, r, :, at] = part.astype(FLOAT)
+                part = chosen[r * rows : (r + 1) * rows]
+                elem_ref[slot, r, :, at] = part
                 left_scr[
                     slot * rows : (slot + 1) * rows,
                     r * total + block * size : r * total + (block + 1) * size,
-                ] = part
+                ] = part.astype(SHORT)
     held = [pair_ref[...]]
     held += [ref[ref.shape[0] - 2 * share :, :] for ref in last_refs]
     for index, values in enumerate(held):
@@ -409,7 +410,7 @@
             ]
 
 
-def finish(here, directions, order, rows, pair, last):
+def finish(directions, order, rows, pair, last):
     pieces = len(rows)
     slots = directions.shape[0]
     height, size = rows[0].shape
@@ -423,13 +424,13 @@
             jax.ShapeDtypeStruct((slots, 2, row_count, total), FLOAT),
             jax.ShapeDtypeStruct((slots, 2, row_count, cols), FLOAT),
         ],
-        [SMEM_SPEC, SMEM_SPEC] + [VMEM_SPEC] * len(operands),
+        [VMEM_SPEC] * (1 + len(operands)),
         [
             pltpu.VMEM((pieces, slots, 2 * row_count, size), SHORT),
             pltpu.VMEM((slots * row_count, 2 * total), SHORT),
             pltpu.VMEM((2, total // share, share, 2 * cols), SHORT),
         ],
-    )(here, directions, *operands)
+    )(jnp.broadcast_to(directions[:, None, None], (slots, 1, size)), *operands)
 
 
 def on_device(vectors, links, directions, peram):
@@ -438,7 +439,6 @@
     wide_count = lax.axis_size("wide")
     narrow_count = lax.axis_size("narrow")
     norm = 1.0 / math.sqrt(12.0 * planes * wide_count * length * narrow_count)
-    here = jnp.stack([lax.axis_index("narrow"), lax.axis_index("wide")]).astype(jnp.int32)
     link_rows = links.reshape(-1, length)
     pair = jnp.concatenate([peram[0], peram[1]], 1)
 
@@ -447,7 +447,7 @@
     edge_halo = from_behind(edge, "narrow", -1)
     every = tuple(range(planes))
     part = functools.partial(
-        direction_part, norm=norm, pieces=narrow_count, here=here, links=link_rows, vec=vec
+        direction_part, norm=norm, pieces=narrow_count, links=link_rows, vec=vec
     )
 
     def over_narrow(parts, tie=None):
@@ -469,10 +469,10 @@
     second = part(1, every, halo=edge_halo)
     inner = part(0, every[:-1], more="first")
     keep, came, plane_halo = over_narrow([second, third], plane_halo)
-    early, near, far = over_wide(*expand(here, keep, came, wide_count, pair), pair)
+    early, near, far = over_wide(*expand(keep, came, wide_count, pair), pair)
     whole = part(0, every[-1:], halo=plane_halo, more=inner)
     keep, came, _ = over_narrow([whole])
-    late, _, rest = over_wide(*expand(here, keep, came, wide_count))
+    late, _, rest = over_wide(*expand(keep, came, wide_count))
     pairs = jnp.concatenate([pair, near[near.shape[0] - pair.shape[0] :]], 0)
 
     rows = [total(late, rest, total(early, far))]
@@ -480,7 +480,7 @@
     for stage in reversed(range(narrow_count.bit_length() - 1)):
         rows = rows + [swap(x, "narrow", 1 << stage) for x in rows]
         order = order + [o ^ (1 << stage) for o in order]
-    return tuple(finish(here, directions, order, rows, pairs, far))
+    return tuple(finish(directions, order, rows, pairs, far))
 
 
 def solution(mesh):

time: 61.9 us -> 60.5 us (0.977)
  Pallas kernels: 20.4 us -> 16.6 us
  starting transfers between devices: 21.9 us -> 23.3 us
  waiting for transfers between devices: 17 us -> 17.9 us
    pallas_call x4, Pallas kernels: 14.7 us -> 12.6 us  [direction_part(): call(functools.partial(direction_kernel, direction, chosen, planes, norm,...]
    ppermute x16, starting transfers between devices: 15.2 us -> 16.6 us  [swap(): return lax.ppermute(x, axis, [(i, i ^ mask) for i in range(length)])]
    pallas_call x2, Pallas kernels: 1.59 us -> 0.5 us  [expand(): call(functools.partial(expand_kernel, extra is not None), [jax.ShapeDtype...]
    ppermute x2, waiting for transfers between devices: 0.32 us -> 1.41 us  [from_behind(): lax.ppermute(x, axis, [(i, (i + by) % length) for i in range(length)])]
  transfers between devices with their start and end apart: 18 -> 18, of which waited for: 10 -> 8; matrix products, arithmetic and copies ran while one was open for 0% -> 0% of each run, Pallas kernels for 29% -> 25%
where the time goes in v5:
time: 60.5 us; the launch traced here: 60.4 us
  starting transfers between devices  23.3 us (39%)
  waiting for transfers between devices  17.9 us (30%)
  Pallas kernels  16.6 us (27%)
  local copies, waits for them, and re-layouts  1.53 us (3%)
  between operations  0.85 us (1%)
    ppermute x16, starting transfers between devices, swap(): return lax.ppermute(x, axis, [(i, i ^ mask) for i in range(length)])  16.6 us
    ppermute x16, waiting for transfers between devices, swap(): return lax.ppermute(x, axis, [(i, i ^ mask) for i in range(length)])  16.5 us
    pallas_call x4, Pallas kernels, direction_part(): call(functools.partial(direction_kernel, direction, chosen, planes, norm,...  12.6 us
    ppermute x2, starting transfers between devices, from_behind(): lax.ppermute(x, axis, [(i, (i + by) % length) for i in range(length)])  6.71 us
    pallas_call x2, Pallas kernels, by_rows(): pl.pallas_call(functools.partial(kernel, planes), grid=(count // block,),...  1.98 us
    unnamed x8, local copies, waits for them, and re-layouts  1.41 us
    ppermute x2, waiting for transfers between devices, from_behind(): lax.ppermute(x, axis, [(i, (i + by) % length) for i in range(length)])  1.41 us
    pallas_call x1, Pallas kernels, finish(): call(functools.partial(finish_kernel, order), [jax.ShapeDtypeStruct((slot...  1.3 us
  transfers between devices with their start and end apart: 18, of which 8 were waited for; matrix products, arithmetic and copies ran while one was open for 0% of the time, Pallas kernels for 25%

profile of v5, /device:TPU:0, one launch (start us, length us, event | category | flops | bytes accessed | tf_op | source)
XLA Modules:
  0.0 60.4 jit_solution(2946190656909860542)
XLA Ops:
  0.6 1.4 %copy-done = bf16[512,2,3,2,128]{4,3,2,1,0:T(2,128)(2,1)S(1)} copy-done((bf16[512,2,3,2,128]{4,3,2,1,0:T(2,128)(2,1)S(1)}, bf16[512,2,3,2,128]{4,3,2,1,0:T(2,128)(2,1)}, u32[]{:S(2)}) %copy-start) | copy-done | bytes 1572888
  2.0 0.4 shard_map.59
  2.5 6.1 %collective-permute-start.3 = (bf16[512,768]{1,0:T(8,128)(2,1)S(1)}, bf16[512,768]{1,0:T(8,128)(2,1)S(1)}, u32[]{:S(2)}, u32[]{:S(2)}) collective-permute-start(bf16[512,768]{1,0:T(8,128)(2,1)S(1)} %shard_map.59), channel_id=1, source_target_pairs={{0,28},{4,0},{8,4},{12,8},{16,12},{20,16},{24,20},{28,24},{1,29},{... | collective-permute-start | bytes 2359304 | tf_op jit(solution)/shard_map/ppermute | solution.py:34
  8.5 1.5 %shard_map.60 = (bf16[512,1536]{1,0:T(8,128)(2,1)S(1)}, bf16[512,256]{1,0:T(8,128)(2,1)}) custom-call(bf16[6144,128]{1,0:T(8,128)(2,1)S(1)} %bitcast.12), custom_call_target="tpu_custom_call" | custom-call | flops 1 | bytes 1 | tf_op jit(solution)/shard_map/pallas_call | solution.py:73
  10.1 0.7 %collective-permute-start = (bf16[512,256]{1,0:T(8,128)(2,1)}, bf16[512,256]{1,0:T(8,128)(2,1)S(1)}, u32[]{:S(2)}, u32[]{:S(2)}) collective-permute-start(bf16[512,256]{1,0:T(8,128)(2,1)} %get-tuple-element.30), channel_id=1, source_target_pairs={{0,3},{1,0},{2,1},{3,2},{4,7},{5,4},{6,5},{7,6},{8,11},{9,8},{10,9... | collective-permute-start | bytes 786440 | tf_op jit(solution)/shard_map/ppermute | solution.py:34
  10.8 4.3 %shard_map.62 = (f32[2,4,128,128]{3,2,1,0:T(8,128)S(1)}, bf16[2,4,128,128]{3,2,1,0:T(8,128)(2,1)S(1)}) custom-call(f32[108,128]{1,0:T(8,128)S(1)} %reshape.13.refs_0_, bf16[512,1536]{1,0:T(8,128)(2,1)S(1)} %get-tuple-element.29.refs_1_), custom_call_target="tpu_custom_call" | custom-call | flops 1 | bytes 1 | tf_op jit(solution)/shard_map/pallas_call | solution.py:230
  15.2 4.3 %shard_map.61 = (f32[2,4,128,128]{3,2,1,0:T(8,128)S(1)}, bf16[2,4,128,128]{3,2,1,0:T(8,128)(2,1)S(1)}) custom-call(f32[108,128]{1,0:T(8,128)S(1)} %reshape.13.refs_0_, bf16[512,1536]{1,0:T(8,128)(2,1)S(1)} %get-tuple-element.29.refs_1_, bf16[512,256]{1,0:T(8,128)(2,1)S(1)} %collective-permute-done.refs_2_), custom_call_target="tpu_custom_call" | custom-call | flops 1 | bytes 1 | tf_op jit(solution)/shard_map/pallas_call | solution.py:230
  19.5 1.1 %collective-permute-start.1 = (bf16[2,4,128,128]{3,2,1,0:T(8,128)(2,1)S(1)}, bf16[2,4,128,128]{3,2,1,0:T(8,128)(2,1)S(1)}, u32[]{:S(2)}, u32[]{:S(2)}) collective-permute-start(bf16[2,4,128,128]{3,2,1,0:T(8,128)(2,1)S(1)} %get-tuple-element.32), channel_id=1, source_target_pairs={{0,1},{1,0},{2,3},{3,2},{4,5},{5,4},{6,7},{7,6},{8,9},{9,8},{10,11... | collective-permute-start | bytes 786440 | tf_op jit(solution)/shard_map/ppermute | solution.py:39
  20.6 2.0 %shard_map.64.refs_3_ = f32[4,4,128,128]{3,2,1,0:T(8,128)S(1)} custom-call(f32[108,128]{1,0:T(8,128)S(1)} %reshape.13.refs_0_, bf16[512,1536]{1,0:T(8,128)(2,1)S(1)} %get-tuple-element.29.refs_1_), custom_call_target="tpu_custom_call" | custom-call | flops 1 | bytes 1 | tf_op jit(solution)/shard_map/pallas_call | solution.py:230
  22.6 0.1 shard_map.63
  22.7 1.2 %collective-permute-start.10 = (bf16[2,1,4,128,128]{4,3,2,1,0:T(8,128)(2,1)S(1)}, bf16[2,1,4,128,128]{4,3,2,1,0:T(8,128)(2,1)S(1)}, u32[]{:S(2)}, u32[]{:S(2)}) collective-permute-start(bf16[2,1,4,128,128]{4,3,2,1,0:T(8,128)(2,1)S(1)} %get-tuple-element.47), channel_id=1, source_target_pairs={{0,2},{1,3},{2,0},{3,1},{4,6},{5,7},{6,4},{7,5},{8,10},{9,11},{10,... | collective-permute-start | bytes 786440 | tf_op jit(solution)/shard_map/ppermute | solution.py:39
  23.9 1.4 %collective-permute-done.3.refs_2_ = bf16[512,768]{1,0:T(8,128)(2,1)S(1)} collective-permute-done((bf16[512,768]{1,0:T(8,128)(2,1)S(1)}, bf16[512,768]{1,0:T(8,128)(2,1)S(1)}, u32[]{:S(2)}, u32[]{:S(2)}) %collective-permute-start.3) | collective-permute-done | bytes 786464 | tf_op jit(solution)/shard_map/ppermute | solution.py:34
  25.3 2.0 %shard_map.65 = (f32[2,4,128,128]{3,2,1,0:T(8,128)S(1)}, bf16[2,4,128,128]{3,2,1,0:T(8,128)(2,1)S(1)}) custom-call(f32[108,128]{1,0:T(8,128)S(1)} %reshape.13.refs_0_, bf16[512,1536]{1,0:T(8,128)(2,1)S(1)} %get-tuple-element.29.refs_1_, bf16[512,768]{1,0:T(8,128)(2,1)S(1)} %collective-permute-done.3.refs_2_, f32[4,4,128,128]{3,2,1,0:T(8,128)S(1)} %shard_map.64.refs_3_), custom_call_target="tpu_custom_call" | custom-call | flops 1 | bytes 1 | tf_op jit(solution)/shard_map/pallas_call | solution.py:230
  27.5 0.1 pad_maximum_fusion.1.refs_0_
  27.6 3.4 %collective-permute-done.10.came_ref = bf16[2,1,4,128,128]{4,3,2,1,0:T(8,128)(2,1)S(1)} collective-permute-done((bf16[2,1,4,128,128]{4,3,2,1,0:T(8,128)(2,1)S(1)}, bf16[2,1,4,128,128]{4,3,2,1,0:T(8,128)(2,1)S(1)}, u32[]{:S(2)}, u32[]{:S(2)}) %collective-permute-start.10) | collective-permute-done | bytes 262176 | tf_op jit(solution)/shard_map/ppermute | solution.py:39
  31.0 0.3 shard_map.69
  31.5 1.3 %collective-permute-start.5 = (bf16[1,1,4,128,128]{4,3,2,1,0:T(8,128)(2,1)S(1)}, bf16[1,1,4,128,128]{4,3,2,1,0:T(8,128)(2,1)S(1)}, u32[]{:S(2)}, u32[]{:S(2)}) collective-permute-start(bf16[1,1,4,128,128]{4,3,2,1,0:T(8,128)(2,1)S(1)} %get-tuple-element.40), channel_id=1, source_target_pairs={{0,2},{1,3},{2,0},{3,1},{4,6},{5,7},{6,4},{7,5},{8,10},{9,11},{10,... | collective-permute-start | bytes 393224 | tf_op jit(solution)/shard_map/ppermute | solution.py:39
  32.7 3.8 %collective-permute-done.5.came_ref = bf16[1,1,4,128,128]{4,3,2,1,0:T(8,128)(2,1)S(1)} collective-permute-done((bf16[1,1,4,128,128]{4,3,2,1,0:T(8,128)(2,1)S(1)}, bf16[1,1,4,128,128]{4,3,2,1,0:T(8,128)(2,1)S(1)}, u32[]{:S(2)}, u32[]{:S(2)}) %collective-permute-start.5) | collective-permute-done | bytes 131104 | tf_op jit(solution)/shard_map/ppermute | solution.py:39
  36.5 0.2 shard_map.67
  36.7 2.1 %collective-permute-start.6 = (bf16[512,128]{1,0:T(8,128)(2,1)S(1)}, bf16[512,128]{1,0:T(8,128)(2,1)S(1)}, u32[]{:S(2)}, u32[]{:S(2)}) collective-permute-start(bf16[512,128]{1,0:T(8,128)(2,1)S(1)} %get-tuple-element.42), channel_id=1, source_target_pairs={{0,4},{4,0},{8,12},{12,8},{16,20},{20,16},{24,28},{28,24},{1,5},{5... | collective-permute-start | bytes 393224 | tf_op jit(solution)/shard_map/ppermute | solution.py:39
  38.8 1.7 %collective-permute-done.11.came_ref = bf16[1088,128]{1,0:T(8,128)(2,1)S(1)} collective-permute-done((bf16[1088,128]{1,0:T(8,128)(2,1)S(1)}, bf16[1088,128]{1,0:T(8,128)(2,1)S(1)}, u32[]{:S(2)}, u32[]{:S(2)}) %collective-permute-start.11) | collective-permute-done | bytes 278560 | tf_op jit(solution)/shard_map/ppermute | solution.py:39
  40.6 1.1 %collective-permute-start.13 = (bf16[384,128]{1,0:T(8,128)(2,1)S(1)}, bf16[384,128]{1,0:T(8,128)(2,1)S(1)}, u32[]{:S(2)}, u32[]{:S(2)}) collective-permute-start(bf16[384,128]{1,0:T(8,128)(2,1)S(1)} %get-tuple-element.52), channel_id=1, source_target_pairs={{0,16},{4,20},{8,24},{12,28},{16,0},{20,4},{24,8},{28,12},{1,17},{... | collective-permute-start | bytes 294920 | tf_op jit(solution)/shard_map/ppermute | solution.py:39
  41.7 3.3 %collective-permute-start.14 = (bf16[384,128]{1,0:T(8,128)(2,1)S(1)}, bf16[384,128]{1,0:T(8,128)(2,1)S(1)}, u32[]{:S(2)}, u32[]{:S(2)}) collective-permute-start(bf16[384,128]{1,0:T(8,128)(2,1)S(1)} %get-tuple-element.53), channel_id=1, source_target_pairs={{0,24},{4,28},{8,16},{12,20},{16,8},{20,12},{24,0},{28,4},{1,25},{... | collective-permute-start | bytes 294920 | tf_op jit(solution)/shard_map/ppermute | solution.py:39
  45.1 1.1 %collective-permute-start.8 = (bf16[128,128]{1,0:T(8,128)(2,1)S(1)}, bf16[128,128]{1,0:T(8,128)(2,1)S(1)}, u32[]{:S(2)}, u32[]{:S(2)}) collective-permute-start(bf16[128,128]{1,0:T(8,128)(2,1)S(1)} %get-tuple-element.45), channel_id=1, source_target_pairs={{0,16},{4,20},{8,24},{12,28},{16,0},{20,4},{24,8},{28,12},{1,17},{... | collective-permute-start | bytes 98312 | tf_op jit(solution)/shard_map/ppermute | solution.py:39
  46.2 3.3 %collective-permute-start.9 = (bf16[128,128]{1,0:T(8,128)(2,1)S(1)}, bf16[128,128]{1,0:T(8,128)(2,1)S(1)}, u32[]{:S(2)}, u32[]{:S(2)}) collective-permute-start(bf16[128,128]{1,0:T(8,128)(2,1)S(1)} %get-tuple-element.46), channel_id=1, source_target_pairs={{0,24},{4,28},{8,16},{12,20},{16,8},{20,12},{24,0},{28,4},{1,25},{... | collective-permute-start | bytes 98312 | tf_op jit(solution)/shard_map/ppermute | solution.py:39
  49.5 1.4 %collective-permute-done.13.refs_2_.refs_6_ = bf16[384,128]{1,0:T(8,128)(2,1)S(1)} collective-permute-done((bf16[384,128]{1,0:T(8,128)(2,1)S(1)}, bf16[384,128]{1,0:T(8,128)(2,1)S(1)}, u32[]{:S(2)}, u32[]{:S(2)}) %collective-permute-start.13) | collective-permute-done | bytes 98336 | tf_op jit(solution)/shard_map/ppermute | solution.py:39
  50.9 2.1 %collective-permute-done.8.refs_2_ = bf16[128,128]{1,0:T(8,128)(2,1)S(1)} collective-permute-done((bf16[128,128]{1,0:T(8,128)(2,1)S(1)}, bf16[128,128]{1,0:T(8,128)(2,1)S(1)}, u32[]{:S(2)}, u32[]{:S(2)}) %collective-permute-start.8) | collective-permute-done | bytes 32800 | tf_op jit(solution)/shard_map/ppermute | solution.py:39
  53.0 1.8 %collective-permute-start.15 = (bf16[384,128]{1,0:T(8,128)(2,1)S(1)}, bf16[384,128]{1,0:T(8,128)(2,1)S(1)}, u32[]{:S(2)}, u32[]{:S(2)}) collective-permute-start(bf16[384,128]{1,0:T(8,128)(2,1)S(1)} %shard_map.72.refs_0_), channel_id=1, source_target_pairs={{0,2},{1,3},{2,0},{3,1},{4,6},{5,7},{6,4},{7,5},{8,10},{9,11},{10,... | collective-permute-start | bytes 294920 | tf_op jit(solution)/shard_map/ppermute | solution.py:39
  54.8 2.9 %collective-permute-done.15.refs_1_ = bf16[384,128]{1,0:T(8,128)(2,1)S(1)} collective-permute-done((bf16[384,128]{1,0:T(8,128)(2,1)S(1)}, bf16[384,128]{1,0:T(8,128)(2,1)S(1)}, u32[]{:S(2)}, u32[]{:S(2)}) %collective-permute-start.15) | collective-permute-done | bytes 98336 | tf_op jit(solution)/shard_map/ppermute | solution.py:39
  57.7 0.1 pad_maximum_fusion.refs_4_
  57.8 1.2 %collective-permute-done.17.refs_3_ = bf16[384,128]{1,0:T(8,128)(2,1)S(1)} collective-permute-done((bf16[384,128]{1,0:T(8,128)(2,1)S(1)}, bf16[384,128]{1,0:T(8,128)(2,1)S(1)}, u32[]{:S(2)}, u32[]{:S(2)}) %collective-permute-start.17) | collective-permute-done | bytes 98336 | tf_op jit(solution)/shard_map/ppermute | solution.py:39
  59.1 1.3 %shard_map.73 = (f32[3,2,64,512]{3,2,1,0:T(8,128)}, f32[3,2,64,64]{3,2,1,0:T(8,128)}) custom-call(s32[3,1,128]{2,1,0:T(1,128)S(1)} %broadcast_in_dim.24.list_ref, bf16[384,128]{1,0:T(8,128)(2,1)S(1)} %shard_map.72.refs_0_, bf16[384,128]{1,0:T(8,128)(2,1)S(1)} %collective-permute-done.15.refs_1_, bf16[384,128]{1,0:T(8,128)(2,1)S(1)} %collective-permute-done.16.refs_2_, ...), custom_call_target="tpu_custom_call" | custom-call | flops 1 | bytes 1 | tf_op jit(solution)/shard_map/pallas_call | solution.py:421
  (33 shorter events, 0.7 us)
Async XLA Ops:
  0.6 1.4 %copy-start = (bf16[512,2,3,2,128]{4,3,2,1,0:T(2,128)(2,1)S(1)}, bf16[512,2,3,2,128]{4,3,2,1,0:T(2,128)(2,1)}, u32[]{:S(2)}) copy-start(bf16[512,2,3,2,128]{4,3,2,1,0:T(2,128)(2,1)} %param.4) | copy-start | bytes 4718596
  2.0 8.7 %copy-start.1 = (f32[3,2,3,3,2,128]{5,4,3,2,1,0:T(2,128)S(1)}, f32[3,2,3,3,2,128]{5,4,3,2,1,0:T(2,128)}, u32[]{:S(2)}) copy-start(f32[3,2,3,3,2,128]{5,4,3,2,1,0:T(2,128)} %param.5) | copy-start | bytes 165892
  2.5 22.9 %collective-permute-start.3 = (bf16[512,768]{1,0:T(8,128)(2,1)S(1)}, bf16[512,768]{1,0:T(8,128)(2,1)S(1)}, u32[]{:S(2)}, u32[]{:S(2)}) collective-permute-start(bf16[512,768]{1,0:T(8,128)(2,1)S(1)} %shard_map.59), channel_id=1, source_target_pairs={{0,28},{4,0},{8,4},{12,8},{16,12},{20,16},{24,20},{28,24},{1,29},{... | collective-permute-start | bytes 2359304 | tf_op jit(solution)/shard_map/ppermute | solution.py:34
  10.1 5.1 %collective-permute-start = (bf16[512,256]{1,0:T(8,128)(2,1)}, bf16[512,256]{1,0:T(8,128)(2,1)S(1)}, u32[]{:S(2)}, u32[]{:S(2)}) collective-permute-start(bf16[512,256]{1,0:T(8,128)(2,1)} %get-tuple-element.30), channel_id=1, source_target_pairs={{0,3},{1,0},{2,1},{3,2},{4,7},{5,4},{6,5},{7,6},{8,11},{9,8},{10,9... | collective-permute-start | bytes 786440 | tf_op jit(solution)/shard_map/ppermute | solution.py:34
  15.1 7.5 %collective-permute-start.2 = (bf16[2,4,128,128]{3,2,1,0:T(8,128)(2,1)S(1)}, bf16[2,4,128,128]{3,2,1,0:T(8,128)(2,1)S(1)}, u32[]{:S(2)}, u32[]{:S(2)}) collective-permute-start(bf16[2,4,128,128]{3,2,1,0:T(8,128)(2,1)S(1)} %get-tuple-element.34), channel_id=1, source_target_pairs={{0,1},{1,0},{2,3},{3,2},{4,5},{5,4},{6,7},{7,6},{8,9},{9,8},{10,11... | collective-permute-start | bytes 786440 | tf_op jit(solution)/shard_map/ppermute | solution.py:39
  19.5 3.1 %collective-permute-start.1 = (bf16[2,4,128,128]{3,2,1,0:T(8,128)(2,1)S(1)}, bf16[2,4,128,128]{3,2,1,0:T(8,128)(2,1)S(1)}, u32[]{:S(2)}, u32[]{:S(2)}) collective-permute-start(bf16[2,4,128,128]{3,2,1,0:T(8,128)(2,1)S(1)} %get-tuple-element.32), channel_id=1, source_target_pairs={{0,1},{1,0},{2,3},{3,2},{4,5},{5,4},{6,7},{7,6},{8,9},{9,8},{10,11... | collective-permute-start | bytes 786440 | tf_op jit(solution)/shard_map/ppermute | solution.py:39
  22.7 8.3 %collective-permute-start.10 = (bf16[2,1,4,128,128]{4,3,2,1,0:T(8,128)(2,1)S(1)}, bf16[2,1,4,128,128]{4,3,2,1,0:T(8,128)(2,1)S(1)}, u32[]{:S(2)}, u32[]{:S(2)}) collective-permute-start(bf16[2,1,4,128,128]{4,3,2,1,0:T(8,128)(2,1)S(1)} %get-tuple-element.47), channel_id=1, source_target_pairs={{0,2},{1,3},{2,0},{3,1},{4,6},{5,7},{6,4},{7,5},{8,10},{9,11},{10,... | collective-permute-start | bytes 786440 | tf_op jit(solution)/shard_map/ppermute | solution.py:39
  25.3 2.1 %copy-start.2 = (bf16[2,64,64]{2,1,0:T(8,128)(2,1)S(1)}, bf16[2,64,64]{2,1,0:T(8,128)(2,1)}, u32[]{:S(2)}) copy-start(bf16[2,64,64]{2,1,0:T(8,128)(2,1)} %param.7) | copy-start | bytes 49156
  27.4 4.0 %collective-permute-start.4 = (bf16[2,4,128,128]{3,2,1,0:T(8,128)(2,1)S(1)}, bf16[2,4,128,128]{3,2,1,0:T(8,128)(2,1)S(1)}, u32[]{:S(2)}, u32[]{:S(2)}) collective-permute-start(bf16[2,4,128,128]{3,2,1,0:T(8,128)(2,1)S(1)} %get-tuple-element.38), channel_id=1, source_target_pairs={{0,1},{1,0},{2,3},{3,2},{4,5},{5,4},{6,7},{7,6},{8,9},{9,8},{10,11... | collective-permute-start | bytes 786440 | tf_op jit(solution)/shard_map/ppermute | solution.py:39
  31.3 9.2 %collective-permute-start.11 = (bf16[1088,128]{1,0:T(8,128)(2,1)S(1)}, bf16[1088,128]{1,0:T(8,128)(2,1)S(1)}, u32[]{:S(2)}, u32[]{:S(2)}) collective-permute-start(bf16[1088,128]{1,0:T(8,128)(2,1)S(1)} %get-tuple-element.49), channel_id=1, source_target_pairs={{0,4},{4,0},{8,12},{12,8},{16,20},{20,16},{24,28},{28,24},{1,5},{5... | collective-permute-start | bytes 835592 | tf_op jit(solution)/shard_map/ppermute | solution.py:39
  31.4 27.6 %copy-start.3 = (s32[3]{0:T(128)S(1)}, s32[3]{0:T(128)}, u32[]{:S(2)}) copy-start(s32[3]{0:T(128)} %param.6) | copy-start | bytes 40
  31.5 5.0 %collective-permute-start.5 = (bf16[1,1,4,128,128]{4,3,2,1,0:T(8,128)(2,1)S(1)}, bf16[1,1,4,128,128]{4,3,2,1,0:T(8,128)(2,1)S(1)}, u32[]{:S(2)}, u32[]{:S(2)}) collective-permute-start(bf16[1,1,4,128,128]{4,3,2,1,0:T(8,128)(2,1)S(1)} %get-tuple-element.40), channel_id=1, source_target_pairs={{0,2},{1,3},{2,0},{3,1},{4,6},{5,7},{6,4},{7,5},{8,10},{9,11},{10,... | collective-permute-start | bytes 393224 | tf_op jit(solution)/shard_map/ppermute | solution.py:39
  36.7 8.3 %collective-permute-start.6 = (bf16[512,128]{1,0:T(8,128)(2,1)S(1)}, bf16[512,128]{1,0:T(8,128)(2,1)S(1)}, u32[]{:S(2)}, u32[]{:S(2)}) collective-permute-start(bf16[512,128]{1,0:T(8,128)(2,1)S(1)} %get-tuple-element.42), channel_id=1, source_target_pairs={{0,4},{4,0},{8,12},{12,8},{16,20},{20,16},{24,28},{28,24},{1,5},{5... | collective-permute-start | bytes 393224 | tf_op jit(solution)/shard_map/ppermute | solution.py:39
  40.5 5.6 %collective-permute-start.12 = (bf16[384,128]{1,0:T(8,128)(2,1)S(1)}, bf16[384,128]{1,0:T(8,128)(2,1)S(1)}, u32[]{:S(2)}, u32[]{:S(2)}) collective-permute-start(bf16[384,128]{1,0:T(8,128)(2,1)S(1)} %get-tuple-element.51), channel_id=1, source_target_pairs={{0,8},{4,12},{8,0},{12,4},{16,24},{20,28},{24,16},{28,20},{1,9},{5... | collective-permute-start | bytes 294920 | tf_op jit(solution)/shard_map/ppermute | solution.py:39
  40.6 10.3 %collective-permute-start.13 = (bf16[384,128]{1,0:T(8,128)(2,1)S(1)}, bf16[384,128]{1,0:T(8,128)(2,1)S(1)}, u32[]{:S(2)}, u32[]{:S(2)}) collective-permute-start(bf16[384,128]{1,0:T(8,128)(2,1)S(1)} %get-tuple-element.52), channel_id=1, source_target_pairs={{0,16},{4,20},{8,24},{12,28},{16,0},{20,4},{24,8},{28,12},{1,17},{... | collective-permute-start | bytes 294920 | tf_op jit(solution)/shard_map/ppermute | solution.py:39
  41.7 9.2 %collective-permute-start.14 = (bf16[384,128]{1,0:T(8,128)(2,1)S(1)}, bf16[384,128]{1,0:T(8,128)(2,1)S(1)}, u32[]{:S(2)}, u32[]{:S(2)}) collective-permute-start(bf16[384,128]{1,0:T(8,128)(2,1)S(1)} %get-tuple-element.53), channel_id=1, source_target_pairs={{0,24},{4,28},{8,16},{12,20},{16,8},{20,12},{24,0},{28,4},{1,25},{... | collective-permute-start | bytes 294920 | tf_op jit(solution)/shard_map/ppermute | solution.py:39
  45.0 5.9 %collective-permute-start.7 = (bf16[128,128]{1,0:T(8,128)(2,1)S(1)}, bf16[128,128]{1,0:T(8,128)(2,1)S(1)}, u32[]{:S(2)}, u32[]{:S(2)}) collective-permute-start(bf16[128,128]{1,0:T(8,128)(2,1)S(1)} %get-tuple-element.44), channel_id=1, source_target_pairs={{0,8},{4,12},{8,0},{12,4},{16,24},{20,28},{24,16},{28,20},{1,9},{5... | collective-permute-start | bytes 98312 | tf_op jit(solution)/shard_map/ppermute | solution.py:39
  45.1 7.9 %collective-permute-start.8 = (bf16[128,128]{1,0:T(8,128)(2,1)S(1)}, bf16[128,128]{1,0:T(8,128)(2,1)S(1)}, u32[]{:S(2)}, u32[]{:S(2)}) collective-permute-start(bf16[128,128]{1,0:T(8,128)(2,1)S(1)} %get-tuple-element.45), channel_id=1, source_target_pairs={{0,16},{4,20},{8,24},{12,28},{16,0},{20,4},{24,8},{28,12},{1,17},{... | collective-permute-start | bytes 98312 | tf_op jit(solution)/shard_map/ppermute | solution.py:39
  46.2 6.8 %collective-permute-start.9 = (bf16[128,128]{1,0:T(8,128)(2,1)S(1)}, bf16[128,128]{1,0:T(8,128)(2,1)S(1)}, u32[]{:S(2)}, u32[]{:S(2)}) collective-permute-start(bf16[128,128]{1,0:T(8,128)(2,1)S(1)} %get-tuple-element.46), channel_id=1, source_target_pairs={{0,24},{4,28},{8,16},{12,20},{16,8},{20,12},{24,0},{28,4},{1,25},{... | collective-permute-start | bytes 98312 | tf_op jit(solution)/shard_map/ppermute | solution.py:39
  53.0 4.7 %collective-permute-start.15 = (bf16[384,128]{1,0:T(8,128)(2,1)S(1)}, bf16[384,128]{1,0:T(8,128)(2,1)S(1)}, u32[]{:S(2)}, u32[]{:S(2)}) collective-permute-start(bf16[384,128]{1,0:T(8,128)(2,1)S(1)} %shard_map.72.refs_0_), channel_id=1, source_target_pairs={{0,2},{1,3},{2,0},{3,1},{4,6},{5,7},{6,4},{7,5},{8,10},{9,11},{10,... | collective-permute-start | bytes 294920 | tf_op jit(solution)/shard_map/ppermute | solution.py:39
  54.8 3.0 %collective-permute-start.16 = (bf16[384,128]{1,0:T(8,128)(2,1)S(1)}, bf16[384,128]{1,0:T(8,128)(2,1)S(1)}, u32[]{:S(2)}, u32[]{:S(2)}) collective-permute-start(bf16[384,128]{1,0:T(8,128)(2,1)S(1)} %shard_map.72.refs_0_), channel_id=1, source_target_pairs={{0,1},{1,0},{2,3},{3,2},{4,5},{5,4},{6,7},{7,6},{8,9},{9,8},{10,11... | collective-permute-start | bytes 294920 | tf_op jit(solution)/shard_map/ppermute | solution.py:39
  57.7 1.3 %collective-permute-start.17 = (bf16[384,128]{1,0:T(8,128)(2,1)S(1)}, bf16[384,128]{1,0:T(8,128)(2,1)S(1)}, u32[]{:S(2)}, u32[]{:S(2)}) collective-permute-start(bf16[384,128]{1,0:T(8,128)(2,1)S(1)} %collective-permute-done.15.refs_1_), channel_id=1, source_target_pairs={{0,1},{1,0},{2,3},{3,2},{4,5},{5,4},{6,7},{7,6},{8,9},{9,8},{10,11... | collective-permute-start | bytes 294920 | tf_op jit(solution)/shard_map/ppermute | solution.py:39

commit v6 on v5

--- a/solution.py
+++ b/solution.py
@@ -260,10 +260,7 @@
     )(*[x for pair in pairs for x in pair])
 
 
-def expand_kernel(has_extra, keep_ref, came_ref, *refs):
-    refs = list(refs)
-    extra_ref = refs.pop(0) if has_extra else None
-    own_ref, send_ref, sum_scr, rows_scr = refs
+def expand_kernel(keep_ref, came_ref, own_ref, send_ref, sum_scr, rows_scr):
     narrow, wide = lax.axis_index("narrow"), lax.axis_index("wide")
     kinds, _, pieces, size, _ = keep_ref.shape
     half, height, _ = own_ref.shape
@@ -290,28 +287,24 @@
         send_ref[index * height : (index + 1) * height] = rows_scr[wide ^ (2 * index + 1)].astype(
             SHORT
         )
-    if has_extra:
-        send_ref[half * height :] = extra_ref[...]
-
-
-def expand(keep, came, wide_count, extra=None):
+
+
+def expand(keep, came, wide_count):
     kinds, _, pieces, size, _ = keep.shape
     height = kinds * 2 * pieces * size // wide_count
     half = wide_count // 2
-    more = 0 if extra is None else extra.shape[0]
-    operands = [keep, came] + ([] if extra is None else [extra])
-    return call(
-        functools.partial(expand_kernel, extra is not None),
+    return call(
+        expand_kernel,
         [
             jax.ShapeDtypeStruct((half, height, size), FLOAT),
-            jax.ShapeDtypeStruct((half * height + more, size), SHORT),
+            jax.ShapeDtypeStruct((half * height, size), SHORT),
         ],
-        [VMEM_SPEC] * len(operands),
+        [VMEM_SPEC] * 2,
         [
             pltpu.VMEM((pieces, size, size), FLOAT),
             pltpu.VMEM((wide_count, height, size), FLOAT),
         ],
-    )(*operands)
+    )(keep, came)
 
 
 def spread_kernel(has_extra, own_ref, came_ref, *refs):
@@ -324,14 +317,12 @@
         came = came_ref[index * height : (index + 1) * height].astype(FLOAT)
         sends[index - 1][:height] = (own_ref[index] + came).astype(SHORT)
         if has_extra:
-            more = extra_ref.shape[0]
-            sends[index - 1][height : height + more] = extra_ref[...]
-            sends[index - 1][height + more :] = came_ref[half * height :]
+            sends[index - 1][height:] = extra_ref[...]
 
 
 def spread(own, came, extra=None):
     half, height, size = own.shape
-    more = 0 if extra is None else 2 * extra.shape[0]
+    more = 0 if extra is None else extra.shape[0]
     operands = [own, came] + ([] if extra is None else [extra])
     return call(
         functools.partial(spread_kernel, extra is not None),
@@ -367,13 +358,12 @@
 def finish_kernel(order, list_ref, *refs):
     pieces = len(order)
     row_refs = refs[:pieces]
-    pair_ref, last_refs = refs[pieces], refs[pieces + 1 : -5]
+    held_refs, other_ref = refs[pieces:-6], refs[-6]
     elem_ref, prod_ref, rows_scr, left_scr, right_scr = refs[-5:]
     narrow, wide = lax.axis_index("narrow"), lax.axis_index("wide")
     slots, _, rows, total = elem_ref.shape
     size = row_refs[0].shape[1]
-    share = pair_ref.shape[0] // 2
-    cols = pair_ref.shape[1] // 2
+    share, cols = right_scr.shape[2], right_scr.shape[3] // 2
     height = row_refs[0].shape[0]
     mine = wide * rows // size
     for position, ref in zip(order, row_refs):
@@ -384,7 +374,7 @@
         for slot in range(slots):
             chosen = piece[0]
             for kind in range(1, slots):
-                chosen = jnp.where(list_ref[slot] == kind, piece[kind], chosen)
+                chosen = jnp.where(list_ref[:, slot : slot + 1] == kind, piece[kind], chosen)
             for r in range(2):
                 part = chosen[r * rows : (r + 1) * rows]
                 elem_ref[slot, r, :, at] = part
@@ -392,15 +382,15 @@
                     slot * rows : (slot + 1) * rows,
                     r * total + block * size : r * total + (block + 1) * size,
                 ] = part.astype(SHORT)
-    held = [pair_ref[...]]
-    held += [ref[ref.shape[0] - 2 * share :, :] for ref in last_refs]
-    for index, values in enumerate(held):
+    for index, ref in enumerate(held_refs):
         for low in range(2):
-            block = values[low * share : (low + 1) * share]
-            turned = jnp.concatenate([-block[:, cols:], block[:, :cols]], 1)
+            if low == 0:
+                block = ref[ref.shape[0] - share :, :]
+            else:
+                block = other_ref[index * share : (index + 1) * share]
             owner = wide ^ (2 * index + low)
             right_scr[0, owner] = block
-            right_scr[1, owner] = turned
+            right_scr[1, owner] = jnp.concatenate([-block[:, cols:], block[:, :cols]], 1)
     right = right_scr[...].reshape(2 * total, 2 * cols)
     product = jnp.dot(left_scr[...], right, preferred_element_type=FLOAT)
     for slot in range(slots):
@@ -410,14 +400,14 @@
             ]
 
 
-def finish(directions, order, rows, pair, last):
+def finish(directions, order, rows, held, other):
     pieces = len(rows)
     slots = directions.shape[0]
     height, size = rows[0].shape
     row_count = height // (2 * slots)
-    share, cols = pair.shape[0] // 2, pair.shape[1] // 2
+    share, cols = held[0].shape[0], held[0].shape[1] // 2
     total = pieces * size
-    operands = [*rows, pair, *last]
+    operands = [*rows, *held, other]
     return call(
         functools.partial(finish_kernel, order),
         [
@@ -430,7 +420,7 @@
             pltpu.VMEM((slots * row_count, 2 * total), SHORT),
             pltpu.VMEM((2, total // share, share, 2 * cols), SHORT),
         ],
-    )(jnp.broadcast_to(directions[:, None, None], (slots, 1, size)), *operands)
+    )(directions[None], *operands)
 
 
 def on_device(vectors, links, directions, peram):
@@ -467,20 +457,25 @@
 
     third = part(2, every)
     second = part(1, every, halo=edge_halo)
-    inner = part(0, every[:-1], more="first")
     keep, came, plane_halo = over_narrow([second, third], plane_halo)
-    early, near, far = over_wide(*expand(keep, came, wide_count, pair), pair)
+    calm, _ = lax.optimization_barrier((vec, keep))
+    inner = part(0, every[:-1], more="first", vec=calm)
+    early, _, far = over_wide(*expand(keep, came, wide_count), pair)
     whole = part(0, every[-1:], halo=plane_halo, more=inner)
     keep, came, _ = over_narrow([whole])
     late, _, rest = over_wide(*expand(keep, came, wide_count))
-    pairs = jnp.concatenate([pair, near[near.shape[0] - pair.shape[0] :]], 0)
+    held = [pair] + [x[x.shape[0] - pair.shape[0] :] for x in far]
+    other = swap(jnp.concatenate(held, 0), "wide", 1)
 
     rows = [total(late, rest, total(early, far))]
     order = [0]
     for stage in reversed(range(narrow_count.bit_length() - 1)):
-        rows = rows + [swap(x, "narrow", 1 << stage) for x in rows]
+        came = [swap(x, "narrow", 1 << stage) for x in rows]
+        if stage > 0:
+            came, other = lax.optimization_barrier((came, other))
+        rows = rows + came
         order = order + [o ^ (1 << stage) for o in order]
-    return tuple(finish(directions, order, rows, pairs, far))
+    return tuple(finish(directions, order, rows, held, other))
 
 
 def solution(mesh):

time: 60.5 us -> 60.3 us (level)
  waiting for transfers between devices: 17.9 us -> 16.8 us
  starting transfers between devices: 23.3 us -> 24.3 us
    ppermute x2, waiting for transfers between devices: 1.41 us -> 0.24 us  [from_behind(): lax.ppermute(x, axis, [(i, (i + by) % length) for i in range(length)])]
    ppermute x16 -> x17, starting transfers between devices: 16.6 us -> 17.6 us  [swap(): return lax.ppermute(x, axis, [(i, i ^ mask) for i in range(length)])]
    ppermute x16 -> x17, waiting for transfers between devices: 16.5 us -> 16.6 us  [swap(): return lax.ppermute(x, axis, [(i, i ^ mask) for i in range(length)])]
  transfers between devices with their start and end apart: 18 -> 19, of which waited for: 8 -> 11; matrix products, arithmetic and copies ran while one was open for 0% -> 0% of each run, Pallas kernels for 25% -> 25%
where the time goes in v6:
time: 60.3 us; the launch traced here: 60.2 us
  starting transfers between devices  24.3 us (40%)
  waiting for transfers between devices  16.8 us (28%)
  Pallas kernels  16.6 us (28%)
  local copies, waits for them, and re-layouts  1.47 us (2%)
  between operations  0.84 us (1%)
    ppermute x17, starting transfers between devices, swap(): return lax.ppermute(x, axis, [(i, i ^ mask) for i in range(length)])  17.6 us
    ppermute x17, waiting for transfers between devices, swap(): return lax.ppermute(x, axis, [(i, i ^ mask) for i in range(length)])  16.6 us
    pallas_call x4, Pallas kernels, direction_part(): call(functools.partial(direction_kernel, direction, chosen, planes, norm,...  12.6 us
    ppermute x2, starting transfers between devices, from_behind(): lax.ppermute(x, axis, [(i, (i + by) % length) for i in range(length)])  6.71 us
    pallas_call x2, Pallas kernels, by_rows(): pl.pallas_call(functools.partial(kernel, planes), grid=(count // block,),...  1.98 us
    unnamed x8, local copies, waits for them, and re-layouts  1.42 us
    pallas_call x1, Pallas kernels, finish(): call(functools.partial(finish_kernel, order), [jax.ShapeDtypeStruct((slot...  1.27 us
  transfers between devices with their start and end apart: 19, of which 11 were waited for; matrix products, arithmetic and copies ran while one was open for 0% of the time, Pallas kernels for 25%

profile of v6, /device:TPU:0, one launch (start us, length us, event | category | flops | bytes accessed | tf_op | source)
XLA Modules:
  0.0 60.2 jit_solution(16506061896253717524)
XLA Ops:
  0.6 1.4 %copy-done = bf16[512,2,3,2,128]{4,3,2,1,0:T(2,128)(2,1)S(1)} copy-done((bf16[512,2,3,2,128]{4,3,2,1,0:T(2,128)(2,1)S(1)}, bf16[512,2,3,2,128]{4,3,2,1,0:T(2,128)(2,1)}, u32[]{:S(2)}) %copy-start) | copy-done | bytes 1572888
  2.0 0.4 shard_map.59
  2.5 6.1 %collective-permute-start.3 = (bf16[512,768]{1,0:T(8,128)(2,1)S(1)}, bf16[512,768]{1,0:T(8,128)(2,1)S(1)}, u32[]{:S(2)}, u32[]{:S(2)}) collective-permute-start(bf16[512,768]{1,0:T(8,128)(2,1)S(1)} %shard_map.59), channel_id=1, source_target_pairs={{0,28},{4,0},{8,4},{12,8},{16,12},{20,16},{24,20},{28,24},{1,29},{... | collective-permute-start | bytes 2359304 | tf_op jit(solution)/shard_map/ppermute | solution.py:34
  8.5 1.5 %shard_map.60 = (bf16[512,1536]{1,0:T(8,128)(2,1)S(1)}, bf16[512,256]{1,0:T(8,128)(2,1)}) custom-call(bf16[6144,128]{1,0:T(8,128)(2,1)S(1)} %bitcast.13), custom_call_target="tpu_custom_call" | custom-call | flops 1 | bytes 1 | tf_op jit(solution)/shard_map/pallas_call | solution.py:73
  10.1 0.7 %collective-permute-start = (bf16[512,256]{1,0:T(8,128)(2,1)}, bf16[512,256]{1,0:T(8,128)(2,1)S(1)}, u32[]{:S(2)}, u32[]{:S(2)}) collective-permute-start(bf16[512,256]{1,0:T(8,128)(2,1)} %get-tuple-element.33), channel_id=1, source_target_pairs={{0,3},{1,0},{2,1},{3,2},{4,7},{5,4},{6,5},{7,6},{8,11},{9,8},{10,9... | collective-permute-start | bytes 786440 | tf_op jit(solution)/shard_map/ppermute | solution.py:34
  10.8 4.3 %shard_map.62 = (f32[2,4,128,128]{3,2,1,0:T(8,128)S(1)}, bf16[2,4,128,128]{3,2,1,0:T(8,128)(2,1)S(1)}) custom-call(f32[108,128]{1,0:T(8,128)S(1)} %reshape.10.refs_0_, bf16[512,1536]{1,0:T(8,128)(2,1)S(1)} %get-tuple-element.40.refs_1_), custom_call_target="tpu_custom_call" | custom-call | flops 1 | bytes 1 | tf_op jit(solution)/shard_map/pallas_call | solution.py:230
  15.2 4.3 %shard_map.61 = (f32[2,4,128,128]{3,2,1,0:T(8,128)S(1)}, bf16[2,4,128,128]{3,2,1,0:T(8,128)(2,1)S(1)}) custom-call(f32[108,128]{1,0:T(8,128)S(1)} %reshape.10.refs_0_, bf16[512,1536]{1,0:T(8,128)(2,1)S(1)} %get-tuple-element.40.refs_1_, bf16[512,256]{1,0:T(8,128)(2,1)S(1)} %collective-permute-done.refs_2_), custom_call_target="tpu_custom_call" | custom-call | flops 1 | bytes 1 | tf_op jit(solution)/shard_map/pallas_call | solution.py:230
  19.5 1.1 %collective-permute-start.1 = (bf16[2,4,128,128]{3,2,1,0:T(8,128)(2,1)S(1)}, bf16[2,4,128,128]{3,2,1,0:T(8,128)(2,1)S(1)}, u32[]{:S(2)}, u32[]{:S(2)}) collective-permute-start(bf16[2,4,128,128]{3,2,1,0:T(8,128)(2,1)S(1)} %get-tuple-element.35), channel_id=1, source_target_pairs={{0,1},{1,0},{2,3},{3,2},{4,5},{5,4},{6,7},{7,6},{8,9},{9,8},{10,11... | collective-permute-start | bytes 786440 | tf_op jit(solution)/shard_map/ppermute | solution.py:39
  20.6 1.2 %collective-permute-done.1 = bf16[2,4,128,128]{3,2,1,0:T(8,128)(2,1)S(1)} collective-permute-done((bf16[2,4,128,128]{3,2,1,0:T(8,128)(2,1)S(1)}, bf16[2,4,128,128]{3,2,1,0:T(8,128)(2,1)S(1)}, u32[]{:S(2)}, u32[]{:S(2)}) %collective-permute-start.1) | collective-permute-done | bytes 262176 | tf_op jit(solution)/shard_map/ppermute | solution.py:39
  21.9 1.3 %collective-permute-start.10 = (bf16[2,1,4,128,128]{4,3,2,1,0:T(8,128)(2,1)S(1)}, bf16[2,1,4,128,128]{4,3,2,1,0:T(8,128)(2,1)S(1)}, u32[]{:S(2)}, u32[]{:S(2)}) collective-permute-start(bf16[2,1,4,128,128]{4,3,2,1,0:T(8,128)(2,1)S(1)} %get-tuple-element.51), channel_id=1, source_target_pairs={{0,2},{1,3},{2,0},{3,1},{4,6},{5,7},{6,4},{7,5},{8,10},{9,11},{10,... | collective-permute-start | bytes 786440 | tf_op jit(solution)/shard_map/ppermute | solution.py:39
  23.1 2.0 %shard_map.64.refs_3_ = f32[4,4,128,128]{3,2,1,0:T(8,128)S(1)} custom-call(f32[108,128]{1,0:T(8,128)S(1)} %reshape.10.refs_0_, bf16[512,1536]{1,0:T(8,128)(2,1)S(1)} %get-tuple-element.40.refs_1_), custom_call_target="tpu_custom_call" | custom-call | flops 1 | bytes 1 | tf_op jit(solution)/shard_map/pallas_call | solution.py:230
  25.1 0.2 collective-permute-done.3.refs_2_
  25.3 2.0 %shard_map.65 = (f32[2,4,128,128]{3,2,1,0:T(8,128)S(1)}, bf16[2,4,128,128]{3,2,1,0:T(8,128)(2,1)S(1)}) custom-call(f32[108,128]{1,0:T(8,128)S(1)} %reshape.10.refs_0_, bf16[512,1536]{1,0:T(8,128)(2,1)S(1)} %get-tuple-element.40.refs_1_, bf16[512,768]{1,0:T(8,128)(2,1)S(1)} %collective-permute-done.3.refs_2_, f32[4,4,128,128]{3,2,1,0:T(8,128)S(1)} %shard_map.64.refs_3_), custom_call_target="tpu_custom_call" | custom-call | flops 1 | bytes 1 | tf_op jit(solution)/shard_map/pallas_call | solution.py:230
  27.5 3.0 %collective-permute-done.10.came_ref = bf16[2,1,4,128,128]{4,3,2,1,0:T(8,128)(2,1)S(1)} collective-permute-done((bf16[2,1,4,128,128]{4,3,2,1,0:T(8,128)(2,1)S(1)}, bf16[2,1,4,128,128]{4,3,2,1,0:T(8,128)(2,1)S(1)}, u32[]{:S(2)}, u32[]{:S(2)}) %collective-permute-start.10) | collective-permute-done | bytes 262176 | tf_op jit(solution)/shard_map/ppermute | solution.py:39
  30.5 0.3 shard_map.69
  31.0 1.3 %collective-permute-start.5 = (bf16[1,1,4,128,128]{4,3,2,1,0:T(8,128)(2,1)S(1)}, bf16[1,1,4,128,128]{4,3,2,1,0:T(8,128)(2,1)S(1)}, u32[]{:S(2)}, u32[]{:S(2)}) collective-permute-start(bf16[1,1,4,128,128]{4,3,2,1,0:T(8,128)(2,1)S(1)} %get-tuple-element.44), channel_id=1, source_target_pairs={{0,2},{1,3},{2,0},{3,1},{4,6},{5,7},{6,4},{7,5},{8,10},{9,11},{10,... | collective-permute-start | bytes 393224 | tf_op jit(solution)/shard_map/ppermute | solution.py:39
  32.3 3.8 %collective-permute-done.5.came_ref = bf16[1,1,4,128,128]{4,3,2,1,0:T(8,128)(2,1)S(1)} collective-permute-done((bf16[1,1,4,128,128]{4,3,2,1,0:T(8,128)(2,1)S(1)}, bf16[1,1,4,128,128]{4,3,2,1,0:T(8,128)(2,1)S(1)}, u32[]{:S(2)}, u32[]{:S(2)}) %collective-permute-start.5) | collective-permute-done | bytes 131104 | tf_op jit(solution)/shard_map/ppermute | solution.py:39
  36.0 0.2 shard_map.67
  36.2 2.1 %collective-permute-start.6 = (bf16[512,128]{1,0:T(8,128)(2,1)S(1)}, bf16[512,128]{1,0:T(8,128)(2,1)S(1)}, u32[]{:S(2)}, u32[]{:S(2)}) collective-permute-start(bf16[512,128]{1,0:T(8,128)(2,1)S(1)} %get-tuple-element.46), channel_id=1, source_target_pairs={{0,4},{4,0},{8,12},{12,8},{16,20},{20,16},{24,28},{28,24},{1,5},{5... | collective-permute-start | bytes 393224 | tf_op jit(solution)/shard_map/ppermute | solution.py:39
  38.4 1.3 %collective-permute-done.11.came_ref = bf16[1024,128]{1,0:T(8,128)(2,1)S(1)} collective-permute-done((bf16[1024,128]{1,0:T(8,128)(2,1)S(1)}, bf16[1024,128]{1,0:T(8,128)(2,1)S(1)}, u32[]{:S(2)}, u32[]{:S(2)}) %collective-permute-start.11) | collective-permute-done | bytes 262176 | tf_op jit(solution)/shard_map/ppermute | solution.py:39
  39.8 1.6 %collective-permute-start.13 = (bf16[320,128]{1,0:T(8,128)(2,1)S(1)}, bf16[320,128]{1,0:T(8,128)(2,1)S(1)}, u32[]{:S(2)}, u32[]{:S(2)}) collective-permute-start(bf16[320,128]{1,0:T(8,128)(2,1)S(1)} %get-tuple-element.56), channel_id=1, source_target_pairs={{0,16},{4,20},{8,24},{12,28},{16,0},{20,4},{24,8},{28,12},{1,17},{... | collective-permute-start | bytes 245768 | tf_op jit(solution)/shard_map/ppermute | solution.py:39
  41.5 2.7 %collective-permute-start.14 = (bf16[320,128]{1,0:T(8,128)(2,1)S(1)}, bf16[320,128]{1,0:T(8,128)(2,1)S(1)}, u32[]{:S(2)}, u32[]{:S(2)}) collective-permute-start(bf16[320,128]{1,0:T(8,128)(2,1)S(1)} %get-tuple-element.57), channel_id=1, source_target_pairs={{0,24},{4,28},{8,16},{12,20},{16,8},{20,12},{24,0},{28,4},{1,25},{... | collective-permute-start | bytes 245768 | tf_op jit(solution)/shard_map/ppermute | solution.py:39
  44.3 1.6 %collective-permute-start.8 = (bf16[128,128]{1,0:T(8,128)(2,1)S(1)}, bf16[128,128]{1,0:T(8,128)(2,1)S(1)}, u32[]{:S(2)}, u32[]{:S(2)}) collective-permute-start(bf16[128,128]{1,0:T(8,128)(2,1)S(1)} %get-tuple-element.49), channel_id=1, source_target_pairs={{0,16},{4,20},{8,24},{12,28},{16,0},{20,4},{24,8},{28,12},{1,17},{... | collective-permute-start | bytes 98312 | tf_op jit(solution)/shard_map/ppermute | solution.py:39
  46.1 2.6 %collective-permute-start.9 = (bf16[128,128]{1,0:T(8,128)(2,1)S(1)}, bf16[128,128]{1,0:T(8,128)(2,1)S(1)}, u32[]{:S(2)}, u32[]{:S(2)}) collective-permute-start(bf16[128,128]{1,0:T(8,128)(2,1)S(1)} %get-tuple-element.50), channel_id=1, source_target_pairs={{0,24},{4,28},{8,16},{12,20},{16,8},{20,12},{24,0},{28,4},{1,25},{... | collective-permute-start | bytes 98312 | tf_op jit(solution)/shard_map/ppermute | solution.py:39
  48.8 0.6 %collective-permute-done.7.refs_1_ = bf16[128,128]{1,0:T(8,128)(2,1)S(1)} collective-permute-done((bf16[128,128]{1,0:T(8,128)(2,1)S(1)}, bf16[128,128]{1,0:T(8,128)(2,1)S(1)}, u32[]{:S(2)}, u32[]{:S(2)}) %collective-permute-start.7) | collective-permute-done | bytes 32800 | tf_op jit(solution)/shard_map/ppermute | solution.py:39
  49.4 1.6 %collective-permute-done.8.refs_2_ = bf16[128,128]{1,0:T(8,128)(2,1)S(1)} collective-permute-done((bf16[128,128]{1,0:T(8,128)(2,1)S(1)}, bf16[128,128]{1,0:T(8,128)(2,1)S(1)}, u32[]{:S(2)}, u32[]{:S(2)}) %collective-permute-start.8) | collective-permute-done | bytes 32800 | tf_op jit(solution)/shard_map/ppermute | solution.py:39
  50.9 0.9 %collective-permute-done.9.refs_3_ = bf16[128,128]{1,0:T(8,128)(2,1)S(1)} collective-permute-done((bf16[128,128]{1,0:T(8,128)(2,1)S(1)}, bf16[128,128]{1,0:T(8,128)(2,1)S(1)}, u32[]{:S(2)}, u32[]{:S(2)}) %collective-permute-start.9) | collective-permute-done | bytes 32800 | tf_op jit(solution)/shard_map/ppermute | solution.py:39
  51.9 1.4 %collective-permute-start.15 = (bf16[384,128]{1,0:T(8,128)(2,1)S(1)}, bf16[384,128]{1,0:T(8,128)(2,1)S(1)}, u32[]{:S(2)}, u32[]{:S(2)}) collective-permute-start(bf16[384,128]{1,0:T(8,128)(2,1)S(1)} %shard_map.72.refs_0_), channel_id=1, source_target_pairs={{0,2},{1,3},{2,0},{3,1},{4,6},{5,7},{6,4},{7,5},{8,10},{9,11},{10,... | collective-permute-start | bytes 294920 | tf_op jit(solution)/shard_map/ppermute | solution.py:39
  53.3 1.6 %collective-permute-start.16 = (bf16[256,128]{1,0:T(8,128)(2,1)S(1)}, bf16[256,128]{1,0:T(8,128)(2,1)S(1)}, u32[]{:S(2)}, u32[]{:S(2)}) collective-permute-start(bf16[256,128]{1,0:T(8,128)(2,1)S(1)} %pad_maximum_fusion), channel_id=1, source_target_pairs={{0,4},{4,0},{8,12},{12,8},{16,20},{20,16},{24,28},{28,24},{1,5},{5... | collective-permute-start | bytes 196616 | tf_op jit(solution)/shard_map/ppermute | solution.py:39
  54.9 2.7 %collective-permute-done.16.refs_8_ = bf16[256,128]{1,0:T(8,128)(2,1)S(1)} collective-permute-done((bf16[256,128]{1,0:T(8,128)(2,1)S(1)}, bf16[256,128]{1,0:T(8,128)(2,1)S(1)}, u32[]{:S(2)}, u32[]{:S(2)}) %collective-permute-start.16) | collective-permute-done | bytes 65568 | tf_op jit(solution)/shard_map/ppermute | solution.py:39
  57.6 1.3 %collective-permute-done.18.refs_3_ = bf16[384,128]{1,0:T(8,128)(2,1)S(1)} collective-permute-done((bf16[384,128]{1,0:T(8,128)(2,1)S(1)}, bf16[384,128]{1,0:T(8,128)(2,1)S(1)}, u32[]{:S(2)}, u32[]{:S(2)}) %collective-permute-start.18) | collective-permute-done | bytes 98336 | tf_op jit(solution)/shard_map/ppermute | solution.py:39
  58.9 1.3 %shard_map.73 = (f32[3,2,64,512]{3,2,1,0:T(8,128)}, f32[3,2,64,64]{3,2,1,0:T(8,128)}) custom-call(s32[1,3]{1,0:T(1,128)S(1)} %bitcast.20, bf16[384,128]{1,0:T(8,128)(2,1)S(1)} %shard_map.72.refs_0_, bf16[384,128]{1,0:T(8,128)(2,1)S(1)} %collective-permute-done.15.refs_1_, bf16[384,128]{1,0:T(8,128)(2,1)S(1)} %collective-permute-done.17.refs_2_, ...), custom_call_target="tpu_custom_call" | custom-call | flops 1 | bytes 1 | tf_op jit(solution)/shard_map/pallas_call | solution.py:411
  (36 shorter events, 1.1 us)
Async XLA Ops:
  0.6 1.4 %copy-start = (bf16[512,2,3,2,128]{4,3,2,1,0:T(2,128)(2,1)S(1)}, bf16[512,2,3,2,128]{4,3,2,1,0:T(2,128)(2,1)}, u32[]{:S(2)}) copy-start(bf16[512,2,3,2,128]{4,3,2,1,0:T(2,128)(2,1)} %param.4) | copy-start | bytes 4718596
  2.0 8.7 %copy-start.2 = (f32[3,2,3,3,2,128]{5,4,3,2,1,0:T(2,128)S(1)}, f32[3,2,3,3,2,128]{5,4,3,2,1,0:T(2,128)}, u32[]{:S(2)}) copy-start(f32[3,2,3,3,2,128]{5,4,3,2,1,0:T(2,128)} %param.5) | copy-start | bytes 165892
  2.5 22.9 %collective-permute-start.3 = (bf16[512,768]{1,0:T(8,128)(2,1)S(1)}, bf16[512,768]{1,0:T(8,128)(2,1)S(1)}, u32[]{:S(2)}, u32[]{:S(2)}) collective-permute-start(bf16[512,768]{1,0:T(8,128)(2,1)S(1)} %shard_map.59), channel_id=1, source_target_pairs={{0,28},{4,0},{8,4},{12,8},{16,12},{20,16},{24,20},{28,24},{1,29},{... | collective-permute-start | bytes 2359304 | tf_op jit(solution)/shard_map/ppermute | solution.py:34
  10.1 5.1 %collective-permute-start = (bf16[512,256]{1,0:T(8,128)(2,1)}, bf16[512,256]{1,0:T(8,128)(2,1)S(1)}, u32[]{:S(2)}, u32[]{:S(2)}) collective-permute-start(bf16[512,256]{1,0:T(8,128)(2,1)} %get-tuple-element.33), channel_id=1, source_target_pairs={{0,3},{1,0},{2,1},{3,2},{4,7},{5,4},{6,5},{7,6},{8,11},{9,8},{10,9... | collective-permute-start | bytes 786440 | tf_op jit(solution)/shard_map/ppermute | solution.py:34
  15.1 5.5 %collective-permute-start.2 = (bf16[2,4,128,128]{3,2,1,0:T(8,128)(2,1)S(1)}, bf16[2,4,128,128]{3,2,1,0:T(8,128)(2,1)S(1)}, u32[]{:S(2)}, u32[]{:S(2)}) collective-permute-start(bf16[2,4,128,128]{3,2,1,0:T(8,128)(2,1)S(1)} %get-tuple-element.37), channel_id=1, source_target_pairs={{0,1},{1,0},{2,3},{3,2},{4,5},{5,4},{6,7},{7,6},{8,9},{9,8},{10,11... | collective-permute-start | bytes 786440 | tf_op jit(solution)/shard_map/ppermute | solution.py:39
  19.5 2.3 %collective-permute-start.1 = (bf16[2,4,128,128]{3,2,1,0:T(8,128)(2,1)S(1)}, bf16[2,4,128,128]{3,2,1,0:T(8,128)(2,1)S(1)}, u32[]{:S(2)}, u32[]{:S(2)}) collective-permute-start(bf16[2,4,128,128]{3,2,1,0:T(8,128)(2,1)S(1)} %get-tuple-element.35), channel_id=1, source_target_pairs={{0,1},{1,0},{2,3},{3,2},{4,5},{5,4},{6,7},{7,6},{8,9},{9,8},{10,11... | collective-permute-start | bytes 786440 | tf_op jit(solution)/shard_map/ppermute | solution.py:39
  21.9 8.7 %collective-permute-start.10 = (bf16[2,1,4,128,128]{4,3,2,1,0:T(8,128)(2,1)S(1)}, bf16[2,1,4,128,128]{4,3,2,1,0:T(8,128)(2,1)S(1)}, u32[]{:S(2)}, u32[]{:S(2)}) collective-permute-start(bf16[2,1,4,128,128]{4,3,2,1,0:T(8,128)(2,1)S(1)} %get-tuple-element.51), channel_id=1, source_target_pairs={{0,2},{1,3},{2,0},{3,1},{4,6},{5,7},{6,4},{7,5},{8,10},{9,11},{10,... | collective-permute-start | bytes 786440 | tf_op jit(solution)/shard_map/ppermute | solution.py:39
  27.4 4.9 %copy-start.3 = (bf16[2,64,64]{2,1,0:T(8,128)(2,1)S(1)}, bf16[2,64,64]{2,1,0:T(8,128)(2,1)}, u32[]{:S(2)}) copy-start(bf16[2,64,64]{2,1,0:T(8,128)(2,1)} %param.7) | copy-start | bytes 49156
  27.4 3.5 %collective-permute-start.4 = (bf16[2,4,128,128]{3,2,1,0:T(8,128)(2,1)S(1)}, bf16[2,4,128,128]{3,2,1,0:T(8,128)(2,1)S(1)}, u32[]{:S(2)}, u32[]{:S(2)}) collective-permute-start(bf16[2,4,128,128]{3,2,1,0:T(8,128)(2,1)S(1)} %get-tuple-element.42), channel_id=1, source_target_pairs={{0,1},{1,0},{2,3},{3,2},{4,5},{5,4},{6,7},{7,6},{8,9},{9,8},{10,11... | collective-permute-start | bytes 786440 | tf_op jit(solution)/shard_map/ppermute | solution.py:39
  30.8 8.8 %collective-permute-start.11 = (bf16[1024,128]{1,0:T(8,128)(2,1)S(1)}, bf16[1024,128]{1,0:T(8,128)(2,1)S(1)}, u32[]{:S(2)}, u32[]{:S(2)}) collective-permute-start(bf16[1024,128]{1,0:T(8,128)(2,1)S(1)} %get-tuple-element.53), channel_id=1, source_target_pairs={{0,4},{4,0},{8,12},{12,8},{16,20},{20,16},{24,28},{28,24},{1,5},{5... | collective-permute-start | bytes 786440 | tf_op jit(solution)/shard_map/ppermute | solution.py:39
  30.9 28.0 %copy-start.1 = (s32[3]{0:T(128)S(1)}, s32[3]{0:T(128)}, u32[]{:S(2)}) copy-start(s32[3]{0:T(128)} %param.6) | copy-start | bytes 40
  31.0 5.0 %collective-permute-start.5 = (bf16[1,1,4,128,128]{4,3,2,1,0:T(8,128)(2,1)S(1)}, bf16[1,1,4,128,128]{4,3,2,1,0:T(8,128)(2,1)S(1)}, u32[]{:S(2)}, u32[]{:S(2)}) collective-permute-start(bf16[1,1,4,128,128]{4,3,2,1,0:T(8,128)(2,1)S(1)} %get-tuple-element.44), channel_id=1, source_target_pairs={{0,2},{1,3},{2,0},{3,1},{4,6},{5,7},{6,4},{7,5},{8,10},{9,11},{10,... | collective-permute-start | bytes 393224 | tf_op jit(solution)/shard_map/ppermute | solution.py:39
  36.2 8.0 %collective-permute-start.6 = (bf16[512,128]{1,0:T(8,128)(2,1)S(1)}, bf16[512,128]{1,0:T(8,128)(2,1)S(1)}, u32[]{:S(2)}, u32[]{:S(2)}) collective-permute-start(bf16[512,128]{1,0:T(8,128)(2,1)S(1)} %get-tuple-element.46), channel_id=1, source_target_pairs={{0,4},{4,0},{8,12},{12,8},{16,20},{20,16},{24,28},{28,24},{1,5},{5... | collective-permute-start | bytes 393224 | tf_op jit(solution)/shard_map/ppermute | solution.py:39
  39.7 6.4 %collective-permute-start.12 = (bf16[320,128]{1,0:T(8,128)(2,1)S(1)}, bf16[320,128]{1,0:T(8,128)(2,1)S(1)}, u32[]{:S(2)}, u32[]{:S(2)}) collective-permute-start(bf16[320,128]{1,0:T(8,128)(2,1)S(1)} %get-tuple-element.55), channel_id=1, source_target_pairs={{0,8},{4,12},{8,0},{12,4},{16,24},{20,28},{24,16},{28,20},{1,9},{5... | collective-permute-start | bytes 245768 | tf_op jit(solution)/shard_map/ppermute | solution.py:39
  39.8 8.9 %collective-permute-start.13 = (bf16[320,128]{1,0:T(8,128)(2,1)S(1)}, bf16[320,128]{1,0:T(8,128)(2,1)S(1)}, u32[]{:S(2)}, u32[]{:S(2)}) collective-permute-start(bf16[320,128]{1,0:T(8,128)(2,1)S(1)} %get-tuple-element.56), channel_id=1, source_target_pairs={{0,16},{4,20},{8,24},{12,28},{16,0},{20,4},{24,8},{28,12},{1,17},{... | collective-permute-start | bytes 245768 | tf_op jit(solution)/shard_map/ppermute | solution.py:39
  41.5 7.2 %collective-permute-start.14 = (bf16[320,128]{1,0:T(8,128)(2,1)S(1)}, bf16[320,128]{1,0:T(8,128)(2,1)S(1)}, u32[]{:S(2)}, u32[]{:S(2)}) collective-permute-start(bf16[320,128]{1,0:T(8,128)(2,1)S(1)} %get-tuple-element.57), channel_id=1, source_target_pairs={{0,24},{4,28},{8,16},{12,20},{16,8},{20,12},{24,0},{28,4},{1,25},{... | collective-permute-start | bytes 245768 | tf_op jit(solution)/shard_map/ppermute | solution.py:39
  44.2 5.1 %collective-permute-start.7 = (bf16[128,128]{1,0:T(8,128)(2,1)S(1)}, bf16[128,128]{1,0:T(8,128)(2,1)S(1)}, u32[]{:S(2)}, u32[]{:S(2)}) collective-permute-start(bf16[128,128]{1,0:T(8,128)(2,1)S(1)} %get-tuple-element.48), channel_id=1, source_target_pairs={{0,8},{4,12},{8,0},{12,4},{16,24},{20,28},{24,16},{28,20},{1,9},{5... | collective-permute-start | bytes 98312 | tf_op jit(solution)/shard_map/ppermute | solution.py:39
  44.3 6.6 %collective-permute-start.8 = (bf16[128,128]{1,0:T(8,128)(2,1)S(1)}, bf16[128,128]{1,0:T(8,128)(2,1)S(1)}, u32[]{:S(2)}, u32[]{:S(2)}) collective-permute-start(bf16[128,128]{1,0:T(8,128)(2,1)S(1)} %get-tuple-element.49), channel_id=1, source_target_pairs={{0,16},{4,20},{8,24},{12,28},{16,0},{20,4},{24,8},{28,12},{1,17},{... | collective-permute-start | bytes 98312 | tf_op jit(solution)/shard_map/ppermute | solution.py:39
  46.1 5.7 %collective-permute-start.9 = (bf16[128,128]{1,0:T(8,128)(2,1)S(1)}, bf16[128,128]{1,0:T(8,128)(2,1)S(1)}, u32[]{:S(2)}, u32[]{:S(2)}) collective-permute-start(bf16[128,128]{1,0:T(8,128)(2,1)S(1)} %get-tuple-element.50), channel_id=1, source_target_pairs={{0,24},{4,28},{8,16},{12,20},{16,8},{20,12},{24,0},{28,4},{1,25},{... | collective-permute-start | bytes 98312 | tf_op jit(solution)/shard_map/ppermute | solution.py:39
  51.9 5.7 %collective-permute-start.15 = (bf16[384,128]{1,0:T(8,128)(2,1)S(1)}, bf16[384,128]{1,0:T(8,128)(2,1)S(1)}, u32[]{:S(2)}, u32[]{:S(2)}) collective-permute-start(bf16[384,128]{1,0:T(8,128)(2,1)S(1)} %shard_map.72.refs_0_), channel_id=1, source_target_pairs={{0,2},{1,3},{2,0},{3,1},{4,6},{5,7},{6,4},{7,5},{8,10},{9,11},{10,... | collective-permute-start | bytes 294920 | tf_op jit(solution)/shard_map/ppermute | solution.py:39
  53.3 4.3 %collective-permute-start.16 = (bf16[256,128]{1,0:T(8,128)(2,1)S(1)}, bf16[256,128]{1,0:T(8,128)(2,1)S(1)}, u32[]{:S(2)}, u32[]{:S(2)}) collective-permute-start(bf16[256,128]{1,0:T(8,128)(2,1)S(1)} %pad_maximum_fusion), channel_id=1, source_target_pairs={{0,4},{4,0},{8,12},{12,8},{16,20},{20,16},{24,28},{28,24},{1,5},{5... | collective-permute-start | bytes 196616 | tf_op jit(solution)/shard_map/ppermute | solution.py:39
  54.9 2.7 %collective-permute-start.17 = (bf16[384,128]{1,0:T(8,128)(2,1)S(1)}, bf16[384,128]{1,0:T(8,128)(2,1)S(1)}, u32[]{:S(2)}, u32[]{:S(2)}) collective-permute-start(bf16[384,128]{1,0:T(8,128)(2,1)S(1)} %shard_map.72.refs_0_), channel_id=1, source_target_pairs={{0,1},{1,0},{2,3},{3,2},{4,5},{5,4},{6,7},{7,6},{8,9},{9,8},{10,11... | collective-permute-start | bytes 294920 | tf_op jit(solution)/shard_map/ppermute | solution.py:39
  57.6 1.3 %collective-permute-start.18 = (bf16[384,128]{1,0:T(8,128)(2,1)S(1)}, bf16[384,128]{1,0:T(8,128)(2,1)S(1)}, u32[]{:S(2)}, u32[]{:S(2)}) collective-permute-start(bf16[384,128]{1,0:T(8,128)(2,1)S(1)} %collective-permute-done.15.refs_1_), channel_id=1, source_target_pairs={{0,1},{1,0},{2,3},{3,2},{4,5},{5,4},{6,7},{7,6},{8,9},{9,8},{10,11... | collective-permute-start | bytes 294920 | tf_op jit(solution)/shard_map/ppermute | solution.py:39

commit v7 on v6

--- a/solution.py
+++ b/solution.py
@@ -160,7 +160,7 @@
                 rot_scr[rows, at + part : at + part + length] = -low_real
             return carry
 
-        lax.fori_loop(0, count // group, step, 0, unroll=8)
+        lax.fori_loop(0, count // group, step, 0, unroll=16)
 
     here = lax.axis_index("narrow")
     pieces = packed.shape[0]

time: 60.3 us -> 60.3 us (level)
  transfers between devices with their start and end apart: 19 -> 19, of which waited for: 11 -> 10; matrix products, arithmetic and copies ran while one was open for 0% -> 0% of each run, Pallas kernels for 25% -> 24%
where the time goes in v7:
time: 60.3 us; the launch traced here: 60.2 us
  starting transfers between devices  24.9 us (41%)
  waiting for transfers between devices  16.7 us (28%)
  Pallas kernels  16.1 us (27%)
  local copies, waits for them, and re-layouts  1.47 us (2%)
  between operations  0.83 us (1%)
    ppermute x17, starting transfers between devices, swap(): return lax.ppermute(x, axis, [(i, i ^ mask) for i in range(length)])  18.2 us
    ppermute x17, waiting for transfers between devices, swap(): return lax.ppermute(x, axis, [(i, i ^ mask) for i in range(length)])  16.2 us
    pallas_call x4, Pallas kernels, direction_part(): call(functools.partial(direction_kernel, direction, chosen, planes, norm,...  12.1 us
    ppermute x2, starting transfers between devices, from_behind(): lax.ppermute(x, axis, [(i, (i + by) % length) for i in range(length)])  6.71 us
    pallas_call x2, Pallas kernels, by_rows(): pl.pallas_call(functools.partial(kernel, planes), grid=(count // block,),...  1.98 us
    unnamed x8, local copies, waits for them, and re-layouts  1.42 us
    pallas_call x1, Pallas kernels, finish(): call(functools.partial(finish_kernel, order), [jax.ShapeDtypeStruct((slot...  1.28 us
  transfers between devices with their start and end apart: 19, of which 10 were waited for; matrix products, arithmetic and copies ran while one was open for 0% of the time, Pallas kernels for 24%

profile of v7, /device:TPU:0, one launch (start us, length us, event | category | flops | bytes accessed | tf_op | source)
XLA Modules:
  0.0 60.2 jit_solution(12010771358979685110)
XLA Ops:
  0.6 1.4 %copy-done = bf16[512,2,3,2,128]{4,3,2,1,0:T(2,128)(2,1)S(1)} copy-done((bf16[512,2,3,2,128]{4,3,2,1,0:T(2,128)(2,1)S(1)}, bf16[512,2,3,2,128]{4,3,2,1,0:T(2,128)(2,1)}, u32[]{:S(2)}) %copy-start) | copy-done | bytes 1572888
  2.0 0.4 shard_map.59
  2.5 6.1 %collective-permute-start.3 = (bf16[512,768]{1,0:T(8,128)(2,1)S(1)}, bf16[512,768]{1,0:T(8,128)(2,1)S(1)}, u32[]{:S(2)}, u32[]{:S(2)}) collective-permute-start(bf16[512,768]{1,0:T(8,128)(2,1)S(1)} %shard_map.59), channel_id=1, source_target_pairs={{0,28},{4,0},{8,4},{12,8},{16,12},{20,16},{24,20},{28,24},{1,29},{... | collective-permute-start | bytes 2359304 | tf_op jit(solution)/shard_map/ppermute | solution.py:34
  8.5 1.5 %shard_map.60 = (bf16[512,1536]{1,0:T(8,128)(2,1)S(1)}, bf16[512,256]{1,0:T(8,128)(2,1)}) custom-call(bf16[6144,128]{1,0:T(8,128)(2,1)S(1)} %bitcast.13), custom_call_target="tpu_custom_call" | custom-call | flops 1 | bytes 1 | tf_op jit(solution)/shard_map/pallas_call | solution.py:73
  10.1 0.7 %collective-permute-start = (bf16[512,256]{1,0:T(8,128)(2,1)}, bf16[512,256]{1,0:T(8,128)(2,1)S(1)}, u32[]{:S(2)}, u32[]{:S(2)}) collective-permute-start(bf16[512,256]{1,0:T(8,128)(2,1)} %get-tuple-element.33), channel_id=1, source_target_pairs={{0,3},{1,0},{2,1},{3,2},{4,7},{5,4},{6,5},{7,6},{8,11},{9,8},{10,9... | collective-permute-start | bytes 786440 | tf_op jit(solution)/shard_map/ppermute | solution.py:34
  10.8 4.0 %shard_map.62 = (f32[2,4,128,128]{3,2,1,0:T(8,128)S(1)}, bf16[2,4,128,128]{3,2,1,0:T(8,128)(2,1)S(1)}) custom-call(f32[108,128]{1,0:T(8,128)S(1)} %reshape.10.refs_0_, bf16[512,1536]{1,0:T(8,128)(2,1)S(1)} %get-tuple-element.40.refs_1_), custom_call_target="tpu_custom_call" | custom-call | flops 1 | bytes 1 | tf_op jit(solution)/shard_map/pallas_call | solution.py:230
  14.9 4.1 %shard_map.61 = (f32[2,4,128,128]{3,2,1,0:T(8,128)S(1)}, bf16[2,4,128,128]{3,2,1,0:T(8,128)(2,1)S(1)}) custom-call(f32[108,128]{1,0:T(8,128)S(1)} %reshape.10.refs_0_, bf16[512,1536]{1,0:T(8,128)(2,1)S(1)} %get-tuple-element.40.refs_1_, bf16[512,256]{1,0:T(8,128)(2,1)S(1)} %collective-permute-done.refs_2_), custom_call_target="tpu_custom_call" | custom-call | flops 1 | bytes 1 | tf_op jit(solution)/shard_map/pallas_call | solution.py:230
  19.0 1.4 %collective-permute-start.1 = (bf16[2,4,128,128]{3,2,1,0:T(8,128)(2,1)S(1)}, bf16[2,4,128,128]{3,2,1,0:T(8,128)(2,1)S(1)}, u32[]{:S(2)}, u32[]{:S(2)}) collective-permute-start(bf16[2,4,128,128]{3,2,1,0:T(8,128)(2,1)S(1)} %get-tuple-element.35), channel_id=1, source_target_pairs={{0,1},{1,0},{2,3},{3,2},{4,5},{5,4},{6,7},{7,6},{8,9},{9,8},{10,11... | collective-permute-start | bytes 786440 | tf_op jit(solution)/shard_map/ppermute | solution.py:39
  20.4 1.2 %collective-permute-done.1 = bf16[2,4,128,128]{3,2,1,0:T(8,128)(2,1)S(1)} collective-permute-done((bf16[2,4,128,128]{3,2,1,0:T(8,128)(2,1)S(1)}, bf16[2,4,128,128]{3,2,1,0:T(8,128)(2,1)S(1)}, u32[]{:S(2)}, u32[]{:S(2)}) %collective-permute-start.1) | collective-permute-done | bytes 262176 | tf_op jit(solution)/shard_map/ppermute | solution.py:39
  21.7 1.3 %collective-permute-start.10 = (bf16[2,1,4,128,128]{4,3,2,1,0:T(8,128)(2,1)S(1)}, bf16[2,1,4,128,128]{4,3,2,1,0:T(8,128)(2,1)S(1)}, u32[]{:S(2)}, u32[]{:S(2)}) collective-permute-start(bf16[2,1,4,128,128]{4,3,2,1,0:T(8,128)(2,1)S(1)} %get-tuple-element.51), channel_id=1, source_target_pairs={{0,2},{1,3},{2,0},{3,1},{4,6},{5,7},{6,4},{7,5},{8,10},{9,11},{10,... | collective-permute-start | bytes 786440 | tf_op jit(solution)/shard_map/ppermute | solution.py:39
  22.9 2.0 %shard_map.64.refs_3_ = f32[4,4,128,128]{3,2,1,0:T(8,128)S(1)} custom-call(f32[108,128]{1,0:T(8,128)S(1)} %reshape.10.refs_0_, bf16[512,1536]{1,0:T(8,128)(2,1)S(1)} %get-tuple-element.40.refs_1_), custom_call_target="tpu_custom_call" | custom-call | flops 1 | bytes 1 | tf_op jit(solution)/shard_map/pallas_call | solution.py:230
  24.9 0.5 collective-permute-done.3.refs_2_
  25.3 2.0 %shard_map.65 = (f32[2,4,128,128]{3,2,1,0:T(8,128)S(1)}, bf16[2,4,128,128]{3,2,1,0:T(8,128)(2,1)S(1)}) custom-call(f32[108,128]{1,0:T(8,128)S(1)} %reshape.10.refs_0_, bf16[512,1536]{1,0:T(8,128)(2,1)S(1)} %get-tuple-element.40.refs_1_, bf16[512,768]{1,0:T(8,128)(2,1)S(1)} %collective-permute-done.3.refs_2_, f32[4,4,128,128]{3,2,1,0:T(8,128)S(1)} %shard_map.64.refs_3_), custom_call_target="tpu_custom_call" | custom-call | flops 1 | bytes 1 | tf_op jit(solution)/shard_map/pallas_call | solution.py:230
  27.5 2.8 %collective-permute-done.10.came_ref = bf16[2,1,4,128,128]{4,3,2,1,0:T(8,128)(2,1)S(1)} collective-permute-done((bf16[2,1,4,128,128]{4,3,2,1,0:T(8,128)(2,1)S(1)}, bf16[2,1,4,128,128]{4,3,2,1,0:T(8,128)(2,1)S(1)}, u32[]{:S(2)}, u32[]{:S(2)}) %collective-permute-start.10) | collective-permute-done | bytes 262176 | tf_op jit(solution)/shard_map/ppermute | solution.py:39
  30.3 0.3 shard_map.69
  30.8 1.3 %collective-permute-start.5 = (bf16[1,1,4,128,128]{4,3,2,1,0:T(8,128)(2,1)S(1)}, bf16[1,1,4,128,128]{4,3,2,1,0:T(8,128)(2,1)S(1)}, u32[]{:S(2)}, u32[]{:S(2)}) collective-permute-start(bf16[1,1,4,128,128]{4,3,2,1,0:T(8,128)(2,1)S(1)} %get-tuple-element.44), channel_id=1, source_target_pairs={{0,2},{1,3},{2,0},{3,1},{4,6},{5,7},{6,4},{7,5},{8,10},{9,11},{10,... | collective-permute-start | bytes 393224 | tf_op jit(solution)/shard_map/ppermute | solution.py:39
  32.0 3.8 %collective-permute-done.5.came_ref = bf16[1,1,4,128,128]{4,3,2,1,0:T(8,128)(2,1)S(1)} collective-permute-done((bf16[1,1,4,128,128]{4,3,2,1,0:T(8,128)(2,1)S(1)}, bf16[1,1,4,128,128]{4,3,2,1,0:T(8,128)(2,1)S(1)}, u32[]{:S(2)}, u32[]{:S(2)}) %collective-permute-start.5) | collective-permute-done | bytes 131104 | tf_op jit(solution)/shard_map/ppermute | solution.py:39
  35.8 0.2 shard_map.67
  36.0 2.1 %collective-permute-start.6 = (bf16[512,128]{1,0:T(8,128)(2,1)S(1)}, bf16[512,128]{1,0:T(8,128)(2,1)S(1)}, u32[]{:S(2)}, u32[]{:S(2)}) collective-permute-start(bf16[512,128]{1,0:T(8,128)(2,1)S(1)} %get-tuple-element.46), channel_id=1, source_target_pairs={{0,4},{4,0},{8,12},{12,8},{16,20},{20,16},{24,28},{28,24},{1,5},{5... | collective-permute-start | bytes 393224 | tf_op jit(solution)/shard_map/ppermute | solution.py:39
  38.2 1.3 %collective-permute-done.11.came_ref = bf16[1024,128]{1,0:T(8,128)(2,1)S(1)} collective-permute-done((bf16[1024,128]{1,0:T(8,128)(2,1)S(1)}, bf16[1024,128]{1,0:T(8,128)(2,1)S(1)}, u32[]{:S(2)}, u32[]{:S(2)}) %collective-permute-start.11) | collective-permute-done | bytes 262176 | tf_op jit(solution)/shard_map/ppermute | solution.py:39
  39.6 1.9 %collective-permute-start.13 = (bf16[320,128]{1,0:T(8,128)(2,1)S(1)}, bf16[320,128]{1,0:T(8,128)(2,1)S(1)}, u32[]{:S(2)}, u32[]{:S(2)}) collective-permute-start(bf16[320,128]{1,0:T(8,128)(2,1)S(1)} %get-tuple-element.56), channel_id=1, source_target_pairs={{0,16},{4,20},{8,24},{12,28},{16,0},{20,4},{24,8},{28,12},{1,17},{... | collective-permute-start | bytes 245768 | tf_op jit(solution)/shard_map/ppermute | solution.py:39
  41.5 2.5 %collective-permute-start.14 = (bf16[320,128]{1,0:T(8,128)(2,1)S(1)}, bf16[320,128]{1,0:T(8,128)(2,1)S(1)}, u32[]{:S(2)}, u32[]{:S(2)}) collective-permute-start(bf16[320,128]{1,0:T(8,128)(2,1)S(1)} %get-tuple-element.57), channel_id=1, source_target_pairs={{0,24},{4,28},{8,16},{12,20},{16,8},{20,12},{24,0},{28,4},{1,25},{... | collective-permute-start | bytes 245768 | tf_op jit(solution)/shard_map/ppermute | solution.py:39
  44.1 1.9 %collective-permute-start.8 = (bf16[128,128]{1,0:T(8,128)(2,1)S(1)}, bf16[128,128]{1,0:T(8,128)(2,1)S(1)}, u32[]{:S(2)}, u32[]{:S(2)}) collective-permute-start(bf16[128,128]{1,0:T(8,128)(2,1)S(1)} %get-tuple-element.49), channel_id=1, source_target_pairs={{0,16},{4,20},{8,24},{12,28},{16,0},{20,4},{24,8},{28,12},{1,17},{... | collective-permute-start | bytes 98312 | tf_op jit(solution)/shard_map/ppermute | solution.py:39
  45.9 2.5 %collective-permute-start.9 = (bf16[128,128]{1,0:T(8,128)(2,1)S(1)}, bf16[128,128]{1,0:T(8,128)(2,1)S(1)}, u32[]{:S(2)}, u32[]{:S(2)}) collective-permute-start(bf16[128,128]{1,0:T(8,128)(2,1)S(1)} %get-tuple-element.50), channel_id=1, source_target_pairs={{0,24},{4,28},{8,16},{12,20},{16,8},{20,12},{24,0},{28,4},{1,25},{... | collective-permute-start | bytes 98312 | tf_op jit(solution)/shard_map/ppermute | solution.py:39
  48.6 0.7 %collective-permute-done.7.refs_1_ = bf16[128,128]{1,0:T(8,128)(2,1)S(1)} collective-permute-done((bf16[128,128]{1,0:T(8,128)(2,1)S(1)}, bf16[128,128]{1,0:T(8,128)(2,1)S(1)}, u32[]{:S(2)}, u32[]{:S(2)}) %collective-permute-start.7) | collective-permute-done | bytes 32800 | tf_op jit(solution)/shard_map/ppermute | solution.py:39
  49.2 1.7 %collective-permute-done.8.refs_2_ = bf16[128,128]{1,0:T(8,128)(2,1)S(1)} collective-permute-done((bf16[128,128]{1,0:T(8,128)(2,1)S(1)}, bf16[128,128]{1,0:T(8,128)(2,1)S(1)}, u32[]{:S(2)}, u32[]{:S(2)}) %collective-permute-start.8) | collective-permute-done | bytes 32800 | tf_op jit(solution)/shard_map/ppermute | solution.py:39
  50.9 0.8 %collective-permute-done.9.refs_3_ = bf16[128,128]{1,0:T(8,128)(2,1)S(1)} collective-permute-done((bf16[128,128]{1,0:T(8,128)(2,1)S(1)}, bf16[128,128]{1,0:T(8,128)(2,1)S(1)}, u32[]{:S(2)}, u32[]{:S(2)}) %collective-permute-start.9) | collective-permute-done | bytes 32800 | tf_op jit(solution)/shard_map/ppermute | solution.py:39
  51.7 1.6 %collective-permute-start.15 = (bf16[384,128]{1,0:T(8,128)(2,1)S(1)}, bf16[384,128]{1,0:T(8,128)(2,1)S(1)}, u32[]{:S(2)}, u32[]{:S(2)}) collective-permute-start(bf16[384,128]{1,0:T(8,128)(2,1)S(1)} %shard_map.72.refs_0_), channel_id=1, source_target_pairs={{0,2},{1,3},{2,0},{3,1},{4,6},{5,7},{6,4},{7,5},{8,10},{9,11},{10,... | collective-permute-start | bytes 294920 | tf_op jit(solution)/shard_map/ppermute | solution.py:39
  53.3 1.6 %collective-permute-start.16 = (bf16[256,128]{1,0:T(8,128)(2,1)S(1)}, bf16[256,128]{1,0:T(8,128)(2,1)S(1)}, u32[]{:S(2)}, u32[]{:S(2)}) collective-permute-start(bf16[256,128]{1,0:T(8,128)(2,1)S(1)} %pad_maximum_fusion), channel_id=1, source_target_pairs={{0,4},{4,0},{8,12},{12,8},{16,20},{20,16},{24,28},{28,24},{1,5},{5... | collective-permute-start | bytes 196616 | tf_op jit(solution)/shard_map/ppermute | solution.py:39
  54.9 2.7 %collective-permute-done.16.refs_8_ = bf16[256,128]{1,0:T(8,128)(2,1)S(1)} collective-permute-done((bf16[256,128]{1,0:T(8,128)(2,1)S(1)}, bf16[256,128]{1,0:T(8,128)(2,1)S(1)}, u32[]{:S(2)}, u32[]{:S(2)}) %collective-permute-start.16) | collective-permute-done | bytes 65568 | tf_op jit(solution)/shard_map/ppermute | solution.py:39
  57.6 1.3 %collective-permute-done.18.refs_3_ = bf16[384,128]{1,0:T(8,128)(2,1)S(1)} collective-permute-done((bf16[384,128]{1,0:T(8,128)(2,1)S(1)}, bf16[384,128]{1,0:T(8,128)(2,1)S(1)}, u32[]{:S(2)}, u32[]{:S(2)}) %collective-permute-start.18) | collective-permute-done | bytes 98336 | tf_op jit(solution)/shard_map/ppermute | solution.py:39
  58.9 1.3 %shard_map.73 = (f32[3,2,64,512]{3,2,1,0:T(8,128)}, f32[3,2,64,64]{3,2,1,0:T(8,128)}) custom-call(s32[1,3]{1,0:T(1,128)S(1)} %bitcast.20, bf16[384,128]{1,0:T(8,128)(2,1)S(1)} %shard_map.72.refs_0_, bf16[384,128]{1,0:T(8,128)(2,1)S(1)} %collective-permute-done.15.refs_1_, bf16[384,128]{1,0:T(8,128)(2,1)S(1)} %collective-permute-done.17.refs_2_, ...), custom_call_target="tpu_custom_call" | custom-call | flops 1 | bytes 1 | tf_op jit(solution)/shard_map/pallas_call | solution.py:411
  (36 shorter events, 1.0 us)
Async XLA Ops:
  0.6 1.4 %copy-start = (bf16[512,2,3,2,128]{4,3,2,1,0:T(2,128)(2,1)S(1)}, bf16[512,2,3,2,128]{4,3,2,1,0:T(2,128)(2,1)}, u32[]{:S(2)}) copy-start(bf16[512,2,3,2,128]{4,3,2,1,0:T(2,128)(2,1)} %param.4) | copy-start | bytes 4718596
  2.0 8.7 %copy-start.2 = (f32[3,2,3,3,2,128]{5,4,3,2,1,0:T(2,128)S(1)}, f32[3,2,3,3,2,128]{5,4,3,2,1,0:T(2,128)}, u32[]{:S(2)}) copy-start(f32[3,2,3,3,2,128]{5,4,3,2,1,0:T(2,128)} %param.5) | copy-start | bytes 165892
  2.5 22.9 %collective-permute-start.3 = (bf16[512,768]{1,0:T(8,128)(2,1)S(1)}, bf16[512,768]{1,0:T(8,128)(2,1)S(1)}, u32[]{:S(2)}, u32[]{:S(2)}) collective-permute-start(bf16[512,768]{1,0:T(8,128)(2,1)S(1)} %shard_map.59), channel_id=1, source_target_pairs={{0,28},{4,0},{8,4},{12,8},{16,12},{20,16},{24,20},{28,24},{1,29},{... | collective-permute-start | bytes 2359304 | tf_op jit(solution)/shard_map/ppermute | solution.py:34
  10.1 4.9 %collective-permute-start = (bf16[512,256]{1,0:T(8,128)(2,1)}, bf16[512,256]{1,0:T(8,128)(2,1)S(1)}, u32[]{:S(2)}, u32[]{:S(2)}) collective-permute-start(bf16[512,256]{1,0:T(8,128)(2,1)} %get-tuple-element.33), channel_id=1, source_target_pairs={{0,3},{1,0},{2,1},{3,2},{4,7},{5,4},{6,5},{7,6},{8,11},{9,8},{10,9... | collective-permute-start | bytes 786440 | tf_op jit(solution)/shard_map/ppermute | solution.py:34
  14.8 5.6 %collective-permute-start.2 = (bf16[2,4,128,128]{3,2,1,0:T(8,128)(2,1)S(1)}, bf16[2,4,128,128]{3,2,1,0:T(8,128)(2,1)S(1)}, u32[]{:S(2)}, u32[]{:S(2)}) collective-permute-start(bf16[2,4,128,128]{3,2,1,0:T(8,128)(2,1)S(1)} %get-tuple-element.37), channel_id=1, source_target_pairs={{0,1},{1,0},{2,3},{3,2},{4,5},{5,4},{6,7},{7,6},{8,9},{9,8},{10,11... | collective-permute-start | bytes 786440 | tf_op jit(solution)/shard_map/ppermute | solution.py:39
  19.0 2.5 %collective-permute-start.1 = (bf16[2,4,128,128]{3,2,1,0:T(8,128)(2,1)S(1)}, bf16[2,4,128,128]{3,2,1,0:T(8,128)(2,1)S(1)}, u32[]{:S(2)}, u32[]{:S(2)}) collective-permute-start(bf16[2,4,128,128]{3,2,1,0:T(8,128)(2,1)S(1)} %get-tuple-element.35), channel_id=1, source_target_pairs={{0,1},{1,0},{2,3},{3,2},{4,5},{5,4},{6,7},{7,6},{8,9},{9,8},{10,11... | collective-permute-start | bytes 786440 | tf_op jit(solution)/shard_map/ppermute | solution.py:39
  21.7 8.7 %collective-permute-start.10 = (bf16[2,1,4,128,128]{4,3,2,1,0:T(8,128)(2,1)S(1)}, bf16[2,1,4,128,128]{4,3,2,1,0:T(8,128)(2,1)S(1)}, u32[]{:S(2)}, u32[]{:S(2)}) collective-permute-start(bf16[2,1,4,128,128]{4,3,2,1,0:T(8,128)(2,1)S(1)} %get-tuple-element.51), channel_id=1, source_target_pairs={{0,2},{1,3},{2,0},{3,1},{4,6},{5,7},{6,4},{7,5},{8,10},{9,11},{10,... | collective-permute-start | bytes 786440 | tf_op jit(solution)/shard_map/ppermute | solution.py:39
  27.4 4.6 %copy-start.3 = (bf16[2,64,64]{2,1,0:T(8,128)(2,1)S(1)}, bf16[2,64,64]{2,1,0:T(8,128)(2,1)}, u32[]{:S(2)}) copy-start(bf16[2,64,64]{2,1,0:T(8,128)(2,1)} %param.7) | copy-start | bytes 49156
  27.4 3.3 %collective-permute-start.4 = (bf16[2,4,128,128]{3,2,1,0:T(8,128)(2,1)S(1)}, bf16[2,4,128,128]{3,2,1,0:T(8,128)(2,1)S(1)}, u32[]{:S(2)}, u32[]{:S(2)}) collective-permute-start(bf16[2,4,128,128]{3,2,1,0:T(8,128)(2,1)S(1)} %get-tuple-element.42), channel_id=1, source_target_pairs={{0,1},{1,0},{2,3},{3,2},{4,5},{5,4},{6,7},{7,6},{8,9},{9,8},{10,11... | collective-permute-start | bytes 786440 | tf_op jit(solution)/shard_map/ppermute | solution.py:39
  30.6 8.8 %collective-permute-start.11 = (bf16[1024,128]{1,0:T(8,128)(2,1)S(1)}, bf16[1024,128]{1,0:T(8,128)(2,1)S(1)}, u32[]{:S(2)}, u32[]{:S(2)}) collective-permute-start(bf16[1024,128]{1,0:T(8,128)(2,1)S(1)} %get-tuple-element.53), channel_id=1, source_target_pairs={{0,4},{4,0},{8,12},{12,8},{16,20},{20,16},{24,28},{28,24},{1,5},{5... | collective-permute-start | bytes 786440 | tf_op jit(solution)/shard_map/ppermute | solution.py:39
  30.7 28.2 %copy-start.1 = (s32[3]{0:T(128)S(1)}, s32[3]{0:T(128)}, u32[]{:S(2)}) copy-start(s32[3]{0:T(128)} %param.6) | copy-start | bytes 40
  30.8 5.0 %collective-permute-start.5 = (bf16[1,1,4,128,128]{4,3,2,1,0:T(8,128)(2,1)S(1)}, bf16[1,1,4,128,128]{4,3,2,1,0:T(8,128)(2,1)S(1)}, u32[]{:S(2)}, u32[]{:S(2)}) collective-permute-start(bf16[1,1,4,128,128]{4,3,2,1,0:T(8,128)(2,1)S(1)} %get-tuple-element.44), channel_id=1, source_target_pairs={{0,2},{1,3},{2,0},{3,1},{4,6},{5,7},{6,4},{7,5},{8,10},{9,11},{10,... | collective-permute-start | bytes 393224 | tf_op jit(solution)/shard_map/ppermute | solution.py:39
  36.0 8.0 %collective-permute-start.6 = (bf16[512,128]{1,0:T(8,128)(2,1)S(1)}, bf16[512,128]{1,0:T(8,128)(2,1)S(1)}, u32[]{:S(2)}, u32[]{:S(2)}) collective-permute-start(bf16[512,128]{1,0:T(8,128)(2,1)S(1)} %get-tuple-element.46), channel_id=1, source_target_pairs={{0,4},{4,0},{8,12},{12,8},{16,20},{20,16},{24,28},{28,24},{1,5},{5... | collective-permute-start | bytes 393224 | tf_op jit(solution)/shard_map/ppermute | solution.py:39
  39.5 6.4 %collective-permute-start.12 = (bf16[320,128]{1,0:T(8,128)(2,1)S(1)}, bf16[320,128]{1,0:T(8,128)(2,1)S(1)}, u32[]{:S(2)}, u32[]{:S(2)}) collective-permute-start(bf16[320,128]{1,0:T(8,128)(2,1)S(1)} %get-tuple-element.55), channel_id=1, source_target_pairs={{0,8},{4,12},{8,0},{12,4},{16,24},{20,28},{24,16},{28,20},{1,9},{5... | collective-permute-start | bytes 245768 | tf_op jit(solution)/shard_map/ppermute | solution.py:39
  39.6 8.9 %collective-permute-start.13 = (bf16[320,128]{1,0:T(8,128)(2,1)S(1)}, bf16[320,128]{1,0:T(8,128)(2,1)S(1)}, u32[]{:S(2)}, u32[]{:S(2)}) collective-permute-start(bf16[320,128]{1,0:T(8,128)(2,1)S(1)} %get-tuple-element.56), channel_id=1, source_target_pairs={{0,16},{4,20},{8,24},{12,28},{16,0},{20,4},{24,8},{28,12},{1,17},{... | collective-permute-start | bytes 245768 | tf_op jit(solution)/shard_map/ppermute | solution.py:39
  41.5 7.0 %collective-permute-start.14 = (bf16[320,128]{1,0:T(8,128)(2,1)S(1)}, bf16[320,128]{1,0:T(8,128)(2,1)S(1)}, u32[]{:S(2)}, u32[]{:S(2)}) collective-permute-start(bf16[320,128]{1,0:T(8,128)(2,1)S(1)} %get-tuple-element.57), channel_id=1, source_target_pairs={{0,24},{4,28},{8,16},{12,20},{16,8},{20,12},{24,0},{28,4},{1,25},{... | collective-permute-start | bytes 245768 | tf_op jit(solution)/shard_map/ppermute | solution.py:39
  44.0 5.2 %collective-permute-start.7 = (bf16[128,128]{1,0:T(8,128)(2,1)S(1)}, bf16[128,128]{1,0:T(8,128)(2,1)S(1)}, u32[]{:S(2)}, u32[]{:S(2)}) collective-permute-start(bf16[128,128]{1,0:T(8,128)(2,1)S(1)} %get-tuple-element.48), channel_id=1, source_target_pairs={{0,8},{4,12},{8,0},{12,4},{16,24},{20,28},{24,16},{28,20},{1,9},{5... | collective-permute-start | bytes 98312 | tf_op jit(solution)/shard_map/ppermute | solution.py:39
  44.1 6.8 %collective-permute-start.8 = (bf16[128,128]{1,0:T(8,128)(2,1)S(1)}, bf16[128,128]{1,0:T(8,128)(2,1)S(1)}, u32[]{:S(2)}, u32[]{:S(2)}) collective-permute-start(bf16[128,128]{1,0:T(8,128)(2,1)S(1)} %get-tuple-element.49), channel_id=1, source_target_pairs={{0,16},{4,20},{8,24},{12,28},{16,0},{20,4},{24,8},{28,12},{1,17},{... | collective-permute-start | bytes 98312 | tf_op jit(solution)/shard_map/ppermute | solution.py:39
  45.9 5.7 %collective-permute-start.9 = (bf16[128,128]{1,0:T(8,128)(2,1)S(1)}, bf16[128,128]{1,0:T(8,128)(2,1)S(1)}, u32[]{:S(2)}, u32[]{:S(2)}) collective-permute-start(bf16[128,128]{1,0:T(8,128)(2,1)S(1)} %get-tuple-element.50), channel_id=1, source_target_pairs={{0,24},{4,28},{8,16},{12,20},{16,8},{20,12},{24,0},{28,4},{1,25},{... | collective-permute-start | bytes 98312 | tf_op jit(solution)/shard_map/ppermute | solution.py:39
  51.7 5.9 %collective-permute-start.15 = (bf16[384,128]{1,0:T(8,128)(2,1)S(1)}, bf16[384,128]{1,0:T(8,128)(2,1)S(1)}, u32[]{:S(2)}, u32[]{:S(2)}) collective-permute-start(bf16[384,128]{1,0:T(8,128)(2,1)S(1)} %shard_map.72.refs_0_), channel_id=1, source_target_pairs={{0,2},{1,3},{2,0},{3,1},{4,6},{5,7},{6,4},{7,5},{8,10},{9,11},{10,... | collective-permute-start | bytes 294920 | tf_op jit(solution)/shard_map/ppermute | solution.py:39
  53.3 4.3 %collective-permute-start.16 = (bf16[256,128]{1,0:T(8,128)(2,1)S(1)}, bf16[256,128]{1,0:T(8,128)(2,1)S(1)}, u32[]{:S(2)}, u32[]{:S(2)}) collective-permute-start(bf16[256,128]{1,0:T(8,128)(2,1)S(1)} %pad_maximum_fusion), channel_id=1, source_target_pairs={{0,4},{4,0},{8,12},{12,8},{16,20},{20,16},{24,28},{28,24},{1,5},{5... | collective-permute-start | bytes 196616 | tf_op jit(solution)/shard_map/ppermute | solution.py:39
  54.9 2.7 %collective-permute-start.17 = (bf16[384,128]{1,0:T(8,128)(2,1)S(1)}, bf16[384,128]{1,0:T(8,128)(2,1)S(1)}, u32[]{:S(2)}, u32[]{:S(2)}) collective-permute-start(bf16[384,128]{1,0:T(8,128)(2,1)S(1)} %shard_map.72.refs_0_), channel_id=1, source_target_pairs={{0,1},{1,0},{2,3},{3,2},{4,5},{5,4},{6,7},{7,6},{8,9},{9,8},{10,11... | collective-permute-start | bytes 294920 | tf_op jit(solution)/shard_map/ppermute | solution.py:39
  57.6 1.3 %collective-permute-start.18 = (bf16[384,128]{1,0:T(8,128)(2,1)S(1)}, bf16[384,128]{1,0:T(8,128)(2,1)S(1)}, u32[]{:S(2)}, u32[]{:S(2)}) collective-permute-start(bf16[384,128]{1,0:T(8,128)(2,1)S(1)} %collective-permute-done.15.refs_1_), channel_id=1, source_target_pairs={{0,1},{1,0},{2,3},{3,2},{4,5},{5,4},{6,7},{7,6},{8,9},{9,8},{10,11... | collective-permute-start | bytes 294920 | tf_op jit(solution)/shard_map/ppermute | solution.py:39
